TPU v7x, 256 devices: a whole 4x4x8 slice. The times are simulated.
256 devices in a mesh: tile: 16 (over x, y), frame: 16 (over z, core).
Axes of the slice: x: 4, y: 4, z: 8, core: 2. Of those that a mesh axis runs over, the one named last changes fastest.
Arguments:
- object_field: float32 [2, 4096, 4096], P(None, 'tile', 'frame'), may hold values from -4 to 4
- probe_modes: float32 [2, 3, 256, 256], replicated, may hold values from -4 to 4
- measured: float32 [256, 256, 256], P(('tile', 'frame')), may hold values from 0.2 to 2.5
- offsets: int32 [256, 2], P(('tile', 'frame')), may hold values from 0 to 255
- ramp_steps: int32 [256, 2], P(('tile', 'frame')), may hold values from 0 to 7
Outputs:
- object_final: float32 [2, 4096, 4096], P(None, 'tile', 'frame')
- probe_final: float32 [2, 3, 256, 256], replicated
- position_grad: float32 [256, 2], P(('tile', 'frame'))
All inputs are finite; a program needn't handle non-finite values.
Results may differ from a plain program's by a relative error of at most 0.0003.
Values sent between devices are 32-bit elements; how exact they have to be, the bound alone decides.
No kernel may reach another device: no remote copies, remote signals or barrier semaphores. Data moves between devices by JAX's collectives and lax.ppermute only.
A program may use at most 128 MiB of HBM per device.

v0:
```python
import math

import jax
import jax.numpy as jnp
from jax import lax
from jax.sharding import PartitionSpec as P

RAMPS = 8
ITERS = 2


object_step = 0.05
probe_step = 0.5
fresnel = 0.25


def shifted(value, axis, steps):
    count = lax.axis_size(axis)
    initial, last = (max(0, -steps), min(count, count - steps))
    return lax.ppermute(value, axis, [(source, source + steps) for source in range(initial, last)])


def dft_tables(length):
    counter = jnp.arange(length, dtype=jnp.int32)
    product = counter[:, None] * counter[None, :] % length
    angles = 2.0 * math.pi / length * product.astype(jnp.float32)
    scaling = 1.0 / math.sqrt(length)
    return (jnp.cos(angles) * scaling, -jnp.sin(angles) * scaling)


def transform(real_part, imag_part, cos_table, sin_table):
    highest = lax.Precision.HIGHEST
    left_real = jnp.einsum("jk,mkl->mjl", cos_table, real_part, precision=highest) - jnp.einsum(
        "jk,mkl->mjl", sin_table, imag_part, precision=highest
    )
    left_imag = jnp.einsum("jk,mkl->mjl", cos_table, imag_part, precision=highest) + jnp.einsum(
        "jk,mkl->mjl", sin_table, real_part, precision=highest
    )
    out_real = jnp.einsum("mjl,lk->mjk", left_real, cos_table, precision=highest) - jnp.einsum(
        "mjl,lk->mjk", left_imag, sin_table, precision=highest
    )
    out_imag = jnp.einsum("mjl,lk->mjk", left_real, sin_table, precision=highest) + jnp.einsum(
        "mjl,lk->mjk", left_imag, cos_table, precision=highest
    )
    return (out_real, out_imag)


def frame_loss(patch_area, modes_in, shift_amount, target):
    length = patch_area.shape[-1]
    cos_table, sin_table = dft_tables(length)
    exit_real = modes_in[0] * patch_area[0] - modes_in[1] * patch_area[1]
    exit_imag = modes_in[0] * patch_area[1] + modes_in[1] * patch_area[0]
    spec_real, spec_imag = transform(exit_real, exit_imag, cos_table, sin_table)
    counter = jnp.arange(length, dtype=jnp.int32)
    signed = jnp.where(counter < length // 2, counter, counter - length).astype(jnp.float32)
    chirp_phase = -math.pi * fresnel / length * signed * signed
    phase_rows = chirp_phase - 2.0 * math.pi / length * signed * shift_amount[0]
    phase_cols = chirp_phase - 2.0 * math.pi / length * signed * shift_amount[1]
    phases = phase_rows[:, None] + phase_cols[None, :]
    kernel_real = jnp.cos(phases)
    kernel_imag = jnp.sin(phases)
    prop_real = kernel_real * spec_real - kernel_imag * spec_imag
    prop_imag = kernel_real * spec_imag + kernel_imag * spec_real
    wave_real, wave_imag = transform(prop_real, prop_imag, cos_table, -sin_table)
    intensity = jnp.sum(wave_real * wave_real + wave_imag * wave_imag, axis=0)
    misfit = intensity - target
    return 0.5 * jnp.sum(misfit * misfit)


def frame_gradients(window, modes_in, measured, corners, ramp_steps):
    det_size = modes_in.shape[-1]

    def visit_frame(running, inputs):
        grad_window, grad_modes = running
        corner, ramp_index, target = inputs
        anchor = (jnp.int32(0), corner[0], corner[1])
        patch_area = lax.dynamic_slice(window, anchor, (2, det_size, det_size))
        shift_amount = ramp_index.astype(jnp.float32) / RAMPS

        def local_loss(patch_in, probe_in, shift_in):
            return frame_loss(patch_in, probe_in, shift_in, target)

        result, pullback = jax.vjp(local_loss, patch_area, modes_in, shift_amount)
        grad_patch, grad_probe, grad_shift = pullback(jnp.ones_like(result))
        current = lax.dynamic_slice(grad_window, anchor, (2, det_size, det_size))
        grad_window = lax.dynamic_update_slice(grad_window, current + grad_patch, anchor)
        return ((grad_window, grad_modes + grad_probe), grad_shift)

    initial = (jnp.zeros_like(window), jnp.zeros_like(modes_in))
    (grad_window, grad_modes), grad_shift = lax.scan(
        visit_frame, initial, (corners, ramp_steps, measured)
    )
    return (grad_window, grad_modes, grad_shift)


def per_device(object_field, probe_modes, measured, offsets, ramp_steps):
    tile_size = object_field.shape[1]
    det_size = probe_modes.shape[-1]
    frame_total = measured.shape[0] * lax.axis_size("tile") * lax.axis_size("frame")
    probe_rate = probe_step / frame_total
    object_tile = object_field
    modes_now = probe_modes
    grad_shift = jnp.zeros((measured.shape[0], 2), jnp.float32)
    for iteration in range(ITERS):
        right_tile = shifted(object_tile, "frame", -1)
        upper_rows = jnp.concatenate([object_tile, right_tile], axis=2)
        lower_rows = shifted(upper_rows, "tile", -1)
        window = jnp.concatenate([upper_rows, lower_rows], axis=1)
        grad_window, grad_modes, grad_shift = frame_gradients(
            window, modes_now, measured, offsets, ramp_steps
        )
        moved_rows = shifted(grad_window[:, tile_size:, :], "tile", 1)
        row_sum = grad_window[:, :tile_size, :] + moved_rows
        arrived = shifted(row_sum[:, :, tile_size:], "frame", 1)
        object_tile = object_tile - object_step * (row_sum[:, :, :tile_size] + arrived)
        total_grad = lax.psum(grad_modes, ("tile", "frame"))
        modes_now = modes_now - probe_rate * total_grad
    return (object_tile, modes_now, grad_shift / det_size)


def solution(mesh):
    placed = (
        P(None, "tile", "frame"),
        P(),
        P(("tile", "frame"), None, None),
        P(("tile", "frame"), None),
        P(("tile", "frame"), None),
    )
    return jax.shard_map(
        per_device,
        mesh=mesh,
        in_specs=placed,
        out_specs=(P(None, "tile", "frame"), P(), P(("tile", "frame"), None)),
        check_vma=False,
    )
```

profile of v0, /device:TPU:1, one launch (start us, length us, event | category | flops | bytes accessed | tf_op | source)
XLA Modules:
  0.0 799.7 jit_solution(16766759890081682630)
XLA Ops:
  7.2 5.2 collective-permute-start
  14.3 5.0 collective-permute-done
  30.7 12.2 %collective-permute-done.1 = f32[2,256,512]{2,1,0:T(8,128)} collective-permute-done((f32[2,256,512]{2,1,0:T(8,128)}, f32[2,256,512]{2,1,0:T(8,128)}, u32[]{:S(2)}, u32[]{:S(2)}) %collective-permute-start.1) | collective-permute-done | bytes 1048608 | tf_op jit(solution)/shard_map/ppermute | solution.py:20
  65.8 2.5 fusion.21
  77.4 2.6 add_reduce_fusion.1
  109.3 4.3 multiply_bitcast_fusion.7
  115.5 6.0 dynamic_update_slice.11
  125.1 19.2 %collective-permute-done.2 = f32[2,256,512]{2,1,0:T(8,128)S(1)} collective-permute-done((f32[2,256,512]{2,1,0:T(8,128)S(1)}, f32[2,256,512]{2,1,0:T(8,128)S(1)}, u32[]{:S(2)}, u32[]{:S(2)}) %collective-permute-start.2) | collective-permute-done | bytes 1048608 | tf_op jit(solution)/shard_map/ppermute | solution.py:20
  144.6 12.6 %collective-permute-start.3 = (f32[2,256,256]{2,1,0:T(8,128)S(1)}, f32[2,256,256]{2,1,0:T(8,128)S(1)}, u32[]{:S(2)}, u32[]{:S(2)}) collective-permute-start(f32[2,256,256]{2,1,0:T(8,128)S(1)} %slice.119), channel_id=1, source_target_pairs={{0,1},{1,2},{2,3},{3,4},{4,5},{5,6},{6,7},{7,8},{8,9},{9,10},{10,1... | collective-permute-start | bytes 1572872 | tf_op jit(solution)/shard_map/ppermute | solution.py:20
  157.2 6.1 collective-permute-done.3
  166.8 8.3 %collective-permute-done.4 = f32[2,256,256]{2,1,0:T(8,128)S(1)} collective-permute-done((f32[2,256,256]{2,1,0:T(8,128)S(1)}, f32[2,256,256]{2,1,0:T(8,128)S(1)}, u32[]{:S(2)}, u32[]{:S(2)}) %collective-permute-start.4) | collective-permute-done | bytes 524320 | tf_op jit(solution)/shard_map/ppermute | solution.py:20
  177.9 254.6 %all-reduce.21.cloned.1.call-done = f32[2,3,256,256]{2,3,1,0:T(8,128)} async-done(((f32[2,3,256,256]{2,3,1,0:T(8,128)}), f32[2,3,256,256]{2,3,1,0:T(8,128)}) %all-reduce.21.cloned.1.call-update) | async-done | bytes 1572880 | tf_op jit(solution)/shard_map/psum | solution.py:116
  432.5 2.8 multiply_subtract_fusion.1
  460.1 2.6 fusion.9
  472.0 2.7 add_reduce_fusion
  487.8 3.1 multiply_reduce_fusion.2
  505.3 4.4 multiply_bitcast_fusion.3
  512.3 6.1 dynamic_update_slice.12
  520.8 4.4 collective-permute-start.6
  530.8 14.5 %collective-permute-done.6 = f32[2,256,512]{2,1,0:T(8,128)} collective-permute-done((f32[2,256,512]{2,1,0:T(8,128)}, f32[2,256,512]{2,1,0:T(8,128)}, u32[]{:S(2)}, u32[]{:S(2)}) %collective-permute-start.6) | collective-permute-done | bytes 1048608 | tf_op jit(solution)/shard_map/ppermute | solution.py:20
  548.0 6.1 collective-permute-start.7
  556.7 228.9 %all-reduce.23.cloned.1.call-done = f32[2,3,256,256]{2,3,1,0:T(8,128)} async-done(((f32[2,3,256,256]{2,3,1,0:T(8,128)}), f32[2,3,256,256]{2,3,1,0:T(8,128)}) %all-reduce.23.cloned.1.call-update) | async-done | bytes 1572880 | tf_op jit(solution)/shard_map/psum | solution.py:116
  785.6 2.8 multiply_subtract_fusion
  788.4 3.1 copy.121
  (146 shorter events, 159.3 us)
Async XLA Ops:
  7.2 14.2 %copy-start.18 = (s32[1,2]{1,0:T(1,128)S(1)}, s32[1,2]{1,0:T(1,128)}, u32[]{:S(2)}) copy-start(s32[1,2]{1,0:T(1,128)} %param.8) | copy-start | bytes 28
  7.2 17.4 %copy-start.19 = (s32[1,2]{1,0:T(1,128)S(1)}, s32[1,2]{1,0:T(1,128)}, u32[]{:S(2)}) copy-start(s32[1,2]{1,0:T(1,128)} %param.9) | copy-start | bytes 28
  7.2 425.3 %all-reduce.21.cloned.1.call-start = ((), (), s32[]{:S(2)}) async-start(), calls=%async_computation | async-start | bytes 3145728 | tf_op jit(solution)/shard_map/psum | solution.py:116
  7.2 12.0 %collective-permute-start = (f32[2,256,256]{2,1,0:T(8,128)}, f32[2,256,256]{2,1,0:T(8,128)S(1)}, u32[]{:S(2)}, u32[]{:S(2)}) collective-permute-start(f32[2,256,256]{2,1,0:T(8,128)} %param.5), channel_id=1, source_target_pairs={{1,0},{2,1},{3,2},{4,3},{5,4},{6,5},{7,6},{8,7},{9,8},{10,9},{11,1... | collective-permute-start | bytes 1572872 | tf_op jit(solution)/shard_map/ppermute | solution.py:20
  20.1 22.8 %collective-permute-start.1 = (f32[2,256,512]{2,1,0:T(8,128)}, f32[2,256,512]{2,1,0:T(8,128)}, u32[]{:S(2)}, u32[]{:S(2)}) collective-permute-start(f32[2,256,512]{2,1,0:T(8,128)} %constant_dynamic-update-slice_fusion), channel_id=1, source_target_pairs={{16,0},{32,16},{48,32},{64,48},{80,64},{96,80},{112,96},{128,112},... | collective-permute-start | bytes 3145736 | tf_op jit(solution)/shard_map/ppermute | solution.py:20
  77.4 2.7 copy-start.13
  121.5 22.8 %copy-start.1 = (f32[2,512,512]{2,1,0:T(8,128)S(1)}, f32[2,512,512]{2,1,0:T(8,128)}, u32[]{:S(2)}) copy-start(f32[2,512,512]{2,1,0:T(8,128)} %dynamic_update_slice.11) | copy-start | bytes 6291460
  123.0 40.3 %copy-start.12 = (f32[2,256,256]{2,1,0:T(8,128)S(1)}, f32[2,256,256]{2,1,0:T(8,128)}, u32[]{:S(2)}) copy-start(f32[2,256,256]{2,1,0:T(8,128)} %param.5) | copy-start | bytes 1572868
  123.0 21.3 %collective-permute-start.2 = (f32[2,256,512]{2,1,0:T(8,128)S(1)}, f32[2,256,512]{2,1,0:T(8,128)S(1)}, u32[]{:S(2)}, u32[]{:S(2)}) collective-permute-start(f32[2,256,512]{2,1,0:T(8,128)S(1)} %slice.117), channel_id=1, source_target_pairs={{0,16},{16,32},{32,48},{48,64},{64,80},{80,96},{96,112},{112,128},... | collective-permute-start | bytes 3145736 | tf_op jit(solution)/shard_map/ppermute | solution.py:20
  144.5 20.8 %copy-start.4 = (f32[1,3,256,256]{2,3,1,0:T(8,128)S(1)}, f32[1,3,256,256]{2,3,1,0:T(8,128)}, u32[]{:S(2)}) copy-start(f32[1,3,256,256]{2,3,1,0:T(8,128)} %get-tuple-element.86) | copy-start | bytes 2359300
  144.5 20.8 %copy-start.5 = (f32[1,3,256,256]{2,3,1,0:T(8,128)S(1)}, f32[1,3,256,256]{2,3,1,0:T(8,128)}, u32[]{:S(2)}) copy-start(f32[1,3,256,256]{2,3,1,0:T(8,128)} %get-tuple-element.87) | copy-start | bytes 2359300
  144.5 20.8 %copy-start.6 = (f32[1,3,256,256]{2,3,1,0:T(8,128)S(1)}, f32[1,3,256,256]{2,3,1,0:T(8,128)}, u32[]{:S(2)}) copy-start(f32[1,3,256,256]{2,3,1,0:T(8,128)} %get-tuple-element.92) | copy-start | bytes 2359300
  144.5 20.8 %copy-start.7 = (f32[1,3,256,256]{2,3,1,0:T(8,128)S(1)}, f32[1,3,256,256]{2,3,1,0:T(8,128)}, u32[]{:S(2)}) copy-start(f32[1,3,256,256]{2,3,1,0:T(8,128)} %get-tuple-element.93) | copy-start | bytes 2359300
  144.6 18.7 %collective-permute-start.3 = (f32[2,256,256]{2,1,0:T(8,128)S(1)}, f32[2,256,256]{2,1,0:T(8,128)S(1)}, u32[]{:S(2)}, u32[]{:S(2)}) collective-permute-start(f32[2,256,256]{2,1,0:T(8,128)S(1)} %slice.119), channel_id=1, source_target_pairs={{0,1},{1,2},{2,3},{3,4},{4,5},{5,6},{6,7},{7,8},{8,9},{9,10},{10,1... | collective-permute-start | bytes 1572872 | tf_op jit(solution)/shard_map/ppermute | solution.py:20
  163.4 11.6 %collective-permute-start.4 = (f32[2,256,256]{2,1,0:T(8,128)S(1)}, f32[2,256,256]{2,1,0:T(8,128)S(1)}, u32[]{:S(2)}, u32[]{:S(2)}) collective-permute-start(f32[2,256,256]{2,1,0:T(8,128)S(1)} %fusion.42), channel_id=1, source_target_pairs={{1,0},{2,1},{3,2},{4,3},{5,4},{6,5},{7,6},{8,7},{9,8},{10,9},{11,1... | collective-permute-start | bytes 1572872 | tf_op jit(solution)/shard_map/ppermute | solution.py:20
  166.8 618.9 %all-reduce.23.cloned.1.call-start = ((), (), s32[]{:S(2)}) async-start(), calls=%async_computation.1 | async-start | bytes 3145728 | tf_op jit(solution)/shard_map/psum | solution.py:116
  176.2 259.1 %collective-permute-start.5 = (f32[2,256,512]{2,1,0:T(8,128)}, f32[2,256,512]{2,1,0:T(8,128)}, u32[]{:S(2)}, u32[]{:S(2)}) collective-permute-start(f32[2,256,512]{2,1,0:T(8,128)} %pad_maximum_fusion), channel_id=1, source_target_pairs={{16,0},{32,16},{48,32},{64,48},{80,64},{96,80},{112,96},{128,112},... | collective-permute-start | bytes 3145736 | tf_op jit(solution)/shard_map/ppermute | solution.py:20
  436.9 2.0 copy-start
  512.3 12.9 %copy-start.8 = (f32[1,3,256,256]{2,3,1,0:T(8,128)S(1)}, f32[1,3,256,256]{2,3,1,0:T(8,128)}, u32[]{:S(2)}) copy-start(f32[1,3,256,256]{2,3,1,0:T(8,128)} %get-tuple-element.78) | copy-start | bytes 2359300
  518.4 6.8 copy-start.9
  518.4 6.8 copy-start.10
  520.8 24.5 %collective-permute-start.6 = (f32[2,256,512]{2,1,0:T(8,128)}, f32[2,256,512]{2,1,0:T(8,128)}, u32[]{:S(2)}, u32[]{:S(2)}) collective-permute-start(f32[2,256,512]{2,1,0:T(8,128)} %slice.125), channel_id=1, source_target_pairs={{0,16},{16,32},{32,48},{48,64},{64,80},{80,96},{96,112},{112,128},... | collective-permute-start | bytes 3145736 | tf_op jit(solution)/shard_map/ppermute | solution.py:20
  548.0 243.5 %collective-permute-start.7 = (f32[2,256,256]{2,1,0:T(8,128)S(1)}, f32[2,256,256]{2,1,0:T(8,128)S(1)}, u32[]{:S(2)}, u32[]{:S(2)}) collective-permute-start(f32[2,256,256]{2,1,0:T(8,128)S(1)} %slice.127), channel_id=1, source_target_pairs={{0,1},{1,2},{2,3},{3,4},{4,5},{5,6},{6,7},{7,8},{8,9},{9,10},{10,1... | collective-permute-start | bytes 1572872 | tf_op jit(solution)/shard_map/ppermute | solution.py:20
  788.4 3.1 copy-start.3
  (6 other events, 6.8 us)
Sparse Core Ops, SparseCore 0:
  166.9 265.5 all-reduce.20
  527.8 257.7 all-reduce.22
where the time goes:
time: 810 us; the launch traced here: 800 us
  waiting for transfers between devices  549 us (68%)
  matrix products  139 us (17%)
  starting transfers between devices  35.3 us (4%)
  local copies, waits for them, and re-layouts  33.7 us (4%)
  other arithmetic  22.4 us (3%)
  between operations  20.5 us (3%)
    psum x2, waiting for transfers between devices, per_device(): total_grad = lax.psum(grad_modes, ('tile', 'frame'))  484 us
    ppermute x8, waiting for transfers between devices, shifted(): lax.ppermute(value, axis, [(source, source + steps) for source in range(i...  65.2 us
    ppermute x8, starting transfers between devices, shifted(): lax.ppermute(value, axis, [(source, source + steps) for source in range(i...  35.3 us
    dot_general x8, matrix products, transform(): jnp.einsum('jk,mkl->mjl', sin_table, imag_part, precision=highest)  21.4 us
    dot_general x8, matrix products, transform(): jnp.einsum('jk,mkl->mjl', cos_table, real_part, precision=highest)  17.8 us
    dot_general x8, matrix products, transform(): jnp.einsum('mjl,lk->mjk', left_imag, cos_table, precision=highest)  17.1 us
    dot_general x8, matrix products, transform(): jnp.einsum('jk,mkl->mjl', sin_table, real_part, precision=highest)  17 us
    dot_general x8, matrix products, transform(): jnp.einsum('jk,mkl->mjl', cos_table, imag_part, precision=highest)  16.7 us
  transfers between devices with their start and end apart: 10, of which 8 were waited for; matrix products, arithmetic and copies ran while one was open for 3% of the time, Pallas kernels for 0%

commit v1 on v0

v1 whole, which is shorter than its diff:
```python
import math

import jax
import jax.numpy as jnp
import numpy as np
from jax import lax
from jax.experimental import pallas as pl
from jax.experimental.pallas import tpu as pltpu
from jax.sharding import PartitionSpec as P

DET = 256
HALF = 128
MODES = 3
RAMPS = 8
STRIP = 16

object_step = 0.05
probe_step = 0.5
fresnel = 0.25

F32 = jnp.float32
BF16 = jnp.bfloat16


def circulant_blocks(eigenvalues):
    counter = np.arange(DET)
    waves = np.exp(2j * np.pi * (np.outer(counter, counter) % DET) / DET)
    column = waves @ eigenvalues / DET
    full = column[(counter[:, None] - counter[None, :]) % DET]
    first, second = full[:HALF, :HALF], full[:HALF, HALF:]

    def real_form(block):
        return np.block([[block.real, -block.imag], [block.imag, block.real]])

    return np.stack([real_form((first + second) / 2), real_form((first - second) / 2)])


def split_table(table):
    table = table.astype(np.float32)
    high = table.astype(BF16)
    low = (table - high.astype(np.float32)).astype(BF16)
    return np.stack([high, low], axis=-3)


def shift_tables():
    counter = np.arange(DET)
    signed = np.where(counter < DET // 2, counter, counter - DET).astype(np.float64)
    chirp = -np.pi * fresnel * signed * signed / DET
    slope = -2j * np.pi * signed / DET
    plain, derived = [], []
    for step in range(RAMPS):
        factor = np.exp(1j * chirp + slope * (step / RAMPS))
        plain.append(circulant_blocks(factor))
        derived.append(circulant_blocks(slope * factor))
    plain, derived = np.stack(plain), np.stack(derived)
    slope_blocks = circulant_blocks(slope)
    turned = np.swapaxes(plain, -1, -2)
    return (
        split_table(plain),
        split_table(turned),
        split_table(derived),
        split_table(np.swapaxes(slope_blocks, -1, -2)),
    )


def split(value):
    high = value.astype(BF16)
    return high, (value - high.astype(F32)).astype(BF16)


def product(left, right):
    return lax.dot_general(
        left, right, (((1,), (0,)), ((), ())), preferred_element_type=F32
    )


def gradient_kernel(last, rate, *refs):
    refs = list(refs)
    take = lambda count: [refs.pop(0) for _ in range(count)]
    (scalars,) = take(1)
    if last:
        patch_in, merged, from_above, from_below, grad_before = take(5)
        total_mine, total_other = take(2)
    else:
        own, right, lower = take(3)
    probe, measured = take(2)
    plain0, turned0, plain1, turned1 = take(4)
    if last:
        derived0, slope1 = take(2)
    if last:
        grad_out, probe_out, keep_out, send_out, shift_out = take(5)
    else:
        grad_out, patch_out, keep_out, send_out = take(4)
    doubled, field, high, low, result, z_high, z_low, z_result = take(8)
    if last:
        slope_result, derived_result = take(2)

    row0, col0, core = scalars[0], scalars[1], scalars[2]

    def build(step, _):
        start = pl.multiple_of(step * STRIP, STRIP)
        rows = pl.ds(start, STRIP)
        again = pl.ds(start + DET, STRIP)
        row_at = lax.broadcasted_iota(jnp.int32, (STRIP, DET), 0) + start
        col_at = lax.broadcasted_iota(jnp.int32, (STRIP, DET), 1)
        if last:
            outside = ((row_at < row0) & (scalars[3] == 1)) | ((col_at < col0) & (scalars[4] == 1))
        for part in range(2):
            if last:
                moved = jnp.where(row_at >= row0, from_above[part, rows, :], from_below[part, rows, :])
                cells = patch_in[part, rows, :] - object_step * (merged[part, rows, :] + moved)
                cells = jnp.where(outside, 0.0, cells)
            else:
                cells = jnp.where(
                    row_at >= row0,
                    jnp.where(col_at >= col0, own[part, rows, :], right[part, rows, :]),
                    lower[part, rows, :],
                )
                patch_out[part, rows, :] = cells
            doubled[part, rows, :] = cells
            doubled[part, again, :] = cells
        if last:
            for mode in range(MODES):
                mine = total_mine[mode, rows, :]
                other = total_other[mode, rows, :]
                probe_out[0, mode, rows, :] = probe[0, mode, rows, :] - rate * jnp.where(core == 0, mine, other)
                probe_out[1, mode, rows, :] = probe[1, mode, rows, :] - rate * jnp.where(core == 0, other, mine)
        return 0

    lax.fori_loop(0, DET // STRIP, build, 0)
    modes = probe_out if last else probe
    back = lax.rem(DET - col0, DET)

    def rows_from(part, first):
        down = lax.rem(first, 8)
        at = pl.ds(pl.multiple_of(first - down, 8), STRIP + 8)
        return pltpu.roll(doubled[part, at, :], lax.rem(STRIP + 8 - down, STRIP + 8), 0)[:STRIP]

    def enter(step, _):
        start = pl.multiple_of(step * STRIP, STRIP)
        rows = pl.ds(start, STRIP)
        real = pltpu.roll(rows_from(0, row0 + start), back, 1)
        imag = pltpu.roll(rows_from(1, row0 + start), back, 1)
        field[0, rows, :] = real
        field[1, rows, :] = imag
        for mode in range(MODES):
            probe_real = modes[0, mode, rows, :]
            probe_imag = modes[1, mode, rows, :]
            exit_real = probe_real * real - probe_imag * imag
            exit_imag = probe_real * imag + probe_imag * real
            at = pl.ds(pl.multiple_of(mode * DET + start, STRIP), STRIP)
            for block, sign in ((0, 1.0), (1, -1.0)):
                both = jnp.concatenate(
                    [
                        exit_real[:, :HALF] + sign * exit_real[:, HALF:],
                        exit_imag[:, :HALF] + sign * exit_imag[:, HALF:],
                    ],
                    axis=1,
                )
                high[block, at, :], low[block, at, :] = split(both)
        return 0

    lax.fori_loop(0, DET // STRIP, enter, 0)

    def times_right(block, mode, table, where):
        at = pl.ds(mode * DET, DET)
        left_high, left_low = high[block, at, :], low[block, at, :]
        where[block, at, :] = (
            product(left_high, table[block, 0])
            + product(left_low, table[block, 0])
            + product(left_high, table[block, 1])
        )

    def times_left(block, mode, table, where):
        at = pl.ds(mode * DET, DET)
        right_high, right_low = z_high[block, :, at], z_low[block, :, at]
        where[block, :, at] = (
            product(table[block, 0], right_high)
            + product(table[block, 0], right_low)
            + product(table[block, 1], right_high)
        )

    for block in range(2):
        for mode in range(MODES):
            times_right(block, mode, turned1, result)
            if last:
                times_right(block, mode, slope1, slope_result)

    def rows_to_blocks(step, _):
        start = pl.multiple_of(step * STRIP, STRIP)
        for mode in range(MODES):
            top = pl.ds(pl.multiple_of(mode * DET + start, STRIP), STRIP)
            bottom = pl.ds(pl.multiple_of(mode * DET + HALF + start, STRIP), STRIP)
            sums = [(result[col, top, :] + result[col, bottom, :]) for col in range(2)]
            gaps = [(result[col, top, :] - result[col, bottom, :]) for col in range(2)]
            for block, pair in ((0, sums), (1, gaps)):
                for part in range(2):
                    lanes = slice(part * HALF, (part + 1) * HALF)
                    both = jnp.concatenate([pair[0][:, lanes], pair[1][:, lanes]], axis=1)
                    at = pl.ds(pl.multiple_of(part * HALF + start, STRIP), STRIP)
                    cols = pl.ds(mode * DET, DET)
                    z_high[block, at, cols], z_low[block, at, cols] = split(both)
        return 0

    lax.fori_loop(0, HALF // STRIP, rows_to_blocks, 0)

    for block in range(2):
        for mode in range(MODES):
            times_left(block, mode, plain0, z_result)
            if last:
                times_left(block, mode, derived0, derived_result)

    def misfits(step, running):
        start = pl.multiple_of(step * STRIP, STRIP)
        low_rows = pl.ds(start, STRIP)
        high_rows = pl.ds(pl.multiple_of(start + HALF, STRIP), STRIP)

        def waves(mode, part):
            at = pl.ds(pl.multiple_of(part * HALF + start, STRIP), STRIP)
            cols = pl.ds(mode * DET, DET)
            even, odd = z_result[0, at, cols], z_result[1, at, cols]

            def spread(value):
                return jnp.concatenate(
                    [value[:, :HALF] + value[:, HALF:], value[:, :HALF] - value[:, HALF:]], axis=1
                )

            return spread(even + odd), spread(even - odd)

        top_sum = bottom_sum = None
        held = []
        for mode in range(MODES):
            for part in range(2):
                top, bottom = waves(mode, part)
                held.append((mode, part, top, bottom))
                top_sum = top * top if top_sum is None else top_sum + top * top
                bottom_sum = bottom * bottom if bottom_sum is None else bottom_sum + bottom * bottom
        top_gap = 2.0 * (top_sum - measured[low_rows, :])
        bottom_gap = 2.0 * (bottom_sum - measured[high_rows, :])

        def fold(value):
            return jnp.concatenate(
                [value[:, :HALF] + value[:, HALF:], value[:, :HALF] - value[:, HALF:]], axis=1
            )

        for mode, part, top, bottom in held:
            top_grad = fold(top_gap * top)
            bottom_grad = fold(bottom_gap * bottom)
            at = pl.ds(pl.multiple_of(part * HALF + start, STRIP), STRIP)
            cols = pl.ds(mode * DET, DET)
            for block, both in ((0, top_grad + bottom_grad), (1, top_grad - bottom_grad)):
                z_high[block, at, cols], z_low[block, at, cols] = split(both)
                if last:
                    running = running + both * derived_result[block, at, cols]
        return running

    zeros = jnp.zeros((STRIP, DET), F32) if last else 0
    slope_rows = lax.fori_loop(0, HALF // STRIP, misfits, zeros)

    for block in range(2):
        for mode in range(MODES):
            times_left(block, mode, turned0, z_result)

    def blocks_to_rows(step, _):
        start = pl.multiple_of(step * STRIP, STRIP)
        for mode in range(MODES):
            cols = pl.ds(mode * DET, DET)
            tops, bottoms = [], []
            for part in range(2):
                at = pl.ds(pl.multiple_of(part * HALF + start, STRIP), STRIP)
                even, odd = z_result[0, at, cols], z_result[1, at, cols]
                tops.append(even + odd)
                bottoms.append(even - odd)
            for offset, pair in ((0, tops), (HALF, bottoms)):
                at = pl.ds(pl.multiple_of(mode * DET + offset + start, STRIP), STRIP)
                for block in range(2):
                    lanes = slice(block * HALF, (block + 1) * HALF)
                    both = jnp.concatenate([pair[0][:, lanes], pair[1][:, lanes]], axis=1)
                    high[block, at, :], low[block, at, :] = split(both)
        return 0

    lax.fori_loop(0, HALF // STRIP, blocks_to_rows, 0)

    for block in range(2):
        for mode in range(MODES):
            times_right(block, mode, plain1, result)

    def leave(step, running):
        start = pl.multiple_of(step * STRIP, STRIP)
        rows = pl.ds(start, STRIP)
        real, imag = field[0, rows, :], field[1, rows, :]
        grad_real = jnp.zeros((STRIP, DET), F32)
        grad_imag = jnp.zeros((STRIP, DET), F32)
        for mode in range(MODES):
            at = pl.ds(pl.multiple_of(mode * DET + start, STRIP), STRIP)
            even, odd = result[0, at, :], result[1, at, :]
            if last:
                running = running + even * slope_result[0, at, :] + odd * slope_result[1, at, :]
            plus, minus = even + odd, even - odd
            exit_real = jnp.concatenate([plus[:, :HALF], minus[:, :HALF]], axis=1)
            exit_imag = jnp.concatenate([plus[:, HALF:], minus[:, HALF:]], axis=1)
            probe_real = modes[0, mode, rows, :]
            probe_imag = modes[1, mode, rows, :]
            grad_real = grad_real + probe_real * exit_real + probe_imag * exit_imag
            grad_imag = grad_imag + probe_real * exit_imag - probe_imag * exit_real
            mode_real = real * exit_real + imag * exit_imag
            mode_imag = real * exit_imag - imag * exit_real
            keep_out[mode, rows, :] = jnp.where(core == 0, mode_real, mode_imag)
            send_out[mode, rows, :] = jnp.where(core == 0, mode_imag, mode_real)
        again = pl.ds(pl.multiple_of(start + DET, STRIP), STRIP)
        for part, value in ((0, grad_real), (1, grad_imag)):
            turned = pltpu.roll(value, col0, 1)
            doubled[part, rows, :] = turned
            doubled[part, again, :] = turned
        return running

    slope_cols = lax.fori_loop(0, DET // STRIP, leave, zeros)

    def wrap(step, _):
        start = pl.multiple_of(step * STRIP, STRIP)
        rows = pl.ds(start, STRIP)
        for part in range(2):
            value = rows_from(part, DET - row0 + start)
            if last:
                value = value + grad_before[part, rows, :]
            grad_out[part, rows, :] = value
        return 0

    lax.fori_loop(0, DET // STRIP, wrap, 0)

    if last:
        lane = lax.broadcasted_iota(jnp.int32, (8, HALF), 1)
        shift_out[...] = jnp.where(lane == 0, jnp.sum(slope_rows), 2.0 * jnp.sum(slope_cols)) / DET


def gradient_call(last, rate, scalars, operands):
    plane = jax.ShapeDtypeStruct((2, DET, DET), F32)
    half = jax.ShapeDtypeStruct((MODES, DET, DET), F32)
    vmem = pl.BlockSpec(memory_space=pltpu.VMEM)
    if last:
        outs = (
            plane,
            jax.ShapeDtypeStruct((2, MODES, DET, DET), F32),
            half,
            half,
            jax.ShapeDtypeStruct((8, HALF), F32),
        )
    else:
        outs = (plane, plane, half, half)
    scratch = [
        pltpu.VMEM((2, 2 * DET + 8, DET), F32),
        pltpu.VMEM((2, DET, DET), F32),
        pltpu.VMEM((2, MODES * DET, DET), BF16),
        pltpu.VMEM((2, MODES * DET, DET), BF16),
        pltpu.VMEM((2, MODES * DET, DET), F32),
        pltpu.VMEM((2, DET, MODES * DET), BF16),
        pltpu.VMEM((2, DET, MODES * DET), BF16),
        pltpu.VMEM((2, DET, MODES * DET), F32),
    ]
    if last:
        scratch += [
            pltpu.VMEM((2, MODES * DET, DET), F32),
            pltpu.VMEM((2, DET, MODES * DET), F32),
        ]

    def body(*refs):
        gradient_kernel(last, rate, *refs)

    return pl.pallas_call(
        body,
        out_shape=outs,
        in_specs=[pl.BlockSpec(memory_space=pltpu.SMEM)] + [vmem] * len(operands),
        out_specs=(vmem,) * len(outs),
        scratch_shapes=scratch,
        compiler_params=pltpu.CompilerParams(vmem_limit_bytes=40 * 2**20),
        name="gradient_last" if last else "gradient_first",
    )(scalars, *operands)


def shifted(value, axis, steps):
    count = lax.axis_size(axis)
    initial, last = (max(0, -steps), min(count, count - steps))
    return lax.ppermute(value, axis, [(source, source + steps) for source in range(initial, last)])


def swapped(value, axis, distance):
    count = lax.axis_size(axis)
    return lax.ppermute(value, axis, [(source, source ^ distance) for source in range(count)])


def reduced(keep, send):
    count = lax.axis_size("tile")
    summed = keep + swapped(send, "frame", 1)
    parts = summed.reshape(count, MODES * DET // count, DET)
    parts = lax.all_to_all(parts, "tile", 0, 0)
    part = jnp.sum(parts, axis=0)
    distance = 2
    while distance < lax.axis_size("frame"):
        part = part + swapped(part, "frame", distance)
        distance *= 2
    return part


def spread(part):
    count = lax.axis_size("tile")
    parts = jnp.broadcast_to(part[None], (count,) + part.shape)
    mine = lax.all_to_all(parts, "tile", 0, 0).reshape(MODES, DET, DET)
    return mine, swapped(mine, "frame", 1)


def per_device(object_field, probe_modes, measured, offsets, ramp_steps):
    tile_at, frame_at = lax.axis_index("tile"), lax.axis_index("frame")
    tile_last = lax.axis_size("tile") - 1
    frame_last = lax.axis_size("frame") - 1
    core = frame_at % 2
    rate = probe_step / (lax.axis_size("tile") * lax.axis_size("frame"))
    plain, turned, derived, slope = (jnp.asarray(table) for table in shift_tables())
    steps = ramp_steps[0]
    pick = lambda table, step: lax.dynamic_index_in_dim(table, step, 0, keepdims=False)
    plain0, turned0 = pick(plain, steps[0]), pick(turned, steps[0])
    plain1, turned1 = pick(plain, steps[1]), pick(turned, steps[1])
    derived0 = pick(derived, steps[0])

    here = offsets[0]
    above = shifted(offsets, "tile", 1)[0]
    below = shifted(offsets, "tile", -1)[0]
    left = shifted(offsets, "frame", 1)[0]
    right = shifted(offsets, "frame", -1)[0]
    scalars = jnp.stack(
        [
            here[0],
            here[1],
            core,
            (tile_at == tile_last).astype(jnp.int32),
            (frame_at == frame_last).astype(jnp.int32),
        ]
    )
    row = lax.broadcasted_iota(jnp.int32, (2, DET, DET), 1)
    col = lax.broadcasted_iota(jnp.int32, (2, DET, DET), 2)

    right_tile = shifted(object_field, "frame", -1)
    lower = shifted(jnp.where(col >= above[1], object_field, right_tile), "tile", -1)

    frame = measured[0]
    grad1, patch, keep1, send1 = gradient_call(
        False,
        rate,
        scalars,
        (object_field, right_tile, lower, probe_modes, frame, plain0, turned0, plain1, turned1),
    )

    grad_left = shifted(grad1, "frame", 1)
    grad_right = shifted(grad1, "frame", -1)
    left_cells = col < left[1]
    right_cells = col >= right[1]
    side_left = jnp.where(left_cells, grad_left, 0.0)
    side_right = jnp.where(right_cells, grad_right, 0.0)

    def rows_of(wanted, edge, value):
        return jnp.where((row < edge) == wanted, value, 0.0)

    def gathered(wanted, start):
        kept = rows_of(wanted, here[0], grad1)
        near = jnp.where(col >= here[1], kept, 0.0) + rows_of(wanted, left[0], side_left)
        far = jnp.where(col < here[1], kept, 0.0) + rows_of(wanted, right[0], side_right)
        return jnp.where(col >= start, near, far)

    inside = row < here[0]
    merged = grad1 + jnp.where(
        col >= here[1],
        jnp.where(inside == (row < left[0]), side_left, 0.0),
        jnp.where(inside == (row < right[0]), side_right, 0.0),
    )
    from_above = shifted(gathered(True, below[1]), "tile", 1)
    from_below = shifted(gathered(False, above[1]), "tile", -1)

    mine, other = spread(reduced(keep1, send1))

    grad_total, modes_now, keep2, send2, shift_grad = gradient_call(
        True,
        rate,
        scalars,
        (patch, merged, from_above, from_below, grad1, mine, other)
        + (probe_modes, frame, plain0, turned0, plain1, turned1, derived0, slope),
    )

    moved = shifted(jnp.where(row < here[0], grad_total, 0.0), "tile", 1)
    own_rows = jnp.where(row >= here[0], grad_total, 0.0)
    to_right = jnp.where(col < here[1], own_rows, 0.0) + jnp.where(col < above[1], moved, 0.0)
    stays = jnp.where(col >= here[1], own_rows, 0.0) + jnp.where(col >= above[1], moved, 0.0)
    object_final = object_field - object_step * (stays + shifted(to_right, "frame", 1))

    mine, other = spread(reduced(keep2, send2))
    first = jnp.where(core == 0, mine, other)
    second = jnp.where(core == 0, other, mine)
    probe_final = modes_now - rate * jnp.stack([first, second])
    return (object_final, probe_final, shift_grad[:1, :2])


def solution(mesh):
    placed = (
        P(None, "tile", "frame"),
        P(),
        P(("tile", "frame"), None, None),
        P(("tile", "frame"), None),
        P(("tile", "frame"), None),
    )
    return jax.shard_map(
        per_device,
        mesh=mesh,
        in_specs=placed,
        out_specs=(P(None, "tile", "frame"), P(), P(("tile", "frame"), None)),
        check_vma=False,
    )
```

time: 810 us -> 214 us (0.26); the launches traced: 800 us -> 213 us
  waiting for transfers between devices: 549 us -> 29.8 us
  matrix products: 139 us -> 0 us
  blocking collectives: 0 us -> 45.4 us
  starting transfers between devices: 35.3 us -> 77.9 us
  Pallas kernels: 0 us -> 20.9 us
  local copies, waits for them, and re-layouts: 33.7 us -> 15.1 us
  between operations: 20.5 us -> 5 us
    psum x2 -> x0, waiting for transfers between devices: 484 us -> none  [per_device(): total_grad = lax.psum(grad_modes, ('tile', 'frame'))]
    dot_general x64 -> x0, matrix products: 139 us -> none  [the longest x8 21.4 us: transform(): jnp.einsum('jk,mkl->mjl', sin_table, imag_part, precision=highest)]
    ppermute x8 -> x12, waiting for transfers between devices: 65.2 us -> 18.2 us  [shifted(): lax.ppermute(value, axis, [(source, source + steps) for source in range(i...]
    all_to_all x0 -> x2, blocking collectives: none -> 45.4 us  [reduced(): parts = lax.all_to_all(parts, 'tile', 0, 0)]
    ppermute x0 -> x10, starting transfers between devices: none -> 29.1 us  [swapped(): lax.ppermute(value, axis, [(source, source ^ distance) for source in rang...]
    pallas_call x0 -> x2, Pallas kernels: none -> 20.9 us  [gradient_call(): pl.pallas_call(body, out_shape=outs, in_specs=[pl.BlockSpec(memory_space=...]
    dynamic_update_slice x2 -> x0, local copies, waits for them, and re-layouts: 12 us -> none  [visit_frame(): lax.dynamic_update_slice(grad_window, current + grad_patch, anchor)]
    ppermute x0 -> x10, waiting for transfers between devices: none -> 11.2 us  [swapped(): lax.ppermute(value, axis, [(source, source ^ distance) for source in rang...]
  transfers between devices with their start and end apart: 10 -> 24, of which waited for: 8 -> 13; matrix products, arithmetic and copies ran while one was open for 3% -> 11% of each run, Pallas kernels for 0% -> 0%
where the time goes in v1:
time: 214 us; the launch traced here: 213 us
  starting transfers between devices  77.9 us (36%)
  blocking collectives  45.4 us (21%)
  waiting for transfers between devices  29.8 us (14%)
  Pallas kernels  20.9 us (10%)
  other arithmetic  18.6 us (9%)
  local copies, waits for them, and re-layouts  15.1 us (7%)
  between operations  5 us (2%)
    all_to_all x2, blocking collectives, reduced(): parts = lax.all_to_all(parts, 'tile', 0, 0)  45.4 us
    ppermute x12, starting transfers between devices, shifted(): lax.ppermute(value, axis, [(source, source + steps) for source in range(i...  38.4 us
    ppermute x10, starting transfers between devices, swapped(): lax.ppermute(value, axis, [(source, source ^ distance) for source in rang...  29.1 us
    pallas_call x2, Pallas kernels, gradient_call(): pl.pallas_call(body, out_shape=outs, in_specs=[pl.BlockSpec(memory_space=...  20.9 us
    ppermute x12, waiting for transfers between devices, shifted(): lax.ppermute(value, axis, [(source, source + steps) for source in range(i...  18.2 us
    ppermute x10, waiting for transfers between devices, swapped(): lax.ppermute(value, axis, [(source, source ^ distance) for source in rang...  11.2 us
    all_to_all x2, starting transfers between devices, spread(): mine = lax.all_to_all(parts, 'tile', 0, 0).reshape(MODES, DET, DET)  10.4 us
    unnamed x38, local copies, waits for them, and re-layouts  4.85 us
  transfers between devices with their start and end apart: 24, of which 13 were waited for; matrix products, arithmetic and copies ran while one was open for 11% of the time, Pallas kernels for 0%

profile of v1, /device:TPU:1, one launch (start us, length us, event | category | flops | bytes accessed | tf_op | source)
XLA Modules:
  0.0 212.6 jit_solution(14845029874088500098)
XLA Ops:
  0.7 5.3 %collective-permute-start = (f32[2,256,256]{2,1,0:T(8,128)}, f32[2,256,256]{2,1,0:T(8,128)S(1)}, u32[]{:S(2)}, u32[]{:S(2)}) collective-permute-start(f32[2,256,256]{2,1,0:T(8,128)} %refs_1_.1), channel_id=1, source_target_pairs={{1,0},{2,1},{3,2},{4,3},{5,4},{6,5},{7,6},{8,7},{9,8},{10,9},{11,1... | collective-permute-start | bytes 1572872 | tf_op jit(solution)/shard_map/ppermute | solution.py:383
  9.4 3.4 %collective-permute-done.refs_2_ = f32[2,256,256]{2,1,0:T(8,128)S(1)} collective-permute-done((f32[2,256,256]{2,1,0:T(8,128)}, f32[2,256,256]{2,1,0:T(8,128)S(1)}, u32[]{:S(2)}, u32[]{:S(2)}) %collective-permute-start) | collective-permute-done | bytes 524320 | tf_op jit(solution)/shard_map/ppermute | solution.py:383
  25.0 3.9 %collective-permute-done.2.refs_3_ = f32[2,256,256]{2,1,0:T(8,128)} collective-permute-done((f32[2,256,256]{2,1,0:T(8,128)}, f32[2,256,256]{2,1,0:T(8,128)}, u32[]{:S(2)}, u32[]{:S(2)}) %collective-permute-start.2) | collective-permute-done | bytes 524320 | tf_op jit(solution)/shard_map/ppermute | solution.py:383
  28.9 9.5 %gradient_first.1 = (f32[2,256,256]{2,1,0:T(8,128)S(1)}, f32[2,256,256]{2,1,0:T(8,128)S(1)}, f32[3,256,256]{2,1,0:T(8,128)S(1)}, f32[3,256,256]{2,1,0:T(8,128)S(1)}) custom-call(s32[5]{0:T(128)S(1)} %stack.32.refs_0_, f32[2,256,256]{2,1,0:T(8,128)S(1)} %copy-done.5, f32[2,256,256]{2,1,0:T(8,128)S(1)} %copy-done.10, ...), custom_call_target="tpu_custom_call" | custom-call | tf_op jit(solution)/shard_map/gradient_first/pallas_call | solution.py:369
  39.3 2.3 %collective-permute-done.10 = f32[3,256,256]{2,1,0:T(8,128)S(1)} collective-permute-done((f32[3,256,256]{2,1,0:T(8,128)S(1)}, f32[3,256,256]{2,1,0:T(8,128)S(1)}, u32[]{:S(2)}, u32[]{:S(2)}) %collective-permute-start.10) | collective-permute-done | bytes 786464 | tf_op jit(solution)/shard_map/ppermute | solution.py:388
  41.7 22.6 %all_to_all.20 = f32[16,48,256]{2,1,0:T(8,128)} all-to-all(f32[16,48,256]{2,1,0:T(8,128)S(1)} %bitcast.36), channel_id=1, replica_groups=mesh['tile'=16,'frame'=16] {'tile'}, dimensions={0} | all-to-all | bytes 1572864 | tf_op jit(solution)/shard_map/all_to_all | solution.py:395
  65.4 2.6 %collective-permute-start.11 = (f32[48,256]{1,0:T(8,128)S(1)}, f32[48,256]{1,0:T(8,128)S(1)}, u32[]{:S(2)}, u32[]{:S(2)}) collective-permute-start(f32[48,256]{1,0:T(8,128)S(1)} %reduce_sum.18), channel_id=1, source_target_pairs={{0,2},{1,3},{2,0},{3,1},{4,6},{5,7},{6,4},{7,5},{8,10},{9,11},{10,... | collective-permute-start | bytes 147464 | tf_op jit(solution)/shard_map/ppermute | solution.py:388
  68.0 3.4 %collective-permute-start.3 = (s32[1,2]{1,0:T(1,128)S(1)}, s32[1,2]{1,0:T(1,128)S(1)}, u32[]{:S(2)}, u32[]{:S(2)}) collective-permute-start(s32[1,2]{1,0:T(1,128)S(1)} %copy-done.18), channel_id=1, source_target_pairs={{0,1},{1,2},{2,3},{3,4},{4,5},{5,6},{6,7},{7,8},{8,9},{9,10},{10,1... | collective-permute-start | bytes 32 | tf_op jit(solution)/shard_map/ppermute | solution.py:383
  74.6 3.4 %collective-permute-start.12 = (f32[48,256]{1,0:T(8,128)S(1)}, f32[48,256]{1,0:T(8,128)S(1)}, u32[]{:S(2)}, u32[]{:S(2)}) collective-permute-start(f32[48,256]{1,0:T(8,128)S(1)} %add.71), channel_id=1, source_target_pairs={{0,4},{1,5},{2,6},{3,7},{4,0},{5,1},{6,2},{7,3},{8,12},{9,13},{10,... | collective-permute-start | bytes 147464 | tf_op jit(solution)/shard_map/ppermute | solution.py:388
  79.6 6.6 %collective-permute-start.13 = (f32[48,256]{1,0:T(8,128)S(1)}, f32[48,256]{1,0:T(8,128)S(1)}, u32[]{:S(2)}, u32[]{:S(2)}) collective-permute-start(f32[48,256]{1,0:T(8,128)S(1)} %add.72), channel_id=1, source_target_pairs={{0,8},{1,9},{2,10},{3,11},{4,12},{5,13},{6,14},{7,15},{8,0},{9,1},... | collective-permute-start | bytes 147464 | tf_op jit(solution)/shard_map/ppermute | solution.py:388
  88.6 4.9 %all-to-all-start.1 = ((f32[16,48,256]{2,1,0:T(8,128)}), f32[16,48,256]{2,1,0:T(8,128)}, u32[]{:S(2)}, u32[]{:S(2)}) async-start(f32[16,48,256]{2,1,0:T(8,128)} %broadcast_in_dim.36), calls=%async_computation.1 | async-start | bytes 1572864 | tf_op jit(solution)/shard_map/all_to_all | solution.py:407
  95.4 6.3 %collective-permute-start.6 = (f32[2,256,256]{2,1,0:T(8,128)}, f32[2,256,256]{2,1,0:T(8,128)}, u32[]{:S(2)}, u32[]{:S(2)}) collective-permute-start(f32[2,256,256]{2,1,0:T(8,128)} %copy-done.7), channel_id=1, source_target_pairs={{1,0},{2,1},{3,2},{4,3},{5,4},{6,5},{7,6},{8,7},{9,8},{10,9},{11,1... | collective-permute-start | bytes 1572872 | tf_op jit(solution)/shard_map/ppermute | solution.py:383
  113.4 4.2 %collective-permute-start.8 = (f32[2,256,256]{2,1,0:T(8,128)S(1)}, f32[2,256,256]{2,1,0:T(8,128)S(1)}, u32[]{:S(2)}, u32[]{:S(2)}) collective-permute-start(f32[2,256,256]{2,1,0:T(8,128)S(1)} %get-tuple-element.26), channel_id=1, source_target_pairs={{0,16},{16,32},{32,48},{48,64},{64,80},{80,96},{96,112},{112,128},... | collective-permute-start | bytes 1572872 | tf_op jit(solution)/shard_map/ppermute | solution.py:383
  118.6 9.2 %collective-permute-done.9.refs_4_ = f32[2,256,256]{2,1,0:T(8,128)S(1)} collective-permute-done((f32[2,256,256]{2,1,0:T(8,128)S(1)}, f32[2,256,256]{2,1,0:T(8,128)S(1)}, u32[]{:S(2)}, u32[]{:S(2)}) %collective-permute-start.9) | collective-permute-done | bytes 524320 | tf_op jit(solution)/shard_map/ppermute | solution.py:383
  128.7 11.4 %gradient_last.1 = (f32[2,256,256]{2,1,0:T(8,128)S(1)}, f32[2,3,256,256]{3,2,1,0:T(8,128)S(1)}, f32[3,256,256]{2,1,0:T(8,128)S(1)}, f32[3,256,256]{2,1,0:T(8,128)S(1)}, f32[8,128]{1,0:T(8,128)S(1)}) custom-call(s32[5]{0:T(128)S(1)} %stack.32.refs_0_, f32[2,256,256]{2,1,0:T(8,128)S(1)} %copy-done.16, f32[2,256,256]{2,1,0:T(8,128)S(1)} %get-tuple-element.27.refs_2_, ...), custom_call_target="tpu_custom_call" | custom-call | tf_op jit(solution)/shard_map/gradient_last/pallas_call | solution.py:369
  145.0 22.8 %all_to_all.21 = f32[16,48,256]{2,1,0:T(8,128)S(1)} all-to-all(f32[16,48,256]{2,1,0:T(8,128)S(1)} %bitcast.37), channel_id=1, replica_groups=mesh['tile'=16,'frame'=16] {'tile'}, dimensions={0} | all-to-all | bytes 1572864 | tf_op jit(solution)/shard_map/all_to_all | solution.py:395
  170.9 4.7 %collective-permute-start.19 = (f32[48,256]{1,0:T(8,128)S(1)}, f32[48,256]{1,0:T(8,128)S(1)}, u32[]{:S(2)}, u32[]{:S(2)}) collective-permute-start(f32[48,256]{1,0:T(8,128)S(1)} %add.78), channel_id=1, source_target_pairs={{0,4},{1,5},{2,6},{3,7},{4,0},{5,1},{6,2},{7,3},{8,12},{9,13},{10,... | collective-permute-start | bytes 147464 | tf_op jit(solution)/shard_map/ppermute | solution.py:388
  175.7 2.2 %collective-permute-start.15 = (f32[2,256,256]{2,1,0:T(8,128)S(1)}, f32[2,256,256]{2,1,0:T(8,128)S(1)}, u32[]{:S(2)}, u32[]{:S(2)}) collective-permute-start(f32[2,256,256]{2,1,0:T(8,128)S(1)} %broadcast_select_fusion), channel_id=1, source_target_pairs={{0,16},{16,32},{32,48},{48,64},{64,80},{80,96},{96,112},{112,128},... | collective-permute-start | bytes 1572872 | tf_op jit(solution)/shard_map/ppermute | solution.py:383
  178.0 2.8 %collective-permute-start.20 = (f32[48,256]{1,0:T(8,128)S(1)}, f32[48,256]{1,0:T(8,128)S(1)}, u32[]{:S(2)}, u32[]{:S(2)}) collective-permute-start(f32[48,256]{1,0:T(8,128)S(1)} %add.79), channel_id=1, source_target_pairs={{0,8},{1,9},{2,10},{3,11},{4,12},{5,13},{6,14},{7,15},{8,0},{9,1},... | collective-permute-start | bytes 147464 | tf_op jit(solution)/shard_map/ppermute | solution.py:388
  180.8 4.1 %collective-permute-done.20 = f32[48,256]{1,0:T(8,128)S(1)} collective-permute-done((f32[48,256]{1,0:T(8,128)S(1)}, f32[48,256]{1,0:T(8,128)S(1)}, u32[]{:S(2)}, u32[]{:S(2)}) %collective-permute-start.20) | collective-permute-done | bytes 49184 | tf_op jit(solution)/shard_map/ppermute | solution.py:388
  185.9 5.5 %all-to-all-start.3 = ((f32[16,48,256]{2,1,0:T(8,128)}), f32[16,48,256]{2,1,0:T(8,128)S(1)}, u32[]{:S(2)}, u32[]{:S(2)}) async-start(f32[16,48,256]{2,1,0:T(8,128)} %broadcast_in_dim.37), calls=%async_computation.3 | async-start | bytes 1572864 | tf_op jit(solution)/shard_map/all_to_all | solution.py:407
  193.5 7.9 %collective-permute-start.16 = (f32[2,256,256]{2,1,0:T(8,128)}, f32[2,256,256]{2,1,0:T(8,128)}, u32[]{:S(2)}, u32[]{:S(2)}) collective-permute-start(f32[2,256,256]{2,1,0:T(8,128)} %select_add_fusion), channel_id=1, source_target_pairs={{0,1},{1,2},{2,3},{3,4},{4,5},{5,6},{6,7},{7,8},{8,9},{9,10},{10,1... | collective-permute-start | bytes 1572872 | tf_op jit(solution)/shard_map/ppermute | solution.py:383
  201.8 5.4 %collective-permute-start.21 = (f32[3,256,256]{2,1,0:T(8,128)S(1)}, f32[3,256,256]{2,1,0:T(8,128)S(1)}, u32[]{:S(2)}, u32[]{:S(2)}) collective-permute-start(f32[3,256,256]{2,1,0:T(8,128)S(1)} %bitcast.38), channel_id=1, source_target_pairs={{0,1},{1,0},{2,3},{3,2},{4,5},{5,4},{6,7},{7,6},{8,9},{9,8},{10,11... | collective-permute-start | bytes 2359304 | tf_op jit(solution)/shard_map/ppermute | solution.py:388
  207.9 2.0 multiply_subtract_fusion
  (105 shorter events, 51.3 us)
Async XLA Ops:
  0.7 12.1 %collective-permute-start = (f32[2,256,256]{2,1,0:T(8,128)}, f32[2,256,256]{2,1,0:T(8,128)S(1)}, u32[]{:S(2)}, u32[]{:S(2)}) collective-permute-start(f32[2,256,256]{2,1,0:T(8,128)} %refs_1_.1), channel_id=1, source_target_pairs={{1,0},{2,1},{3,2},{4,3},{5,4},{6,5},{7,6},{8,7},{9,8},{10,9},{11,1... | collective-permute-start | bytes 1572872 | tf_op jit(solution)/shard_map/ppermute | solution.py:383
  5.9 2.3 %collective-permute-start.1 = (s32[1,2]{1,0:T(1,128)}, s32[1,2]{1,0:T(1,128)S(1)}, u32[]{:S(2)}, u32[]{:S(2)}) collective-permute-start(s32[1,2]{1,0:T(1,128)} %param.12), channel_id=1, source_target_pairs={{0,16},{16,32},{32,48},{48,64},{64,80},{80,96},{96,112},{112,128},... | collective-permute-start | bytes 32 | tf_op jit(solution)/shard_map/ppermute | solution.py:383
  15.5 13.4 %collective-permute-start.2 = (f32[2,256,256]{2,1,0:T(8,128)}, f32[2,256,256]{2,1,0:T(8,128)}, u32[]{:S(2)}, u32[]{:S(2)}) collective-permute-start(f32[2,256,256]{2,1,0:T(8,128)} %broadcast_select_fusion.1), channel_id=1, source_target_pairs={{16,0},{32,16},{48,32},{64,48},{80,64},{96,80},{112,96},{128,112},... | collective-permute-start | bytes 1572872 | tf_op jit(solution)/shard_map/ppermute | solution.py:383
  39.3 2.3 %collective-permute-start.10 = (f32[3,256,256]{2,1,0:T(8,128)S(1)}, f32[3,256,256]{2,1,0:T(8,128)S(1)}, u32[]{:S(2)}, u32[]{:S(2)}) collective-permute-start(f32[3,256,256]{2,1,0:T(8,128)S(1)} %get-tuple-element.15), channel_id=1, source_target_pairs={{0,1},{1,0},{2,3},{3,2},{4,5},{5,4},{6,7},{7,6},{8,9},{9,8},{10,11... | collective-permute-start | bytes 2359304 | tf_op jit(solution)/shard_map/ppermute | solution.py:388
  65.4 9.2 %collective-permute-start.11 = (f32[48,256]{1,0:T(8,128)S(1)}, f32[48,256]{1,0:T(8,128)S(1)}, u32[]{:S(2)}, u32[]{:S(2)}) collective-permute-start(f32[48,256]{1,0:T(8,128)S(1)} %reduce_sum.18), channel_id=1, source_target_pairs={{0,2},{1,3},{2,0},{3,1},{4,6},{5,7},{6,4},{7,5},{8,10},{9,11},{10,... | collective-permute-start | bytes 147464 | tf_op jit(solution)/shard_map/ppermute | solution.py:388
  68.0 25.5 %collective-permute-start.3 = (s32[1,2]{1,0:T(1,128)S(1)}, s32[1,2]{1,0:T(1,128)S(1)}, u32[]{:S(2)}, u32[]{:S(2)}) collective-permute-start(s32[1,2]{1,0:T(1,128)S(1)} %copy-done.18), channel_id=1, source_target_pairs={{0,1},{1,2},{2,3},{3,4},{4,5},{5,6},{6,7},{7,8},{8,9},{9,10},{10,1... | collective-permute-start | bytes 32 | tf_op jit(solution)/shard_map/ppermute | solution.py:383
  71.4 15.4 %collective-permute-start.7 = (s32[1,2]{1,0:T(1,128)S(1)}, s32[1,2]{1,0:T(1,128)S(1)}, u32[]{:S(2)}, u32[]{:S(2)}) collective-permute-start(s32[1,2]{1,0:T(1,128)S(1)} %copy-done.18), channel_id=1, source_target_pairs={{16,0},{32,16},{48,32},{64,48},{80,64},{96,80},{112,96},{128,112},... | collective-permute-start | bytes 32 | tf_op jit(solution)/shard_map/ppermute | solution.py:383
  72.7 31.6 %collective-permute-start.5 = (s32[1,2]{1,0:T(1,128)S(1)}, s32[1,2]{1,0:T(1,128)S(1)}, u32[]{:S(2)}, u32[]{:S(2)}) collective-permute-start(s32[1,2]{1,0:T(1,128)S(1)} %copy-done.18), channel_id=1, source_target_pairs={{1,0},{2,1},{3,2},{4,3},{5,4},{6,5},{7,6},{8,7},{9,8},{10,9},{11,1... | collective-permute-start | bytes 32 | tf_op jit(solution)/shard_map/ppermute | solution.py:383
  74.6 4.9 %collective-permute-start.12 = (f32[48,256]{1,0:T(8,128)S(1)}, f32[48,256]{1,0:T(8,128)S(1)}, u32[]{:S(2)}, u32[]{:S(2)}) collective-permute-start(f32[48,256]{1,0:T(8,128)S(1)} %add.71), channel_id=1, source_target_pairs={{0,4},{1,5},{2,6},{3,7},{4,0},{5,1},{6,2},{7,3},{8,12},{9,13},{10,... | collective-permute-start | bytes 147464 | tf_op jit(solution)/shard_map/ppermute | solution.py:388
  79.6 8.1 %collective-permute-start.13 = (f32[48,256]{1,0:T(8,128)S(1)}, f32[48,256]{1,0:T(8,128)S(1)}, u32[]{:S(2)}, u32[]{:S(2)}) collective-permute-start(f32[48,256]{1,0:T(8,128)S(1)} %add.72), channel_id=1, source_target_pairs={{0,8},{1,9},{2,10},{3,11},{4,12},{5,13},{6,14},{7,15},{8,0},{9,1},... | collective-permute-start | bytes 147464 | tf_op jit(solution)/shard_map/ppermute | solution.py:388
  88.6 20.1 %all-to-all-start.1 = ((f32[16,48,256]{2,1,0:T(8,128)}), f32[16,48,256]{2,1,0:T(8,128)}, u32[]{:S(2)}, u32[]{:S(2)}) async-start(f32[16,48,256]{2,1,0:T(8,128)} %broadcast_in_dim.36), calls=%async_computation.1 | async-start | bytes 1572864 | tf_op jit(solution)/shard_map/all_to_all | solution.py:407
  95.4 14.7 %collective-permute-start.6 = (f32[2,256,256]{2,1,0:T(8,128)}, f32[2,256,256]{2,1,0:T(8,128)}, u32[]{:S(2)}, u32[]{:S(2)}) collective-permute-start(f32[2,256,256]{2,1,0:T(8,128)} %copy-done.7), channel_id=1, source_target_pairs={{1,0},{2,1},{3,2},{4,3},{5,4},{6,5},{7,6},{8,7},{9,8},{10,9},{11,1... | collective-permute-start | bytes 1572872 | tf_op jit(solution)/shard_map/ppermute | solution.py:383
  101.7 8.4 %collective-permute-start.4 = (f32[2,256,256]{2,1,0:T(8,128)}, f32[2,256,256]{2,1,0:T(8,128)}, u32[]{:S(2)}, u32[]{:S(2)}) collective-permute-start(f32[2,256,256]{2,1,0:T(8,128)} %copy-done.7), channel_id=1, source_target_pairs={{0,1},{1,2},{2,3},{3,4},{4,5},{5,6},{6,7},{7,8},{8,9},{9,10},{10,1... | collective-permute-start | bytes 1572872 | tf_op jit(solution)/shard_map/ppermute | solution.py:383
  108.7 19.9 %collective-permute-start.14 = (f32[3,256,256]{2,1,0:T(8,128)}, f32[3,256,256]{2,1,0:T(8,128)S(1)}, u32[]{:S(2)}, u32[]{:S(2)}) collective-permute-start(f32[3,256,256]{2,1,0:T(8,128)} %bitcast.21.refs_6_), channel_id=1, source_target_pairs={{0,1},{1,0},{2,3},{3,2},{4,5},{5,4},{6,7},{7,6},{8,9},{9,8},{10,11... | collective-permute-start | bytes 2359304 | tf_op jit(solution)/shard_map/ppermute | solution.py:388
  112.1 15.7 %collective-permute-start.9 = (f32[2,256,256]{2,1,0:T(8,128)S(1)}, f32[2,256,256]{2,1,0:T(8,128)S(1)}, u32[]{:S(2)}, u32[]{:S(2)}) collective-permute-start(f32[2,256,256]{2,1,0:T(8,128)S(1)} %get-tuple-element.25), channel_id=1, source_target_pairs={{16,0},{32,16},{48,32},{64,48},{80,64},{96,80},{112,96},{128,112},... | collective-permute-start | bytes 1572872 | tf_op jit(solution)/shard_map/ppermute | solution.py:383
  113.4 15.3 %collective-permute-start.8 = (f32[2,256,256]{2,1,0:T(8,128)S(1)}, f32[2,256,256]{2,1,0:T(8,128)S(1)}, u32[]{:S(2)}, u32[]{:S(2)}) collective-permute-start(f32[2,256,256]{2,1,0:T(8,128)S(1)} %get-tuple-element.26), channel_id=1, source_target_pairs={{0,16},{16,32},{32,48},{48,64},{64,80},{80,96},{96,112},{112,128},... | collective-permute-start | bytes 1572872 | tf_op jit(solution)/shard_map/ppermute | solution.py:383
  142.0 2.9 %collective-permute-start.17 = (f32[3,256,256]{2,1,0:T(8,128)S(1)}, f32[3,256,256]{2,1,0:T(8,128)S(1)}, u32[]{:S(2)}, u32[]{:S(2)}) collective-permute-start(f32[3,256,256]{2,1,0:T(8,128)S(1)} %get-tuple-element.19), channel_id=1, source_target_pairs={{0,1},{1,0},{2,3},{3,2},{4,5},{5,4},{6,7},{7,6},{8,9},{9,8},{10,11... | collective-permute-start | bytes 2359304 | tf_op jit(solution)/shard_map/ppermute | solution.py:388
  167.9 3.0 %collective-permute-start.18 = (f32[48,256]{1,0:T(8,128)S(1)}, f32[48,256]{1,0:T(8,128)S(1)}, u32[]{:S(2)}, u32[]{:S(2)}) collective-permute-start(f32[48,256]{1,0:T(8,128)S(1)} %reduce_sum.19), channel_id=1, source_target_pairs={{0,2},{1,3},{2,0},{3,1},{4,6},{5,7},{6,4},{7,5},{8,10},{9,11},{10,... | collective-permute-start | bytes 147464 | tf_op jit(solution)/shard_map/ppermute | solution.py:388
  170.9 7.0 %collective-permute-start.19 = (f32[48,256]{1,0:T(8,128)S(1)}, f32[48,256]{1,0:T(8,128)S(1)}, u32[]{:S(2)}, u32[]{:S(2)}) collective-permute-start(f32[48,256]{1,0:T(8,128)S(1)} %add.78), channel_id=1, source_target_pairs={{0,4},{1,5},{2,6},{3,7},{4,0},{5,1},{6,2},{7,3},{8,12},{9,13},{10,... | collective-permute-start | bytes 147464 | tf_op jit(solution)/shard_map/ppermute | solution.py:388
  175.7 16.9 %collective-permute-start.15 = (f32[2,256,256]{2,1,0:T(8,128)S(1)}, f32[2,256,256]{2,1,0:T(8,128)S(1)}, u32[]{:S(2)}, u32[]{:S(2)}) collective-permute-start(f32[2,256,256]{2,1,0:T(8,128)S(1)} %broadcast_select_fusion), channel_id=1, source_target_pairs={{0,16},{16,32},{32,48},{48,64},{64,80},{80,96},{96,112},{112,128},... | collective-permute-start | bytes 1572872 | tf_op jit(solution)/shard_map/ppermute | solution.py:383
  178.0 6.9 %collective-permute-start.20 = (f32[48,256]{1,0:T(8,128)S(1)}, f32[48,256]{1,0:T(8,128)S(1)}, u32[]{:S(2)}, u32[]{:S(2)}) collective-permute-start(f32[48,256]{1,0:T(8,128)S(1)} %add.79), channel_id=1, source_target_pairs={{0,8},{1,9},{2,10},{3,11},{4,12},{5,13},{6,14},{7,15},{8,0},{9,1},... | collective-permute-start | bytes 147464 | tf_op jit(solution)/shard_map/ppermute | solution.py:388
  185.9 16.0 %all-to-all-start.3 = ((f32[16,48,256]{2,1,0:T(8,128)}), f32[16,48,256]{2,1,0:T(8,128)S(1)}, u32[]{:S(2)}, u32[]{:S(2)}) async-start(f32[16,48,256]{2,1,0:T(8,128)} %broadcast_in_dim.37), calls=%async_computation.3 | async-start | bytes 1572864 | tf_op jit(solution)/shard_map/all_to_all | solution.py:407
  193.5 14.3 %collective-permute-start.16 = (f32[2,256,256]{2,1,0:T(8,128)}, f32[2,256,256]{2,1,0:T(8,128)}, u32[]{:S(2)}, u32[]{:S(2)}) collective-permute-start(f32[2,256,256]{2,1,0:T(8,128)} %select_add_fusion), channel_id=1, source_target_pairs={{0,1},{1,2},{2,3},{3,4},{4,5},{5,6},{6,7},{7,8},{8,9},{9,10},{10,1... | collective-permute-start | bytes 1572872 | tf_op jit(solution)/shard_map/ppermute | solution.py:383
  201.8 8.1 %collective-permute-start.21 = (f32[3,256,256]{2,1,0:T(8,128)S(1)}, f32[3,256,256]{2,1,0:T(8,128)S(1)}, u32[]{:S(2)}, u32[]{:S(2)}) collective-permute-start(f32[3,256,256]{2,1,0:T(8,128)S(1)} %bitcast.38), channel_id=1, source_target_pairs={{0,1},{1,0},{2,3},{3,2},{4,5},{5,4},{6,7},{7,6},{8,9},{9,8},{10,11... | collective-permute-start | bytes 2359304 | tf_op jit(solution)/shard_map/ppermute | solution.py:388
  (19 other events, 207.2 us)

commit v2 on v1

--- a/solution.py
+++ b/solution.py
@@ -55,12 +55,8 @@
     plain, derived = np.stack(plain), np.stack(derived)
     slope_blocks = circulant_blocks(slope)
     turned = np.swapaxes(plain, -1, -2)
-    return (
-        split_table(plain),
-        split_table(turned),
-        split_table(derived),
-        split_table(np.swapaxes(slope_blocks, -1, -2)),
-    )
+    order = (plain, turned, derived, np.swapaxes(slope_blocks, -1, -2)[None])
+    return np.concatenate([split_table(table) for table in order])
 
 
 def split(value):
@@ -77,16 +73,13 @@
 def gradient_kernel(last, rate, *refs):
     refs = list(refs)
     take = lambda count: [refs.pop(0) for _ in range(count)]
-    (scalars,) = take(1)
+    corner, ramp, place = take(3)
     if last:
         patch_in, merged, from_above, from_below, grad_before = take(5)
         total_mine, total_other = take(2)
     else:
-        own, right, lower = take(3)
-    probe, measured = take(2)
-    plain0, turned0, plain1, turned1 = take(4)
-    if last:
-        derived0, slope1 = take(2)
+        own, first_low, first_side, second_low, second_side = take(5)
+    probe_kept, measured_kept, tables = take(3)
     if last:
         grad_out, probe_out, keep_out, send_out, shift_out = take(5)
     else:
@@ -94,8 +87,29 @@
     doubled, field, high, low, result, z_high, z_low, z_result = take(8)
     if last:
         slope_result, derived_result = take(2)
-
-    row0, col0, core = scalars[0], scalars[1], scalars[2]
+    probe, measured, plain0, turned0, plain1, turned1 = take(6)
+    if last:
+        derived0, slope1 = take(2)
+    (arrived,) = take(1)
+
+    row0, col0, core = corner[0, 0], corner[0, 1], place[0]
+    step0, step1 = ramp[0, 0], ramp[0, 1]
+    moves = [
+        (probe_kept, probe),
+        (tables.at[RAMPS + step1], turned1),
+        (tables.at[step0], plain0),
+        (measured_kept.at[0], measured),
+        (tables.at[RAMPS + step0], turned0),
+        (tables.at[step1], plain1),
+    ]
+    if last:
+        moves += [(tables.at[2 * RAMPS + step0], derived0), (tables.at[3 * RAMPS], slope1)]
+    copies = [
+        pltpu.make_async_copy(source, target, arrived.at[index])
+        for index, (source, target) in enumerate(moves)
+    ]
+    for copy in copies:
+        copy.start()
 
     def build(step, _):
         start = pl.multiple_of(step * STRIP, STRIP)
@@ -104,18 +118,20 @@
         row_at = lax.broadcasted_iota(jnp.int32, (STRIP, DET), 0) + start
         col_at = lax.broadcasted_iota(jnp.int32, (STRIP, DET), 1)
         if last:
-            outside = ((row_at < row0) & (scalars[3] == 1)) | ((col_at < col0) & (scalars[4] == 1))
+            outside = ((row_at < row0) & (place[1] == 1)) | ((col_at < col0) & (place[2] == 1))
         for part in range(2):
             if last:
                 moved = jnp.where(row_at >= row0, from_above[part, rows, :], from_below[part, rows, :])
                 cells = patch_in[part, rows, :] - object_step * (merged[part, rows, :] + moved)
                 cells = jnp.where(outside, 0.0, cells)
             else:
-                cells = jnp.where(
-                    row_at >= row0,
-                    jnp.where(col_at >= col0, own[part, rows, :], right[part, rows, :]),
-                    lower[part, rows, :],
-                )
+                mine = own[part, rows, :]
+                if part == 0:
+                    column = jnp.where(row_at >= row0, mine, first_low[rows, :])
+                    cells = jnp.where(col_at >= col0, column, first_side[rows, :])
+                else:
+                    line = jnp.where(col_at >= col0, mine, second_side[rows, :])
+                    cells = jnp.where(row_at >= row0, line, second_low[rows, :])
                 patch_out[part, rows, :] = cells
             doubled[part, rows, :] = cells
             doubled[part, again, :] = cells
@@ -127,7 +143,11 @@
                 probe_out[1, mode, rows, :] = probe[1, mode, rows, :] - rate * jnp.where(core == 0, other, mine)
         return 0
 
+    if last:
+        copies[0].wait()
     lax.fori_loop(0, DET // STRIP, build, 0)
+    if not last:
+        copies[0].wait()
     modes = probe_out if last else probe
     back = lax.rem(DET - col0, DET)
 
@@ -161,6 +181,8 @@
         return 0
 
     lax.fori_loop(0, DET // STRIP, enter, 0)
+    for copy in copies[1:]:
+        copy.wait()
 
     def times_right(block, mode, table, where):
         at = pl.ds(mode * DET, DET)
@@ -333,10 +355,11 @@
         shift_out[...] = jnp.where(lane == 0, jnp.sum(slope_rows), 2.0 * jnp.sum(slope_cols)) / DET
 
 
-def gradient_call(last, rate, scalars, operands):
+def gradient_call(last, rate, scalars, operands, kept):
     plane = jax.ShapeDtypeStruct((2, DET, DET), F32)
     half = jax.ShapeDtypeStruct((MODES, DET, DET), F32)
     vmem = pl.BlockSpec(memory_space=pltpu.VMEM)
+    smem = pl.BlockSpec(memory_space=pltpu.SMEM)
     if last:
         outs = (
             plane,
@@ -362,6 +385,10 @@
             pltpu.VMEM((2, MODES * DET, DET), F32),
             pltpu.VMEM((2, DET, MODES * DET), F32),
         ]
+    scratch += [pltpu.VMEM((2, MODES, DET, DET), F32), pltpu.VMEM((DET, DET), F32)]
+    tables = 6 if last else 4
+    scratch += [pltpu.VMEM((2, 2, DET, DET), BF16)] * tables
+    scratch += [pltpu.SemaphoreType.DMA((tables + 2,))]
 
     def body(*refs):
         gradient_kernel(last, rate, *refs)
@@ -369,12 +396,101 @@
     return pl.pallas_call(
         body,
         out_shape=outs,
-        in_specs=[pl.BlockSpec(memory_space=pltpu.SMEM)] + [vmem] * len(operands),
+        in_specs=[smem] * len(scalars)
+        + [vmem] * len(operands)
+        + [pl.BlockSpec(memory_space=pltpu.HBM)] * len(kept),
         out_specs=(vmem,) * len(outs),
         scratch_shapes=scratch,
-        compiler_params=pltpu.CompilerParams(vmem_limit_bytes=40 * 2**20),
+        compiler_params=pltpu.CompilerParams(vmem_limit_bytes=(44 if last else 46) * 2**20),
         name="gradient_last" if last else "gradient_first",
-    )(scalars, *operands)
+    )(*scalars, *operands, *kept)
+
+
+def plane_call(name, body, scalars, operands, outputs):
+    def kernel(*refs):
+        at_scalars, refs = refs[: len(scalars)], refs[len(scalars) :]
+
+        def strip(step, _):
+            start = pl.multiple_of(step * STRIP, STRIP)
+            row = lax.broadcasted_iota(jnp.int32, (STRIP, DET), 0) + start
+            col = lax.broadcasted_iota(jnp.int32, (STRIP, DET), 1)
+            for part in range(2):
+                at = (part, pl.ds(start, STRIP), slice(None))
+                values = [ref[at] for ref in refs[: len(operands)]]
+                for ref, value in zip(refs[len(operands) :], body(at_scalars, row, col, *values)):
+                    ref[at] = value
+            return 0
+
+        lax.fori_loop(0, DET // STRIP, strip, 0)
+
+    vmem = pl.BlockSpec(memory_space=pltpu.VMEM)
+    return pl.pallas_call(
+        kernel,
+        out_shape=[jax.ShapeDtypeStruct((2, DET, DET), F32)] * outputs,
+        in_specs=[pl.BlockSpec(memory_space=pltpu.SMEM)] * len(scalars) + [vmem] * len(operands),
+        out_specs=[vmem] * outputs,
+        compiler_params=pltpu.CompilerParams(vmem_limit_bytes=8 * 2**20),
+        name=name,
+    )(*scalars, *operands)
+
+
+def side_kernel(left_at, above_at, own, lower, right, to_left, to_above):
+    def strip(step, _):
+        start = pl.multiple_of(step * STRIP, STRIP)
+        rows = pl.ds(start, STRIP)
+        row = lax.broadcasted_iota(jnp.int32, (STRIP, DET), 0) + start
+        col = lax.broadcasted_iota(jnp.int32, (STRIP, DET), 1)
+        to_left[rows, :] = jnp.where(row >= left_at[0, 0], own[0, rows, :], lower[rows, :])
+        to_above[rows, :] = jnp.where(col >= above_at[0, 1], own[1, rows, :], right[rows, :])
+        return 0
+
+    lax.fori_loop(0, DET // STRIP, strip, 0)
+
+
+def side_call(left_at, above_at, own, lower, right):
+    vmem = pl.BlockSpec(memory_space=pltpu.VMEM)
+    return pl.pallas_call(
+        side_kernel,
+        out_shape=[jax.ShapeDtypeStruct((DET, DET), F32)] * 2,
+        in_specs=[pl.BlockSpec(memory_space=pltpu.SMEM)] * 2 + [vmem] * 3,
+        out_specs=[vmem] * 2,
+        compiler_params=pltpu.CompilerParams(vmem_limit_bytes=8 * 2**20),
+        name="sides",
+    )(left_at, above_at, own, lower, right)
+
+
+def merge_cells(corners, row, col, own, left, right):
+    here_at, left_at, right_at, above_at, below_at = corners
+    inside = row < here_at[0, 0]
+    inside_left = row < left_at[0, 0]
+    inside_right = row < right_at[0, 0]
+    near = col >= here_at[0, 1]
+    left = jnp.where(col < left_at[0, 1], left, 0.0)
+    right = jnp.where(col >= right_at[0, 1], right, 0.0)
+    own_near = jnp.where(near, own, 0.0)
+    own_far = jnp.where(near, 0.0, own)
+
+    def gathered(wanted, start):
+        near_sum = jnp.where(inside == wanted, own_near, 0.0) + jnp.where(inside_left == wanted, left, 0.0)
+        far_sum = jnp.where(inside == wanted, own_far, 0.0) + jnp.where(inside_right == wanted, right, 0.0)
+        return jnp.where(col >= start, near_sum, far_sum)
+
+    merged = own + jnp.where(
+        near,
+        jnp.where(inside == inside_left, left, 0.0),
+        jnp.where(inside == inside_right, right, 0.0),
+    )
+    return merged, gathered(True, below_at[0, 1]), gathered(False, above_at[0, 1])
+
+
+def settle_cells(corners, row, col, own, left):
+    here_at, left_at = corners
+    own = jnp.where(col >= here_at[0, 1], own, 0.0)
+    left = jnp.where(col < left_at[0, 1], left, 0.0)
+    own_here, left_here = row >= here_at[0, 0], row >= left_at[0, 0]
+    down = jnp.where(own_here, 0.0, own) + jnp.where(left_here, 0.0, left)
+    stays = jnp.where(own_here, own, 0.0) + jnp.where(left_here, left, 0.0)
+    return down, stays
 
 
 def shifted(value, axis, steps):
@@ -388,12 +504,14 @@
     return lax.ppermute(value, axis, [(source, source ^ distance) for source in range(count)])
 
 
-def reduced(keep, send):
+def tile_sum(keep, send):
     count = lax.axis_size("tile")
     summed = keep + swapped(send, "frame", 1)
     parts = summed.reshape(count, MODES * DET // count, DET)
-    parts = lax.all_to_all(parts, "tile", 0, 0)
-    part = jnp.sum(parts, axis=0)
+    return jnp.sum(lax.all_to_all(parts, "tile", 0, 0), axis=0)
+
+
+def chip_sum(part):
     distance = 2
     while distance < lax.axis_size("frame"):
         part = part + swapped(part, "frame", distance)
@@ -410,90 +528,75 @@
 
 def per_device(object_field, probe_modes, measured, offsets, ramp_steps):
     tile_at, frame_at = lax.axis_index("tile"), lax.axis_index("frame")
-    tile_last = lax.axis_size("tile") - 1
-    frame_last = lax.axis_size("frame") - 1
-    core = frame_at % 2
+    core = frame_at & 1
+    place = jnp.stack(
+        [
+            core,
+            (tile_at == lax.axis_size("tile") - 1).astype(jnp.int32),
+            (frame_at == lax.axis_size("frame") - 1).astype(jnp.int32),
+        ]
+    )
     rate = probe_step / (lax.axis_size("tile") * lax.axis_size("frame"))
-    plain, turned, derived, slope = (jnp.asarray(table) for table in shift_tables())
-    steps = ramp_steps[0]
-    pick = lambda table, step: lax.dynamic_index_in_dim(table, step, 0, keepdims=False)
-    plain0, turned0 = pick(plain, steps[0]), pick(turned, steps[0])
-    plain1, turned1 = pick(plain, steps[1]), pick(turned, steps[1])
-    derived0 = pick(derived, steps[0])
-
-    here = offsets[0]
-    above = shifted(offsets, "tile", 1)[0]
-    below = shifted(offsets, "tile", -1)[0]
-    left = shifted(offsets, "frame", 1)[0]
-    right = shifted(offsets, "frame", -1)[0]
-    scalars = jnp.stack(
-        [
-            here[0],
-            here[1],
-            core,
-            (tile_at == tile_last).astype(jnp.int32),
-            (frame_at == frame_last).astype(jnp.int32),
-        ]
-    )
-    row = lax.broadcasted_iota(jnp.int32, (2, DET, DET), 1)
-    col = lax.broadcasted_iota(jnp.int32, (2, DET, DET), 2)
-
-    right_tile = shifted(object_field, "frame", -1)
-    lower = shifted(jnp.where(col >= above[1], object_field, right_tile), "tile", -1)
-
-    frame = measured[0]
+    together = lax.optimization_barrier
+
+    lower = shifted(object_field[0], "tile", -1)
+    right = shifted(object_field[1], "frame", -1)
+    at_left = shifted(offsets, "frame", 1)
+    at_above = shifted(offsets, "tile", 1)
+    lower, right, at_left, at_above = together((lower, right, at_left, at_above))
+    to_left, to_above = side_call(at_left, at_above, object_field, lower, right)
+    side = shifted(to_left, "frame", -1)
+    below = shifted(to_above, "tile", -1)
+
+    scalars = (offsets, ramp_steps, place)
+    kept = (probe_modes, measured, jnp.asarray(shift_tables()))
     grad1, patch, keep1, send1 = gradient_call(
-        False,
-        rate,
-        scalars,
-        (object_field, right_tile, lower, probe_modes, frame, plain0, turned0, plain1, turned1),
+        False, rate, scalars, (object_field, lower, side, below, right), kept
     )
 
     grad_left = shifted(grad1, "frame", 1)
     grad_right = shifted(grad1, "frame", -1)
-    left_cells = col < left[1]
-    right_cells = col >= right[1]
-    side_left = jnp.where(left_cells, grad_left, 0.0)
-    side_right = jnp.where(right_cells, grad_right, 0.0)
-
-    def rows_of(wanted, edge, value):
-        return jnp.where((row < edge) == wanted, value, 0.0)
-
-    def gathered(wanted, start):
-        kept = rows_of(wanted, here[0], grad1)
-        near = jnp.where(col >= here[1], kept, 0.0) + rows_of(wanted, left[0], side_left)
-        far = jnp.where(col < here[1], kept, 0.0) + rows_of(wanted, right[0], side_right)
-        return jnp.where(col >= start, near, far)
-
-    inside = row < here[0]
-    merged = grad1 + jnp.where(
-        col >= here[1],
-        jnp.where(inside == (row < left[0]), side_left, 0.0),
-        jnp.where(inside == (row < right[0]), side_right, 0.0),
-    )
-    from_above = shifted(gathered(True, below[1]), "tile", 1)
-    from_below = shifted(gathered(False, above[1]), "tile", -1)
-
-    mine, other = spread(reduced(keep1, send1))
+    keep1, send1, corner = together((keep1, send1, offsets))
+    at_right = shifted(corner, "frame", -1)
+    at_below = shifted(corner, "tile", -1)
+    part = tile_sum(keep1, send1)
+    part, grad_left, grad_right, at_right, at_below = together((part, grad_left, grad_right, at_right, at_below))
+    merged, down, up = plane_call(
+        "merge", merge_cells, (offsets, at_left, at_right, at_above, at_below), (grad1, grad_left, grad_right), 3
+    )
+    part, down, up = together((part, down, up))
+    from_above = shifted(down, "tile", 1)
+    from_below = shifted(up, "tile", -1)
+    part, from_above, from_below = together((chip_sum(part), from_above, from_below))
+    mine, other = spread(part)
 
     grad_total, modes_now, keep2, send2, shift_grad = gradient_call(
         True,
         rate,
         scalars,
-        (patch, merged, from_above, from_below, grad1, mine, other)
-        + (probe_modes, frame, plain0, turned0, plain1, turned1, derived0, slope),
-    )
-
-    moved = shifted(jnp.where(row < here[0], grad_total, 0.0), "tile", 1)
-    own_rows = jnp.where(row >= here[0], grad_total, 0.0)
-    to_right = jnp.where(col < here[1], own_rows, 0.0) + jnp.where(col < above[1], moved, 0.0)
-    stays = jnp.where(col >= here[1], own_rows, 0.0) + jnp.where(col >= above[1], moved, 0.0)
-    object_final = object_field - object_step * (stays + shifted(to_right, "frame", 1))
-
-    mine, other = spread(reduced(keep2, send2))
-    first = jnp.where(core == 0, mine, other)
-    second = jnp.where(core == 0, other, mine)
-    probe_final = modes_now - rate * jnp.stack([first, second])
+        (patch, merged, from_above, from_below, grad1, mine, other),
+        kept,
+    )
+
+    count = lax.axis_size("tile")
+    planes = modes_now.reshape(2, count, MODES * DET // count, DET)
+    own_part = lax.dynamic_slice(planes, (core, tile_at, 0, 0), (1, 1) + planes.shape[2:])[0, 0]
+
+    moved = shifted(grad_total, "frame", 1)
+    part = tile_sum(keep2, send2)
+    part, moved = together((part, moved))
+    down, stays = plane_call(
+        "settle", settle_cells, (offsets, at_left), (grad_total, moved), 2
+    )
+    part, down = together((part, down))
+    arrived = shifted(down, "tile", 1)
+    part = own_part - rate * chip_sum(part)
+    part, arrived = together((part, arrived))
+    object_final = object_field - object_step * (stays + arrived)
+
+    mine, other = spread(part)
+    plane = lax.broadcasted_iota(jnp.int32, (2, MODES, DET, DET), 0)
+    probe_final = jnp.where(plane == core, mine[None], other[None])
     return (object_final, probe_final, shift_grad[:1, :2])
 
 

time: 214 us -> 196 us (0.916)
  waiting for transfers between devices: 29.8 us -> 43.4 us
  other arithmetic: 18.6 us -> 7.56 us
  local copies, waits for them, and re-layouts: 15.1 us -> 4.26 us
  blocking collectives: 45.4 us -> 35.3 us
  between operations: 5 us -> 0.98 us
  starting transfers between devices: 77.9 us -> 80.4 us
    all_to_all x2, waiting for transfers between devices: 0.39 us -> 12 us  [tile_sum(): return jnp.sum(lax.all_to_all(parts, 'tile', 0, 0), axis=0)]
    all_to_all x2, blocking collectives: 45.4 us -> 35.3 us  [spread(): mine = lax.all_to_all(parts, 'tile', 0, 0).reshape(MODES, DET, DET)]
    ppermute x10, waiting for transfers between devices: 11.2 us -> 20.5 us  [swapped(): lax.ppermute(value, axis, [(source, source ^ distance) for source in rang...]
    ppermute x12 -> x14, waiting for transfers between devices: 18.2 us -> 10.9 us  [shifted(): lax.ppermute(value, axis, [(source, source + steps) for source in range(i...]
    lt x6 -> x0, other arithmetic: 4.95 us -> none  [the longest x1 1.82 us: per_device(): left_cells = col < left[1]]
    slice x6 -> x0, local copies, waits for them, and re-layouts: 3.59 us -> none  [the longest x1 0.66 us: per_device(): from_above = shifted(gathered(True, below[1]), 'tile', 1)]
    all_to_all x2, starting transfers between devices: 10.4 us -> 13.4 us  [tile_sum(): return jnp.sum(lax.all_to_all(parts, 'tile', 0, 0), axis=0)]
    select_n x3 -> x1, other arithmetic: 3.93 us -> 1.38 us  [per_device(): probe_final = jnp.where(plane == core, mine[None], other[None])]
  transfers between devices with their start and end apart: 24 -> 26, of which waited for: 13 -> 16; matrix products, arithmetic and copies ran while one was open for 11% -> 2% of each run, Pallas kernels for 0% -> 0%
where the time goes in v2:
time: 196 us; the launch traced here: 195 us
  starting transfers between devices  80.4 us (41%)
  waiting for transfers between devices  43.4 us (22%)
  blocking collectives  35.3 us (18%)
  Pallas kernels  22.8 us (12%)
  other arithmetic  7.56 us (4%)
  local copies, waits for them, and re-layouts  4.26 us (2%)
    ppermute x14, starting transfers between devices, shifted(): lax.ppermute(value, axis, [(source, source + steps) for source in range(i...  38.1 us
    all_to_all x2, blocking collectives, spread(): mine = lax.all_to_all(parts, 'tile', 0, 0).reshape(MODES, DET, DET)  35.3 us
    ppermute x10, starting transfers between devices, swapped(): lax.ppermute(value, axis, [(source, source ^ distance) for source in rang...  28.9 us
    ppermute x10, waiting for transfers between devices, swapped(): lax.ppermute(value, axis, [(source, source ^ distance) for source in rang...  20.5 us
    pallas_call x2, Pallas kernels, gradient_call(): pl.pallas_call(body, out_shape=outs, in_specs=[smem] * len(scalars) + [vm...  20.2 us
    all_to_all x2, starting transfers between devices, tile_sum(): return jnp.sum(lax.all_to_all(parts, 'tile', 0, 0), axis=0)  13.4 us
    all_to_all x2, waiting for transfers between devices, tile_sum(): return jnp.sum(lax.all_to_all(parts, 'tile', 0, 0), axis=0)  12 us
    ppermute x14, waiting for transfers between devices, shifted(): lax.ppermute(value, axis, [(source, source + steps) for source in range(i...  10.9 us
  transfers between devices with their start and end apart: 26, of which 16 were waited for; matrix products, arithmetic and copies ran while one was open for 2% of the time, Pallas kernels for 0%

profile of v2, /device:TPU:1, one launch (start us, length us, event | category | flops | bytes accessed | tf_op | source)
XLA Modules:
  0.0 194.7 jit_solution(17391003995438836352)
XLA Ops:
  3.1 5.1 %collective-permute-start.1 = (f32[256,256]{1,0:T(8,128)S(1)}, f32[256,256]{1,0:T(8,128)S(1)}, u32[]{:S(2)}, u32[]{:S(2)}) collective-permute-start(f32[256,256]{1,0:T(8,128)S(1)} %get-tuple-element.83), channel_id=1, source_target_pairs={{1,0},{2,1},{3,2},{4,3},{5,4},{6,5},{7,6},{8,7},{9,8},{10,9},{11,1... | collective-permute-start | bytes 786440 | tf_op jit(solution)/shard_map/ppermute | solution.py:499
  10.2 4.3 %collective-permute-start.3 = (s32[1,2]{1,0:T(1,128)}, s32[1,2]{1,0:T(1,128)S(1)}, u32[]{:S(2)}, u32[]{:S(2)}) collective-permute-start(s32[1,2]{1,0:T(1,128)} %refs_0_.7), channel_id=1, source_target_pairs={{0,16},{16,32},{32,48},{48,64},{64,80},{80,96},{96,112},{112,128},... | collective-permute-start | bytes 32 | tf_op jit(solution)/shard_map/ppermute | solution.py:499
  17.0 3.3 %collective-permute-start.4 = (f32[256,256]{1,0:T(8,128)S(1)}, f32[256,256]{1,0:T(8,128)S(1)}, u32[]{:S(2)}, u32[]{:S(2)}) collective-permute-start(f32[256,256]{1,0:T(8,128)S(1)} %get-tuple-element.47), channel_id=1, source_target_pairs={{1,0},{2,1},{3,2},{4,3},{5,4},{6,5},{7,6},{8,7},{9,8},{10,9},{11,1... | collective-permute-start | bytes 786440 | tf_op jit(solution)/shard_map/ppermute | solution.py:499
  21.7 3.3 %collective-permute-done.4.refs_5_ = f32[256,256]{1,0:T(8,128)S(1)} collective-permute-done((f32[256,256]{1,0:T(8,128)S(1)}, f32[256,256]{1,0:T(8,128)S(1)}, u32[]{:S(2)}, u32[]{:S(2)}) %collective-permute-start.4) | collective-permute-done | bytes 262176 | tf_op jit(solution)/shard_map/ppermute | solution.py:499
  25.0 5.3 %collective-permute-done.5.refs_6_ = f32[256,256]{1,0:T(8,128)S(1)} collective-permute-done((f32[256,256]{1,0:T(8,128)S(1)}, f32[256,256]{1,0:T(8,128)S(1)}, u32[]{:S(2)}, u32[]{:S(2)}) %collective-permute-start.5) | collective-permute-done | bytes 262176 | tf_op jit(solution)/shard_map/ppermute | solution.py:499
  31.7 9.2 %gradient_first.1 = (f32[2,256,256]{2,1,0:T(8,128)S(1)}, f32[2,256,256]{2,1,0:T(8,128)S(1)}, f32[3,256,256]{2,1,0:T(8,128)S(1)}, f32[3,256,256]{2,1,0:T(8,128)S(1)}) custom-call(s32[1,2]{1,0:T(1,128)S(1)} %copy-done.5, s32[1,2]{1,0:T(1,128)S(1)} %copy-done.6, s32[3]{0:T(128)S(1)} %pad_add_fusion.refs_2_, f32[2,256,256]{2,1,0:T(8,128)S(1)} %copy-done.1, ...), custom_call_target="tpu_custom_call" | custom-call | tf_op jit(solution)/shard_map/gradient_first/pallas_call | solution.py:396
  44.3 9.1 %all-to-all-start = ((f32[16,48,256]{2,1,0:T(8,128)}), f32[16,48,256]{2,1,0:T(8,128)}, u32[]{:S(2)}, u32[]{:S(2)}) async-start(f32[16,48,256]{2,1,0:T(8,128)} %bitcast.5), calls=%async_computation | async-start | bytes 1572864 | tf_op jit(solution)/shard_map/all_to_all | solution.py:511
  53.4 4.8 %collective-permute-start.7 = (f32[2,256,256]{2,1,0:T(8,128)S(1)}, f32[2,256,256]{2,1,0:T(8,128)S(1)}, u32[]{:S(2)}, u32[]{:S(2)}) collective-permute-start(f32[2,256,256]{2,1,0:T(8,128)S(1)} %get-tuple-element.54.refs_5_.refs_7_), channel_id=1, source_target_pairs={{0,1},{1,2},{2,3},{3,4},{4,5},{5,6},{6,7},{7,8},{8,9},{9,10},{10,1... | collective-permute-start | bytes 1572872 | tf_op jit(solution)/shard_map/ppermute | solution.py:499
  63.4 2.8 %all-to-all-done = f32[16,48,256]{2,1,0:T(8,128)} async-done(((f32[16,48,256]{2,1,0:T(8,128)}), f32[16,48,256]{2,1,0:T(8,128)}, u32[]{:S(2)}, u32[]{:S(2)}) %all-to-all-start) | async-done | bytes 786464 | tf_op jit(solution)/shard_map/all_to_all | solution.py:511
  70.0 3.7 %collective-permute-start.14 = (f32[2,256,256]{2,1,0:T(8,128)S(1)}, f32[2,256,256]{2,1,0:T(8,128)S(1)}, u32[]{:S(2)}, u32[]{:S(2)}) collective-permute-start(f32[2,256,256]{2,1,0:T(8,128)S(1)} %get-tuple-element.65), channel_id=1, source_target_pairs={{0,16},{16,32},{32,48},{48,64},{64,80},{80,96},{96,112},{112,128},... | collective-permute-start | bytes 1572872 | tf_op jit(solution)/shard_map/ppermute | solution.py:499
  78.1 5.8 %collective-permute-start.12 = (f32[48,256]{1,0:T(8,128)S(1)}, f32[48,256]{1,0:T(8,128)S(1)}, u32[]{:S(2)}, u32[]{:S(2)}) collective-permute-start(f32[48,256]{1,0:T(8,128)S(1)} %add.34), channel_id=1, source_target_pairs={{0,4},{1,5},{2,6},{3,7},{4,0},{5,1},{6,2},{7,3},{8,12},{9,13},{10,... | collective-permute-start | bytes 147464 | tf_op jit(solution)/shard_map/ppermute | solution.py:504
  85.5 2.5 %collective-permute-start.13 = (f32[48,256]{1,0:T(8,128)S(1)}, f32[48,256]{1,0:T(8,128)S(1)}, u32[]{:S(2)}, u32[]{:S(2)}) collective-permute-start(f32[48,256]{1,0:T(8,128)S(1)} %add.35), channel_id=1, source_target_pairs={{0,8},{1,9},{2,10},{3,11},{4,12},{5,13},{6,14},{7,15},{8,0},{9,1},... | collective-permute-start | bytes 147464 | tf_op jit(solution)/shard_map/ppermute | solution.py:504
  88.0 4.4 %collective-permute-done.13 = f32[48,256]{1,0:T(8,128)S(1)} collective-permute-done((f32[48,256]{1,0:T(8,128)S(1)}, f32[48,256]{1,0:T(8,128)S(1)}, u32[]{:S(2)}, u32[]{:S(2)}) %collective-permute-start.13) | collective-permute-done | bytes 49184 | tf_op jit(solution)/shard_map/ppermute | solution.py:504
  92.6 19.4 %all_to_all.20 = f32[16,48,256]{2,1,0:T(8,128)S(1)} all-to-all(f32[16,48,256]{2,1,0:T(8,128)S(1)} %broadcast_in_dim.31), channel_id=1, replica_groups=mesh['tile'=16,'frame'=16] {'tile'}, dimensions={0} | all-to-all | bytes 1572864 | tf_op jit(solution)/shard_map/all_to_all | solution.py:525
  112.0 3.3 %collective-permute-start.16 = (f32[3,256,256]{2,1,0:T(8,128)S(1)}, f32[3,256,256]{2,1,0:T(8,128)S(1)}, u32[]{:S(2)}, u32[]{:S(2)}) collective-permute-start(f32[3,256,256]{2,1,0:T(8,128)S(1)} %bitcast.14), channel_id=1, source_target_pairs={{0,1},{1,0},{2,3},{3,2},{4,5},{5,4},{6,7},{7,6},{8,9},{9,8},{10,11... | collective-permute-start | bytes 2359304 | tf_op jit(solution)/shard_map/ppermute | solution.py:504
  117.2 11.0 %gradient_last.1 = (f32[2,256,256]{2,1,0:T(8,128)S(1)}, f32[2,3,256,256]{3,2,1,0:T(8,128)S(1)}, f32[3,256,256]{2,1,0:T(8,128)S(1)}, f32[3,256,256]{2,1,0:T(8,128)S(1)}, f32[8,128]{1,0:T(8,128)S(1)}) custom-call(s32[1,2]{1,0:T(1,128)S(1)} %copy-done.5, s32[1,2]{1,0:T(1,128)S(1)} %copy-done.6, s32[3]{0:T(128)S(1)} %pad_add_fusion.refs_2_, ...), custom_call_target="tpu_custom_call" | custom-call | tf_op jit(solution)/shard_map/gradient_last/pallas_call | solution.py:396
  131.6 4.3 %all-to-all-start.2 = ((f32[16,48,256]{2,1,0:T(8,128)}), f32[16,48,256]{2,1,0:T(8,128)}, u32[]{:S(2)}, u32[]{:S(2)}) async-start(f32[16,48,256]{2,1,0:T(8,128)} %bitcast.7), calls=%async_computation.2 | async-start | bytes 1572864 | tf_op jit(solution)/shard_map/all_to_all | solution.py:511
  135.9 3.6 %collective-permute-start.18 = (f32[2,256,256]{2,1,0:T(8,128)S(1)}, f32[2,256,256]{2,1,0:T(8,128)S(1)}, u32[]{:S(2)}, u32[]{:S(2)}) collective-permute-start(f32[2,256,256]{2,1,0:T(8,128)S(1)} %get-tuple-element.70.refs_2_), channel_id=1, source_target_pairs={{0,1},{1,2},{2,3},{3,4},{4,5},{5,6},{6,7},{7,8},{8,9},{9,10},{10,1... | collective-permute-start | bytes 1572872 | tf_op jit(solution)/shard_map/ppermute | solution.py:499
  139.5 9.2 %all-to-all-done.2 = f32[16,48,256]{2,1,0:T(8,128)} async-done(((f32[16,48,256]{2,1,0:T(8,128)}), f32[16,48,256]{2,1,0:T(8,128)}, u32[]{:S(2)}, u32[]{:S(2)}) %all-to-all-start.2) | async-done | bytes 786464 | tf_op jit(solution)/shard_map/all_to_all | solution.py:511
  156.1 3.4 %collective-permute-start.20 = (f32[48,256]{1,0:T(8,128)S(1)}, f32[48,256]{1,0:T(8,128)S(1)}, u32[]{:S(2)}, u32[]{:S(2)}) collective-permute-start(f32[48,256]{1,0:T(8,128)S(1)} %add.40), channel_id=1, source_target_pairs={{0,4},{1,5},{2,6},{3,7},{4,0},{5,1},{6,2},{7,3},{8,12},{9,13},{10,... | collective-permute-start | bytes 147464 | tf_op jit(solution)/shard_map/ppermute | solution.py:504
  161.0 3.7 %collective-permute-start.21 = (f32[48,256]{1,0:T(8,128)S(1)}, f32[48,256]{1,0:T(8,128)S(1)}, u32[]{:S(2)}, u32[]{:S(2)}) collective-permute-start(f32[48,256]{1,0:T(8,128)S(1)} %add.41), channel_id=1, source_target_pairs={{0,8},{1,9},{2,10},{3,11},{4,12},{5,13},{6,14},{7,15},{8,0},{9,1},... | collective-permute-start | bytes 147464 | tf_op jit(solution)/shard_map/ppermute | solution.py:504
  164.7 3.8 %collective-permute-done.21 = f32[48,256]{1,0:T(8,128)S(1)} collective-permute-done((f32[48,256]{1,0:T(8,128)S(1)}, f32[48,256]{1,0:T(8,128)S(1)}, u32[]{:S(2)}, u32[]{:S(2)}) %collective-permute-start.21) | collective-permute-done | bytes 49184 | tf_op jit(solution)/shard_map/ppermute | solution.py:504
  169.3 15.9 %all_to_all.21 = f32[16,48,256]{2,1,0:T(8,128)S(1)} all-to-all(f32[16,48,256]{2,1,0:T(8,128)S(1)} %broadcast_in_dim.32), channel_id=1, replica_groups=mesh['tile'=16,'frame'=16] {'tile'}, dimensions={0} | all-to-all | bytes 1572864 | tf_op jit(solution)/shard_map/all_to_all | solution.py:525
  185.3 6.2 %collective-permute-start.23 = (f32[3,256,256]{2,1,0:T(8,128)S(1)}, f32[3,256,256]{2,1,0:T(8,128)S(1)}, u32[]{:S(2)}, u32[]{:S(2)}) collective-permute-start(f32[3,256,256]{2,1,0:T(8,128)S(1)} %bitcast.17), channel_id=1, source_target_pairs={{0,1},{1,0},{2,3},{3,2},{4,5},{5,4},{6,7},{7,6},{8,9},{9,8},{10,11... | collective-permute-start | bytes 2359304 | tf_op jit(solution)/shard_map/ppermute | solution.py:504
  (69 shorter events, 46.4 us)
Async XLA Ops:
  1.8 13.5 %collective-permute-start = (f32[256,256]{1,0:T(8,128)S(1)}, f32[256,256]{1,0:T(8,128)S(1)}, u32[]{:S(2)}, u32[]{:S(2)}) collective-permute-start(f32[256,256]{1,0:T(8,128)S(1)} %get-tuple-element.84), channel_id=1, source_target_pairs={{16,0},{32,16},{48,32},{64,48},{80,64},{96,80},{112,96},{128,112},... | collective-permute-start | bytes 786440 | tf_op jit(solution)/shard_map/ppermute | solution.py:499
  3.1 12.2 %collective-permute-start.1 = (f32[256,256]{1,0:T(8,128)S(1)}, f32[256,256]{1,0:T(8,128)S(1)}, u32[]{:S(2)}, u32[]{:S(2)}) collective-permute-start(f32[256,256]{1,0:T(8,128)S(1)} %get-tuple-element.83), channel_id=1, source_target_pairs={{1,0},{2,1},{3,2},{4,3},{5,4},{6,5},{7,6},{8,7},{9,8},{10,9},{11,1... | collective-permute-start | bytes 786440 | tf_op jit(solution)/shard_map/ppermute | solution.py:499
  8.3 6.2 %collective-permute-start.2 = (s32[1,2]{1,0:T(1,128)}, s32[1,2]{1,0:T(1,128)S(1)}, u32[]{:S(2)}, u32[]{:S(2)}) collective-permute-start(s32[1,2]{1,0:T(1,128)} %refs_0_.7), channel_id=1, source_target_pairs={{0,1},{1,2},{2,3},{3,4},{4,5},{5,6},{6,7},{7,8},{8,9},{9,10},{10,1... | collective-permute-start | bytes 32 | tf_op jit(solution)/shard_map/ppermute | solution.py:499
  10.2 5.1 %collective-permute-start.3 = (s32[1,2]{1,0:T(1,128)}, s32[1,2]{1,0:T(1,128)S(1)}, u32[]{:S(2)}, u32[]{:S(2)}) collective-permute-start(s32[1,2]{1,0:T(1,128)} %refs_0_.7), channel_id=1, source_target_pairs={{0,16},{16,32},{32,48},{48,64},{64,80},{80,96},{96,112},{112,128},... | collective-permute-start | bytes 32 | tf_op jit(solution)/shard_map/ppermute | solution.py:499
  17.0 8.0 %collective-permute-start.4 = (f32[256,256]{1,0:T(8,128)S(1)}, f32[256,256]{1,0:T(8,128)S(1)}, u32[]{:S(2)}, u32[]{:S(2)}) collective-permute-start(f32[256,256]{1,0:T(8,128)S(1)} %get-tuple-element.47), channel_id=1, source_target_pairs={{1,0},{2,1},{3,2},{4,3},{5,4},{6,5},{7,6},{8,7},{9,8},{10,9},{11,1... | collective-permute-start | bytes 786440 | tf_op jit(solution)/shard_map/ppermute | solution.py:499
  20.3 10.0 %collective-permute-start.5 = (f32[256,256]{1,0:T(8,128)S(1)}, f32[256,256]{1,0:T(8,128)S(1)}, u32[]{:S(2)}, u32[]{:S(2)}) collective-permute-start(f32[256,256]{1,0:T(8,128)S(1)} %get-tuple-element.48), channel_id=1, source_target_pairs={{16,0},{32,16},{48,32},{64,48},{80,64},{96,80},{112,96},{128,112},... | collective-permute-start | bytes 786440 | tf_op jit(solution)/shard_map/ppermute | solution.py:499
  44.3 21.9 %all-to-all-start = ((f32[16,48,256]{2,1,0:T(8,128)}), f32[16,48,256]{2,1,0:T(8,128)}, u32[]{:S(2)}, u32[]{:S(2)}) async-start(f32[16,48,256]{2,1,0:T(8,128)} %bitcast.5), calls=%async_computation | async-start | bytes 1572864 | tf_op jit(solution)/shard_map/all_to_all | solution.py:511
  53.4 15.4 %collective-permute-start.7 = (f32[2,256,256]{2,1,0:T(8,128)S(1)}, f32[2,256,256]{2,1,0:T(8,128)S(1)}, u32[]{:S(2)}, u32[]{:S(2)}) collective-permute-start(f32[2,256,256]{2,1,0:T(8,128)S(1)} %get-tuple-element.54.refs_5_.refs_7_), channel_id=1, source_target_pairs={{0,1},{1,2},{2,3},{3,4},{4,5},{5,6},{6,7},{7,8},{8,9},{9,10},{10,1... | collective-permute-start | bytes 1572872 | tf_op jit(solution)/shard_map/ppermute | solution.py:499
  58.2 10.6 %collective-permute-start.8 = (f32[2,256,256]{2,1,0:T(8,128)S(1)}, f32[2,256,256]{2,1,0:T(8,128)S(1)}, u32[]{:S(2)}, u32[]{:S(2)}) collective-permute-start(f32[2,256,256]{2,1,0:T(8,128)S(1)} %get-tuple-element.54.refs_5_.refs_7_), channel_id=1, source_target_pairs={{1,0},{2,1},{3,2},{4,3},{5,4},{6,5},{7,6},{8,7},{9,8},{10,9},{11,1... | collective-permute-start | bytes 1572872 | tf_op jit(solution)/shard_map/ppermute | solution.py:499
  60.2 7.2 %collective-permute-start.10 = (s32[1,2]{1,0:T(1,128)S(1)}, s32[1,2]{1,0:T(1,128)S(1)}, u32[]{:S(2)}, u32[]{:S(2)}) collective-permute-start(s32[1,2]{1,0:T(1,128)S(1)} %copy-done.5), channel_id=1, source_target_pairs={{16,0},{32,16},{48,32},{64,48},{80,64},{96,80},{112,96},{128,112},... | collective-permute-start | bytes 32 | tf_op jit(solution)/shard_map/ppermute | solution.py:499
  61.5 7.3 %collective-permute-start.9 = (s32[1,2]{1,0:T(1,128)S(1)}, s32[1,2]{1,0:T(1,128)S(1)}, u32[]{:S(2)}, u32[]{:S(2)}) collective-permute-start(s32[1,2]{1,0:T(1,128)S(1)} %copy-done.5), channel_id=1, source_target_pairs={{1,0},{2,1},{3,2},{4,3},{5,4},{6,5},{7,6},{8,7},{9,8},{10,9},{11,1... | collective-permute-start | bytes 32 | tf_op jit(solution)/shard_map/ppermute | solution.py:499
  70.0 22.5 %collective-permute-start.14 = (f32[2,256,256]{2,1,0:T(8,128)S(1)}, f32[2,256,256]{2,1,0:T(8,128)S(1)}, u32[]{:S(2)}, u32[]{:S(2)}) collective-permute-start(f32[2,256,256]{2,1,0:T(8,128)S(1)} %get-tuple-element.65), channel_id=1, source_target_pairs={{0,16},{16,32},{32,48},{48,64},{64,80},{80,96},{96,112},{112,128},... | collective-permute-start | bytes 1572872 | tf_op jit(solution)/shard_map/ppermute | solution.py:499
  73.7 18.8 %collective-permute-start.15 = (f32[2,256,256]{2,1,0:T(8,128)S(1)}, f32[2,256,256]{2,1,0:T(8,128)S(1)}, u32[]{:S(2)}, u32[]{:S(2)}) collective-permute-start(f32[2,256,256]{2,1,0:T(8,128)S(1)} %get-tuple-element.66), channel_id=1, source_target_pairs={{16,0},{32,16},{48,32},{64,48},{80,64},{96,80},{112,96},{128,112},... | collective-permute-start | bytes 1572872 | tf_op jit(solution)/shard_map/ppermute | solution.py:499
  75.0 3.2 %collective-permute-start.11 = (f32[48,256]{1,0:T(8,128)S(1)}, f32[48,256]{1,0:T(8,128)S(1)}, u32[]{:S(2)}, u32[]{:S(2)}) collective-permute-start(f32[48,256]{1,0:T(8,128)S(1)} %reduce_sum.18), channel_id=1, source_target_pairs={{0,2},{1,3},{2,0},{3,1},{4,6},{5,7},{6,4},{7,5},{8,10},{9,11},{10,... | collective-permute-start | bytes 147464 | tf_op jit(solution)/shard_map/ppermute | solution.py:504
  78.1 7.4 %collective-permute-start.12 = (f32[48,256]{1,0:T(8,128)S(1)}, f32[48,256]{1,0:T(8,128)S(1)}, u32[]{:S(2)}, u32[]{:S(2)}) collective-permute-start(f32[48,256]{1,0:T(8,128)S(1)} %add.34), channel_id=1, source_target_pairs={{0,4},{1,5},{2,6},{3,7},{4,0},{5,1},{6,2},{7,3},{8,12},{9,13},{10,... | collective-permute-start | bytes 147464 | tf_op jit(solution)/shard_map/ppermute | solution.py:504
  85.5 6.9 %collective-permute-start.13 = (f32[48,256]{1,0:T(8,128)S(1)}, f32[48,256]{1,0:T(8,128)S(1)}, u32[]{:S(2)}, u32[]{:S(2)}) collective-permute-start(f32[48,256]{1,0:T(8,128)S(1)} %add.35), channel_id=1, source_target_pairs={{0,8},{1,9},{2,10},{3,11},{4,12},{5,13},{6,14},{7,15},{8,0},{9,1},... | collective-permute-start | bytes 147464 | tf_op jit(solution)/shard_map/ppermute | solution.py:504
  112.0 5.3 %collective-permute-start.16 = (f32[3,256,256]{2,1,0:T(8,128)S(1)}, f32[3,256,256]{2,1,0:T(8,128)S(1)}, u32[]{:S(2)}, u32[]{:S(2)}) collective-permute-start(f32[3,256,256]{2,1,0:T(8,128)S(1)} %bitcast.14), channel_id=1, source_target_pairs={{0,1},{1,0},{2,3},{3,2},{4,5},{5,4},{6,7},{7,6},{8,9},{9,8},{10,11... | collective-permute-start | bytes 2359304 | tf_op jit(solution)/shard_map/ppermute | solution.py:504
  131.6 17.1 %all-to-all-start.2 = ((f32[16,48,256]{2,1,0:T(8,128)}), f32[16,48,256]{2,1,0:T(8,128)}, u32[]{:S(2)}, u32[]{:S(2)}) async-start(f32[16,48,256]{2,1,0:T(8,128)} %bitcast.7), calls=%async_computation.2 | async-start | bytes 1572864 | tf_op jit(solution)/shard_map/all_to_all | solution.py:511
  135.9 14.0 %collective-permute-start.18 = (f32[2,256,256]{2,1,0:T(8,128)S(1)}, f32[2,256,256]{2,1,0:T(8,128)S(1)}, u32[]{:S(2)}, u32[]{:S(2)}) collective-permute-start(f32[2,256,256]{2,1,0:T(8,128)S(1)} %get-tuple-element.70.refs_2_), channel_id=1, source_target_pairs={{0,1},{1,2},{2,3},{3,4},{4,5},{5,6},{6,7},{7,8},{8,9},{9,10},{10,1... | collective-permute-start | bytes 1572872 | tf_op jit(solution)/shard_map/ppermute | solution.py:499
  150.7 18.5 %collective-permute-start.22 = (f32[2,256,256]{2,1,0:T(8,128)S(1)}, f32[2,256,256]{2,1,0:T(8,128)S(1)}, u32[]{:S(2)}, u32[]{:S(2)}) collective-permute-start(f32[2,256,256]{2,1,0:T(8,128)S(1)} %get-tuple-element.79), channel_id=1, source_target_pairs={{0,16},{16,32},{32,48},{48,64},{64,80},{80,96},{96,112},{112,128},... | collective-permute-start | bytes 1572872 | tf_op jit(solution)/shard_map/ppermute | solution.py:499
  153.1 3.0 %collective-permute-start.19 = (f32[48,256]{1,0:T(8,128)S(1)}, f32[48,256]{1,0:T(8,128)S(1)}, u32[]{:S(2)}, u32[]{:S(2)}) collective-permute-start(f32[48,256]{1,0:T(8,128)S(1)} %reduce_sum.19), channel_id=1, source_target_pairs={{0,2},{1,3},{2,0},{3,1},{4,6},{5,7},{6,4},{7,5},{8,10},{9,11},{10,... | collective-permute-start | bytes 147464 | tf_op jit(solution)/shard_map/ppermute | solution.py:504
  156.1 4.9 %collective-permute-start.20 = (f32[48,256]{1,0:T(8,128)S(1)}, f32[48,256]{1,0:T(8,128)S(1)}, u32[]{:S(2)}, u32[]{:S(2)}) collective-permute-start(f32[48,256]{1,0:T(8,128)S(1)} %add.40), channel_id=1, source_target_pairs={{0,4},{1,5},{2,6},{3,7},{4,0},{5,1},{6,2},{7,3},{8,12},{9,13},{10,... | collective-permute-start | bytes 147464 | tf_op jit(solution)/shard_map/ppermute | solution.py:504
  161.0 7.4 %collective-permute-start.21 = (f32[48,256]{1,0:T(8,128)S(1)}, f32[48,256]{1,0:T(8,128)S(1)}, u32[]{:S(2)}, u32[]{:S(2)}) collective-permute-start(f32[48,256]{1,0:T(8,128)S(1)} %add.41), channel_id=1, source_target_pairs={{0,8},{1,9},{2,10},{3,11},{4,12},{5,13},{6,14},{7,15},{8,0},{9,1},... | collective-permute-start | bytes 147464 | tf_op jit(solution)/shard_map/ppermute | solution.py:504
  185.3 8.1 %collective-permute-start.23 = (f32[3,256,256]{2,1,0:T(8,128)S(1)}, f32[3,256,256]{2,1,0:T(8,128)S(1)}, u32[]{:S(2)}, u32[]{:S(2)}) collective-permute-start(f32[3,256,256]{2,1,0:T(8,128)S(1)} %bitcast.17), channel_id=1, source_target_pairs={{0,1},{1,0},{2,3},{3,2},{4,5},{5,4},{6,7},{7,6},{8,9},{9,8},{10,11... | collective-permute-start | bytes 2359304 | tf_op jit(solution)/shard_map/ppermute | solution.py:504
  (10 other events, 176.4 us)

commit v3 on v2

--- a/solution.py
+++ b/solution.py
@@ -13,10 +13,13 @@
 MODES = 3
 RAMPS = 8
 STRIP = 16
+FIRST = 384
 
 object_step = 0.05
 probe_step = 0.5
 fresnel = 0.25
+
+WEIGHT = 2 * 10**10
 
 F32 = jnp.float32
 BF16 = jnp.bfloat16
@@ -78,8 +81,8 @@
         patch_in, merged, from_above, from_below, grad_before = take(5)
         total_mine, total_other = take(2)
     else:
-        own, first_low, first_side, second_low, second_side = take(5)
-    probe_kept, measured_kept, tables = take(3)
+        own_first, own_second, lower, right, side, below = take(6)
+    probe, measured, tables = take(3)
     if last:
         grad_out, probe_out, keep_out, send_out, shift_out = take(5)
     else:
@@ -87,7 +90,7 @@
     doubled, field, high, low, result, z_high, z_low, z_result = take(8)
     if last:
         slope_result, derived_result = take(2)
-    probe, measured, plain0, turned0, plain1, turned1 = take(6)
+    plain0, turned0, plain1, turned1 = take(4)
     if last:
         derived0, slope1 = take(2)
     (arrived,) = take(1)
@@ -95,10 +98,8 @@
     row0, col0, core = corner[0, 0], corner[0, 1], place[0]
     step0, step1 = ramp[0, 0], ramp[0, 1]
     moves = [
-        (probe_kept, probe),
         (tables.at[RAMPS + step1], turned1),
         (tables.at[step0], plain0),
-        (measured_kept.at[0], measured),
         (tables.at[RAMPS + step0], turned0),
         (tables.at[step1], plain1),
     ]
@@ -111,8 +112,8 @@
     for copy in copies:
         copy.start()
 
-    def build(step, _):
-        start = pl.multiple_of(step * STRIP, STRIP)
+    def build(step):
+        start = step * STRIP
         rows = pl.ds(start, STRIP)
         again = pl.ds(start + DET, STRIP)
         row_at = lax.broadcasted_iota(jnp.int32, (STRIP, DET), 0) + start
@@ -125,13 +126,15 @@
                 cells = patch_in[part, rows, :] - object_step * (merged[part, rows, :] + moved)
                 cells = jnp.where(outside, 0.0, cells)
             else:
-                mine = own[part, rows, :]
-                if part == 0:
-                    column = jnp.where(row_at >= row0, mine, first_low[rows, :])
-                    cells = jnp.where(col_at >= col0, column, first_side[rows, :])
+                flat = part * DET + step * STRIP
+                if flat < FIRST:
+                    at = pl.ds(flat, STRIP)
+                    column = jnp.where(row_at >= row0, own_first[at, :], lower[at, :])
+                    cells = jnp.where(col_at >= col0, column, side[at, :])
                 else:
-                    line = jnp.where(col_at >= col0, mine, second_side[rows, :])
-                    cells = jnp.where(row_at >= row0, line, second_low[rows, :])
+                    at = pl.ds(flat - FIRST, STRIP)
+                    line = jnp.where(col_at >= col0, own_second[at, :], right[at, :])
+                    cells = jnp.where(row_at >= row0, line, below[at, :])
                 patch_out[part, rows, :] = cells
             doubled[part, rows, :] = cells
             doubled[part, again, :] = cells
@@ -141,13 +144,9 @@
                 other = total_other[mode, rows, :]
                 probe_out[0, mode, rows, :] = probe[0, mode, rows, :] - rate * jnp.where(core == 0, mine, other)
                 probe_out[1, mode, rows, :] = probe[1, mode, rows, :] - rate * jnp.where(core == 0, other, mine)
-        return 0
-
-    if last:
-        copies[0].wait()
-    lax.fori_loop(0, DET // STRIP, build, 0)
-    if not last:
-        copies[0].wait()
+
+    for step in range(DET // STRIP):
+        build(step)
     modes = probe_out if last else probe
     back = lax.rem(DET - col0, DET)
 
@@ -180,9 +179,10 @@
                 high[block, at, :], low[block, at, :] = split(both)
         return 0
 
-    lax.fori_loop(0, DET // STRIP, enter, 0)
-    for copy in copies[1:]:
-        copy.wait()
+    lax.fori_loop(0, DET // STRIP, enter, 0, unroll=16)
+    copies[0].wait()
+    if last:
+        copies[5].wait()
 
     def times_right(block, mode, table, where):
         at = pl.ds(mode * DET, DET)
@@ -224,7 +224,10 @@
                     z_high[block, at, cols], z_low[block, at, cols] = split(both)
         return 0
 
-    lax.fori_loop(0, HALF // STRIP, rows_to_blocks, 0)
+    lax.fori_loop(0, HALF // STRIP, rows_to_blocks, 0, unroll=8)
+    copies[1].wait()
+    if last:
+        copies[4].wait()
 
     for block in range(2):
         for mode in range(MODES):
@@ -257,8 +260,8 @@
                 held.append((mode, part, top, bottom))
                 top_sum = top * top if top_sum is None else top_sum + top * top
                 bottom_sum = bottom * bottom if bottom_sum is None else bottom_sum + bottom * bottom
-        top_gap = 2.0 * (top_sum - measured[low_rows, :])
-        bottom_gap = 2.0 * (bottom_sum - measured[high_rows, :])
+        top_gap = 2.0 * (top_sum - measured[0, low_rows, :])
+        bottom_gap = 2.0 * (bottom_sum - measured[0, high_rows, :])
 
         def fold(value):
             return jnp.concatenate(
@@ -277,7 +280,8 @@
         return running
 
     zeros = jnp.zeros((STRIP, DET), F32) if last else 0
-    slope_rows = lax.fori_loop(0, HALF // STRIP, misfits, zeros)
+    slope_rows = lax.fori_loop(0, HALF // STRIP, misfits, zeros, unroll=8)
+    copies[2].wait()
 
     for block in range(2):
         for mode in range(MODES):
@@ -301,7 +305,8 @@
                     high[block, at, :], low[block, at, :] = split(both)
         return 0
 
-    lax.fori_loop(0, HALF // STRIP, blocks_to_rows, 0)
+    lax.fori_loop(0, HALF // STRIP, blocks_to_rows, 0, unroll=8)
+    copies[3].wait()
 
     for block in range(2):
         for mode in range(MODES):
@@ -336,7 +341,7 @@
             doubled[part, again, :] = turned
         return running
 
-    slope_cols = lax.fori_loop(0, DET // STRIP, leave, zeros)
+    slope_cols = lax.fori_loop(0, DET // STRIP, leave, zeros, unroll=16)
 
     def wrap(step, _):
         start = pl.multiple_of(step * STRIP, STRIP)
@@ -348,7 +353,7 @@
             grad_out[part, rows, :] = value
         return 0
 
-    lax.fori_loop(0, DET // STRIP, wrap, 0)
+    lax.fori_loop(0, DET // STRIP, wrap, 0, unroll=16)
 
     if last:
         lane = lax.broadcasted_iota(jnp.int32, (8, HALF), 1)
@@ -385,10 +390,9 @@
             pltpu.VMEM((2, MODES * DET, DET), F32),
             pltpu.VMEM((2, DET, MODES * DET), F32),
         ]
-    scratch += [pltpu.VMEM((2, MODES, DET, DET), F32), pltpu.VMEM((DET, DET), F32)]
     tables = 6 if last else 4
     scratch += [pltpu.VMEM((2, 2, DET, DET), BF16)] * tables
-    scratch += [pltpu.SemaphoreType.DMA((tables + 2,))]
+    scratch += [pltpu.SemaphoreType.DMA((tables,))]
 
     def body(*refs):
         gradient_kernel(last, rate, *refs)
@@ -398,15 +402,15 @@
         out_shape=outs,
         in_specs=[smem] * len(scalars)
         + [vmem] * len(operands)
-        + [pl.BlockSpec(memory_space=pltpu.HBM)] * len(kept),
+        + [vmem, vmem, pl.BlockSpec(memory_space=pltpu.HBM)],
         out_specs=(vmem,) * len(outs),
         scratch_shapes=scratch,
-        compiler_params=pltpu.CompilerParams(vmem_limit_bytes=(44 if last else 46) * 2**20),
+        compiler_params=pltpu.CompilerParams(vmem_limit_bytes=(42 if last else 44) * 2**20),
         name="gradient_last" if last else "gradient_first",
     )(*scalars, *operands, *kept)
 
 
-def plane_call(name, body, scalars, operands, outputs):
+def plane_call(name, body, scalars, operands, outputs, weight=0):
     def kernel(*refs):
         at_scalars, refs = refs[: len(scalars)], refs[len(scalars) :]
 
@@ -421,7 +425,7 @@
                     ref[at] = value
             return 0
 
-        lax.fori_loop(0, DET // STRIP, strip, 0)
+        lax.fori_loop(0, DET // STRIP, strip, 0, unroll=16)
 
     vmem = pl.BlockSpec(memory_space=pltpu.VMEM)
     return pl.pallas_call(
@@ -431,32 +435,33 @@
         out_specs=[vmem] * outputs,
         compiler_params=pltpu.CompilerParams(vmem_limit_bytes=8 * 2**20),
         name=name,
+        cost_estimate=pl.CostEstimate(flops=weight, bytes_accessed=weight // 400, transcendentals=0) if weight else None,
     )(*scalars, *operands)
 
 
-def side_kernel(left_at, above_at, own, lower, right, to_left, to_above):
-    def strip(step, _):
-        start = pl.multiple_of(step * STRIP, STRIP)
-        rows = pl.ds(start, STRIP)
-        row = lax.broadcasted_iota(jnp.int32, (STRIP, DET), 0) + start
-        col = lax.broadcasted_iota(jnp.int32, (STRIP, DET), 1)
-        to_left[rows, :] = jnp.where(row >= left_at[0, 0], own[0, rows, :], lower[rows, :])
-        to_above[rows, :] = jnp.where(col >= above_at[0, 1], own[1, rows, :], right[rows, :])
-        return 0
-
-    lax.fori_loop(0, DET // STRIP, strip, 0)
-
-
-def side_call(left_at, above_at, own, lower, right):
+def side_kernel(left_at, above_at, first, second, lower, right, to_left, to_above):
+    for step in range(2 * DET // STRIP):
+        flat = step * STRIP
+        if flat < FIRST:
+            at = pl.ds(flat, STRIP)
+            row = lax.broadcasted_iota(jnp.int32, (STRIP, DET), 0) + flat % DET
+            to_left[at, :] = jnp.where(row >= left_at[0, 0], first[at, :], lower[at, :])
+        else:
+            at = pl.ds(flat - FIRST, STRIP)
+            col = lax.broadcasted_iota(jnp.int32, (STRIP, DET), 1)
+            to_above[at, :] = jnp.where(col >= above_at[0, 1], second[at, :], right[at, :])
+
+
+def side_call(left_at, above_at, *operands):
     vmem = pl.BlockSpec(memory_space=pltpu.VMEM)
     return pl.pallas_call(
         side_kernel,
-        out_shape=[jax.ShapeDtypeStruct((DET, DET), F32)] * 2,
-        in_specs=[pl.BlockSpec(memory_space=pltpu.SMEM)] * 2 + [vmem] * 3,
+        out_shape=[jax.ShapeDtypeStruct((rows, DET), F32) for rows in (FIRST, 2 * DET - FIRST)],
+        in_specs=[pl.BlockSpec(memory_space=pltpu.SMEM)] * 2 + [vmem] * 4,
         out_specs=[vmem] * 2,
         compiler_params=pltpu.CompilerParams(vmem_limit_bytes=8 * 2**20),
         name="sides",
-    )(left_at, above_at, own, lower, right)
+    )(left_at, above_at, *operands)
 
 
 def merge_cells(corners, row, col, own, left, right):
@@ -504,11 +509,10 @@
     return lax.ppermute(value, axis, [(source, source ^ distance) for source in range(count)])
 
 
-def tile_sum(keep, send):
+def tile_parts(keep, send):
     count = lax.axis_size("tile")
     summed = keep + swapped(send, "frame", 1)
-    parts = summed.reshape(count, MODES * DET // count, DET)
-    return jnp.sum(lax.all_to_all(parts, "tile", 0, 0), axis=0)
+    return lax.all_to_all(summed.reshape(count, MODES * DET // count, DET), "tile", 0, 0)
 
 
 def chip_sum(part):
@@ -539,35 +543,43 @@
     rate = probe_step / (lax.axis_size("tile") * lax.axis_size("frame"))
     together = lax.optimization_barrier
 
-    lower = shifted(object_field[0], "tile", -1)
-    right = shifted(object_field[1], "frame", -1)
+    flat = object_field.reshape(2 * DET, DET)
+    first, second = flat[:FIRST], flat[FIRST:]
+    lower = shifted(first, "tile", -1)
+    right = shifted(second, "frame", -1)
     at_left = shifted(offsets, "frame", 1)
     at_above = shifted(offsets, "tile", 1)
     lower, right, at_left, at_above = together((lower, right, at_left, at_above))
-    to_left, to_above = side_call(at_left, at_above, object_field, lower, right)
+    to_left, to_above = side_call(at_left, at_above, first, second, lower, right)
+    to_left, to_above, corner = together((to_left, to_above, offsets))
     side = shifted(to_left, "frame", -1)
     below = shifted(to_above, "tile", -1)
+    at_right = shifted(corner, "frame", -1)
+    at_below = shifted(corner, "tile", -1)
+    side, below, at_right, at_below = together((side, below, at_right, at_below))
 
     scalars = (offsets, ramp_steps, place)
     kept = (probe_modes, measured, jnp.asarray(shift_tables()))
     grad1, patch, keep1, send1 = gradient_call(
-        False, rate, scalars, (object_field, lower, side, below, right), kept
+        False, rate, scalars, (first, second, lower, right, side, below), kept
     )
 
     grad_left = shifted(grad1, "frame", 1)
     grad_right = shifted(grad1, "frame", -1)
-    keep1, send1, corner = together((keep1, send1, offsets))
-    at_right = shifted(corner, "frame", -1)
-    at_below = shifted(corner, "tile", -1)
-    part = tile_sum(keep1, send1)
-    part, grad_left, grad_right, at_right, at_below = together((part, grad_left, grad_right, at_right, at_below))
+    parts = tile_parts(keep1, send1)
     merged, down, up = plane_call(
-        "merge", merge_cells, (offsets, at_left, at_right, at_above, at_below), (grad1, grad_left, grad_right), 3
-    )
-    part, down, up = together((part, down, up))
+        "merge",
+        merge_cells,
+        (offsets, at_left, at_right, at_above, at_below),
+        (grad1, grad_left, grad_right),
+        3,
+        WEIGHT,
+    )
+    parts, _, _, _ = together((parts, merged, down, up))
     from_above = shifted(down, "tile", 1)
     from_below = shifted(up, "tile", -1)
-    part, from_above, from_below = together((chip_sum(part), from_above, from_below))
+    part = chip_sum(jnp.sum(parts, axis=0))
+    part, from_above, from_below = together((part, from_above, from_below))
     mine, other = spread(part)
 
     grad_total, modes_now, keep2, send2, shift_grad = gradient_call(
@@ -583,12 +595,12 @@
     own_part = lax.dynamic_slice(planes, (core, tile_at, 0, 0), (1, 1) + planes.shape[2:])[0, 0]
 
     moved = shifted(grad_total, "frame", 1)
-    part = tile_sum(keep2, send2)
-    part, moved = together((part, moved))
+    parts = tile_parts(keep2, send2)
     down, stays = plane_call(
-        "settle", settle_cells, (offsets, at_left), (grad_total, moved), 2
-    )
-    part, down = together((part, down))
+        "settle", settle_cells, (offsets, at_left), (grad_total, moved), 2, WEIGHT
+    )
+    parts, _, _ = together((parts, down, stays))
+    part = jnp.sum(parts, axis=0)
     arrived = shifted(down, "tile", 1)
     part = own_part - rate * chip_sum(part)
     part, arrived = together((part, arrived))

time: 196 us -> 182 us (0.929)
  blocking collectives: 35.3 us -> 27.8 us
  waiting for transfers between devices: 43.4 us -> 36.7 us
  local copies, waits for them, and re-layouts: 4.26 us -> 7.44 us
    all_to_all x2, blocking collectives: 35.3 us -> 27.8 us  [spread(): mine = lax.all_to_all(parts, 'tile', 0, 0).reshape(MODES, DET, DET)]
    ppermute x14, waiting for transfers between devices: 10.9 us -> 6.21 us  [shifted(): lax.ppermute(value, axis, [(source, source + steps) for source in range(i...]
    pallas_call x2, Pallas kernels: 20.2 us -> 16.3 us  [gradient_call(): pl.pallas_call(body, out_shape=outs, in_specs=[smem] * len(scalars) + [vm...]
    unnamed x16 -> x36, local copies, waits for them, and re-layouts: 2.48 us -> 4.72 us
    slice x0 -> x2, local copies, waits for them, and re-layouts: none -> 2.07 us  [per_device(): first, second = (flat[:FIRST], flat[FIRST:])]
  transfers between devices with their start and end apart: 26 -> 26, of which waited for: 16 -> 13; matrix products, arithmetic and copies ran while one was open for 2% -> 4% of each run, Pallas kernels for 0% -> 2%
where the time goes in v3:
time: 182 us; the launch traced here: 181 us
  starting transfers between devices  78.8 us (43%)
  waiting for transfers between devices  36.7 us (20%)
  blocking collectives  27.8 us (15%)
  Pallas kernels  21.4 us (12%)
  other arithmetic  7.49 us (4%)
  local copies, waits for them, and re-layouts  7.44 us (4%)
    ppermute x14, starting transfers between devices, shifted(): lax.ppermute(value, axis, [(source, source + steps) for source in range(i...  39 us
    all_to_all x2, blocking collectives, spread(): mine = lax.all_to_all(parts, 'tile', 0, 0).reshape(MODES, DET, DET)  27.8 us
    ppermute x10, starting transfers between devices, swapped(): lax.ppermute(value, axis, [(source, source ^ distance) for source in rang...  27.1 us
    ppermute x10, waiting for transfers between devices, swapped(): lax.ppermute(value, axis, [(source, source ^ distance) for source in rang...  19.5 us
    pallas_call x2, Pallas kernels, gradient_call(): pl.pallas_call(body, out_shape=outs, in_specs=[smem] * len(scalars) + [vm...  16.3 us
    all_to_all x2, starting transfers between devices, tile_parts(): lax.all_to_all(summed.reshape(count, MODES * DET // count, DET), 'tile',...  12.7 us
    all_to_all x2, waiting for transfers between devices, tile_parts(): lax.all_to_all(summed.reshape(count, MODES * DET // count, DET), 'tile',...  11.1 us
    ppermute x14, waiting for transfers between devices, shifted(): lax.ppermute(value, axis, [(source, source + steps) for source in range(i...  6.21 us
  transfers between devices with their start and end apart: 26, of which 13 were waited for; matrix products, arithmetic and copies ran while one was open for 4% of the time, Pallas kernels for 2%

profile of v3, /device:TPU:1, one launch (start us, length us, event | category | flops | bytes accessed | tf_op | source)
XLA Modules:
  0.0 180.6 jit_solution(14056536822842966421)
XLA Ops:
  4.1 5.1 %collective-permute-start.1 = (f32[128,256]{1,0:T(8,128)S(1)}, f32[128,256]{1,0:T(8,128)S(1)}, u32[]{:S(2)}, u32[]{:S(2)}) collective-permute-start(f32[128,256]{1,0:T(8,128)S(1)} %slice.13.second.refs_4_), channel_id=1, source_target_pairs={{1,0},{2,1},{3,2},{4,3},{5,4},{6,5},{7,6},{8,7},{9,8},{10,9},{11,1... | collective-permute-start | bytes 393224 | tf_op jit(solution)/shard_map/ppermute | solution.py:504
  11.1 4.3 %collective-permute-start.3 = (s32[1,2]{1,0:T(1,128)}, s32[1,2]{1,0:T(1,128)S(1)}, u32[]{:S(2)}, u32[]{:S(2)}) collective-permute-start(s32[1,2]{1,0:T(1,128)} %refs_0_.7), channel_id=1, source_target_pairs={{0,16},{16,32},{32,48},{48,64},{64,80},{80,96},{96,112},{112,128},... | collective-permute-start | bytes 32 | tf_op jit(solution)/shard_map/ppermute | solution.py:504
  17.6 3.2 %collective-permute-start.4 = (f32[384,256]{1,0:T(8,128)}, f32[384,256]{1,0:T(8,128)S(1)}, u32[]{:S(2)}, u32[]{:S(2)}) collective-permute-start(f32[384,256]{1,0:T(8,128)} %get-tuple-element.43), channel_id=1, source_target_pairs={{1,0},{2,1},{3,2},{4,3},{5,4},{6,5},{7,6},{8,7},{9,8},{10,9},{11,1... | collective-permute-start | bytes 1179656 | tf_op jit(solution)/shard_map/ppermute | solution.py:504
  31.9 6.2 %gradient_first.1 = (f32[2,256,256]{2,1,0:T(8,128)S(1)}, f32[2,256,256]{2,1,0:T(8,128)S(1)}, f32[3,256,256]{2,1,0:T(8,128)S(1)}, f32[3,256,256]{2,1,0:T(8,128)S(1)}) custom-call(s32[1,2]{1,0:T(1,128)S(1)} %copy-done.7, s32[1,2]{1,0:T(1,128)S(1)} %copy-done.6, s32[3]{0:T(128)S(1)} %pad_add_fusion.refs_2_, f32[384,256]{1,0:T(8,128)S(1)} %slice.12.first.refs_3_, ...), custom_call_target="tpu_custom_call" | custom-call | tf_op jit(solution)/shard_map/gradient_first/pallas_call | solution.py:400
  38.3 4.5 %collective-permute-start.8 = (f32[2,256,256]{2,1,0:T(8,128)S(1)}, f32[2,256,256]{2,1,0:T(8,128)S(1)}, u32[]{:S(2)}, u32[]{:S(2)}) collective-permute-start(f32[2,256,256]{2,1,0:T(8,128)S(1)} %get-tuple-element.51.refs_5_.refs_7_), channel_id=1, source_target_pairs={{0,1},{1,2},{2,3},{3,4},{4,5},{5,6},{6,7},{7,8},{8,9},{9,10},{10,1... | collective-permute-start | bytes 1572872 | tf_op jit(solution)/shard_map/ppermute | solution.py:504
  45.8 9.1 %all-to-all-start = ((f32[16,48,256]{2,1,0:T(8,128)}), f32[16,48,256]{2,1,0:T(8,128)}, u32[]{:S(2)}, u32[]{:S(2)}) async-start(f32[16,48,256]{2,1,0:T(8,128)} %bitcast.14), calls=%async_computation | async-start | bytes 1572864 | tf_op jit(solution)/shard_map/all_to_all | solution.py:515
  56.8 2.5 %merge.1 = (f32[2,256,256]{2,1,0:T(8,128)S(1)}, f32[2,256,256]{2,1,0:T(8,128)}, f32[2,256,256]{2,1,0:T(8,128)}) custom-call(s32[1,2]{1,0:T(1,128)S(1)} %copy-done.7, s32[1,2]{1,0:T(1,128)S(1)} %collective-permute-done.2.left_at.refs_1_, s32[1,2]{1,0:T(1,128)S(1)} %copy-done.14, s32[1,2]{1,0:T(1,128)S(1)} %copy-done.10, s32[1,2]{1,0:T(1,128)S(1)} %copy-done.16, ...), custom_call_target="tpu_custom_call" | custom-call | flops 20000000000 | bytes 50000000 | tf_op jit(solution)/shard_map/merge/pallas_call | solution.py:431
  59.2 4.0 %collective-permute-start.14 = (f32[2,256,256]{2,1,0:T(8,128)}, f32[2,256,256]{2,1,0:T(8,128)}, u32[]{:S(2)}, u32[]{:S(2)}) collective-permute-start(f32[2,256,256]{2,1,0:T(8,128)} %get-tuple-element.55), channel_id=1, source_target_pairs={{0,16},{16,32},{32,48},{48,64},{64,80},{80,96},{96,112},{112,128},... | collective-permute-start | bytes 1572872 | tf_op jit(solution)/shard_map/ppermute | solution.py:504
  64.6 3.1 %all-to-all-done = f32[16,48,256]{2,1,0:T(8,128)} async-done(((f32[16,48,256]{2,1,0:T(8,128)}), f32[16,48,256]{2,1,0:T(8,128)}, u32[]{:S(2)}, u32[]{:S(2)}) %all-to-all-start) | async-done | bytes 786464 | tf_op jit(solution)/shard_map/all_to_all | solution.py:515
  72.4 7.3 %collective-permute-start.12 = (f32[48,256]{1,0:T(8,128)S(1)}, f32[48,256]{1,0:T(8,128)S(1)}, u32[]{:S(2)}, u32[]{:S(2)}) collective-permute-start(f32[48,256]{1,0:T(8,128)S(1)} %add.34), channel_id=1, source_target_pairs={{0,4},{1,5},{2,6},{3,7},{4,0},{5,1},{6,2},{7,3},{8,12},{9,13},{10,... | collective-permute-start | bytes 147464 | tf_op jit(solution)/shard_map/ppermute | solution.py:509
  82.3 5.8 %collective-permute-done.13 = f32[48,256]{1,0:T(8,128)S(1)} collective-permute-done((f32[48,256]{1,0:T(8,128)S(1)}, f32[48,256]{1,0:T(8,128)S(1)}, u32[]{:S(2)}, u32[]{:S(2)}) %collective-permute-start.13) | collective-permute-done | bytes 49184 | tf_op jit(solution)/shard_map/ppermute | solution.py:509
  88.2 14.2 %all_to_all.20 = f32[16,48,256]{2,1,0:T(8,128)S(1)} all-to-all(f32[16,48,256]{2,1,0:T(8,128)S(1)} %broadcast_in_dim.31), channel_id=1, replica_groups=mesh['tile'=16,'frame'=16] {'tile'}, dimensions={0} | all-to-all | bytes 1572864 | tf_op jit(solution)/shard_map/all_to_all | solution.py:529
  102.4 4.7 %collective-permute-start.16 = (f32[3,256,256]{2,1,0:T(8,128)S(1)}, f32[3,256,256]{2,1,0:T(8,128)S(1)}, u32[]{:S(2)}, u32[]{:S(2)}) collective-permute-start(f32[3,256,256]{2,1,0:T(8,128)S(1)} %bitcast.11), channel_id=1, source_target_pairs={{0,1},{1,0},{2,3},{3,2},{4,5},{5,4},{6,7},{7,6},{8,9},{9,8},{10,11... | collective-permute-start | bytes 2359304 | tf_op jit(solution)/shard_map/ppermute | solution.py:509
  109.0 10.1 %gradient_last.1 = (f32[2,256,256]{2,1,0:T(8,128)}, f32[2,3,256,256]{3,2,1,0:T(8,128)S(1)}, f32[3,256,256]{2,1,0:T(8,128)S(1)}, f32[3,256,256]{2,1,0:T(8,128)S(1)}, f32[8,128]{1,0:T(8,128)S(1)}) custom-call(s32[1,2]{1,0:T(1,128)S(1)} %copy-done.7, s32[1,2]{1,0:T(1,128)S(1)} %copy-done.6, s32[3]{0:T(128)S(1)} %pad_add_fusion.refs_2_, ...), custom_call_target="tpu_custom_call" | custom-call | tf_op jit(solution)/shard_map/gradient_last/pallas_call | solution.py:400
  119.6 4.0 %collective-permute-start.17 = (f32[2,256,256]{2,1,0:T(8,128)}, f32[2,256,256]{2,1,0:T(8,128)S(1)}, u32[]{:S(2)}, u32[]{:S(2)}) collective-permute-start(f32[2,256,256]{2,1,0:T(8,128)} %get-tuple-element.61.refs_2_), channel_id=1, source_target_pairs={{0,1},{1,2},{2,3},{3,4},{4,5},{5,6},{6,7},{7,8},{8,9},{9,10},{10,1... | collective-permute-start | bytes 1572872 | tf_op jit(solution)/shard_map/ppermute | solution.py:504
  124.7 3.6 %all-to-all-start.2 = ((f32[16,48,256]{2,1,0:T(8,128)}), f32[16,48,256]{2,1,0:T(8,128)S(1)}, u32[]{:S(2)}, u32[]{:S(2)}) async-start(f32[16,48,256]{2,1,0:T(8,128)} %bitcast.8), calls=%async_computation.2 | async-start | bytes 1572864 | tf_op jit(solution)/shard_map/all_to_all | solution.py:515
  131.3 2.8 %collective-permute-start.22 = (f32[2,256,256]{2,1,0:T(8,128)S(1)}, f32[2,256,256]{2,1,0:T(8,128)}, u32[]{:S(2)}, u32[]{:S(2)}) collective-permute-start(f32[2,256,256]{2,1,0:T(8,128)S(1)} %get-tuple-element.66), channel_id=1, source_target_pairs={{0,16},{16,32},{32,48},{48,64},{64,80},{80,96},{96,112},{112,128},... | collective-permute-start | bytes 1572872 | tf_op jit(solution)/shard_map/ppermute | solution.py:504
  134.1 8.0 %all-to-all-done.2 = f32[16,48,256]{2,1,0:T(8,128)S(1)} async-done(((f32[16,48,256]{2,1,0:T(8,128)}), f32[16,48,256]{2,1,0:T(8,128)S(1)}, u32[]{:S(2)}, u32[]{:S(2)}) %all-to-all-start.2) | async-done | bytes 786464 | tf_op jit(solution)/shard_map/all_to_all | solution.py:515
  142.2 2.2 %collective-permute-start.19 = (f32[48,256]{1,0:T(8,128)S(1)}, f32[48,256]{1,0:T(8,128)S(1)}, u32[]{:S(2)}, u32[]{:S(2)}) collective-permute-start(f32[48,256]{1,0:T(8,128)S(1)} %reduce_sum.19), channel_id=1, source_target_pairs={{0,2},{1,3},{2,0},{3,1},{4,6},{5,7},{6,4},{7,5},{8,10},{9,11},{10,... | collective-permute-start | bytes 147464 | tf_op jit(solution)/shard_map/ppermute | solution.py:509
  145.9 3.2 %collective-permute-start.20 = (f32[48,256]{1,0:T(8,128)S(1)}, f32[48,256]{1,0:T(8,128)S(1)}, u32[]{:S(2)}, u32[]{:S(2)}) collective-permute-start(f32[48,256]{1,0:T(8,128)S(1)} %add.40), channel_id=1, source_target_pairs={{0,4},{1,5},{2,6},{3,7},{4,0},{5,1},{6,2},{7,3},{8,12},{9,13},{10,... | collective-permute-start | bytes 147464 | tf_op jit(solution)/shard_map/ppermute | solution.py:509
  152.1 5.4 %collective-permute-done.21 = f32[48,256]{1,0:T(8,128)S(1)} collective-permute-done((f32[48,256]{1,0:T(8,128)S(1)}, f32[48,256]{1,0:T(8,128)S(1)}, u32[]{:S(2)}, u32[]{:S(2)}) %collective-permute-start.21) | collective-permute-done | bytes 49184 | tf_op jit(solution)/shard_map/ppermute | solution.py:509
  158.5 13.6 %all_to_all.21 = f32[16,48,256]{2,1,0:T(8,128)S(1)} all-to-all(f32[16,48,256]{2,1,0:T(8,128)S(1)} %broadcast_in_dim.32), channel_id=1, replica_groups=mesh['tile'=16,'frame'=16] {'tile'}, dimensions={0} | all-to-all | bytes 1572864 | tf_op jit(solution)/shard_map/all_to_all | solution.py:529
  172.0 4.7 %collective-permute-start.23 = (f32[3,256,256]{2,1,0:T(8,128)S(1)}, f32[3,256,256]{2,1,0:T(8,128)S(1)}, u32[]{:S(2)}, u32[]{:S(2)}) collective-permute-start(f32[3,256,256]{2,1,0:T(8,128)S(1)} %bitcast.15), channel_id=1, source_target_pairs={{0,1},{1,0},{2,3},{3,2},{4,5},{5,4},{6,7},{7,6},{8,9},{9,8},{10,11... | collective-permute-start | bytes 2359304 | tf_op jit(solution)/shard_map/ppermute | solution.py:509
  177.3 1.9 %multiply_subtract_fusion = f32[2,256,256]{2,1,0:T(8,128)} fusion(f32[2,256,256]{2,1,0:T(8,128)S(1)} %copy-done.17, f32[2,256,256]{2,1,0:T(8,128)S(1)} %get-tuple-element.62, f32[2,256,256]{2,1,0:T(8,128)} %collective-permute-done.22), kind=kLoop, calls=%fused_computation.1 | loop fusion | flops 393216 | bytes 2097152 | tf_op jit(solution)/shard_map/sub | solution.py:607
  (90 shorter events, 45.8 us)
Async XLA Ops:
  1.8 14.4 %collective-permute-start = (f32[384,256]{1,0:T(8,128)S(1)}, f32[384,256]{1,0:T(8,128)S(1)}, u32[]{:S(2)}, u32[]{:S(2)}) collective-permute-start(f32[384,256]{1,0:T(8,128)S(1)} %slice.12.first.refs_3_), channel_id=1, source_target_pairs={{16,0},{32,16},{48,32},{64,48},{80,64},{96,80},{112,96},{128,112},... | collective-permute-start | bytes 1179656 | tf_op jit(solution)/shard_map/ppermute | solution.py:504
  4.1 12.2 %collective-permute-start.1 = (f32[128,256]{1,0:T(8,128)S(1)}, f32[128,256]{1,0:T(8,128)S(1)}, u32[]{:S(2)}, u32[]{:S(2)}) collective-permute-start(f32[128,256]{1,0:T(8,128)S(1)} %slice.13.second.refs_4_), channel_id=1, source_target_pairs={{1,0},{2,1},{3,2},{4,3},{5,4},{6,5},{7,6},{8,7},{9,8},{10,9},{11,1... | collective-permute-start | bytes 393224 | tf_op jit(solution)/shard_map/ppermute | solution.py:504
  9.2 6.2 %collective-permute-start.2 = (s32[1,2]{1,0:T(1,128)}, s32[1,2]{1,0:T(1,128)S(1)}, u32[]{:S(2)}, u32[]{:S(2)}) collective-permute-start(s32[1,2]{1,0:T(1,128)} %refs_0_.7), channel_id=1, source_target_pairs={{0,1},{1,2},{2,3},{3,4},{4,5},{5,6},{6,7},{7,8},{8,9},{9,10},{10,1... | collective-permute-start | bytes 32 | tf_op jit(solution)/shard_map/ppermute | solution.py:504
  11.1 5.1 %collective-permute-start.3 = (s32[1,2]{1,0:T(1,128)}, s32[1,2]{1,0:T(1,128)S(1)}, u32[]{:S(2)}, u32[]{:S(2)}) collective-permute-start(s32[1,2]{1,0:T(1,128)} %refs_0_.7), channel_id=1, source_target_pairs={{0,16},{16,32},{32,48},{48,64},{64,80},{80,96},{96,112},{112,128},... | collective-permute-start | bytes 32 | tf_op jit(solution)/shard_map/ppermute | solution.py:504
  17.6 12.6 %collective-permute-start.4 = (f32[384,256]{1,0:T(8,128)}, f32[384,256]{1,0:T(8,128)S(1)}, u32[]{:S(2)}, u32[]{:S(2)}) collective-permute-start(f32[384,256]{1,0:T(8,128)} %get-tuple-element.43), channel_id=1, source_target_pairs={{1,0},{2,1},{3,2},{4,3},{5,4},{6,5},{7,6},{8,7},{9,8},{10,9},{11,1... | collective-permute-start | bytes 1179656 | tf_op jit(solution)/shard_map/ppermute | solution.py:504
  20.9 9.3 %collective-permute-start.5 = (f32[128,256]{1,0:T(8,128)S(1)}, f32[128,256]{1,0:T(8,128)S(1)}, u32[]{:S(2)}, u32[]{:S(2)}) collective-permute-start(f32[128,256]{1,0:T(8,128)S(1)} %get-tuple-element.44), channel_id=1, source_target_pairs={{16,0},{32,16},{48,32},{64,48},{80,64},{96,80},{112,96},{128,112},... | collective-permute-start | bytes 393224 | tf_op jit(solution)/shard_map/ppermute | solution.py:504
  22.3 5.1 %collective-permute-start.6 = (s32[1,2]{1,0:T(1,128)S(1)}, s32[1,2]{1,0:T(1,128)S(1)}, u32[]{:S(2)}, u32[]{:S(2)}) collective-permute-start(s32[1,2]{1,0:T(1,128)S(1)} %copy-done.7), channel_id=1, source_target_pairs={{1,0},{2,1},{3,2},{4,3},{5,4},{6,5},{7,6},{8,7},{9,8},{10,9},{11,1... | collective-permute-start | bytes 32 | tf_op jit(solution)/shard_map/ppermute | solution.py:504
  24.2 5.4 %collective-permute-start.7 = (s32[1,2]{1,0:T(1,128)S(1)}, s32[1,2]{1,0:T(1,128)S(1)}, u32[]{:S(2)}, u32[]{:S(2)}) collective-permute-start(s32[1,2]{1,0:T(1,128)S(1)} %copy-done.7), channel_id=1, source_target_pairs={{16,0},{32,16},{48,32},{64,48},{80,64},{96,80},{112,96},{128,112},... | collective-permute-start | bytes 32 | tf_op jit(solution)/shard_map/ppermute | solution.py:504
  38.2 6.5 %collective-permute-start.10 = (f32[3,256,256]{2,1,0:T(8,128)S(1)}, f32[3,256,256]{2,1,0:T(8,128)S(1)}, u32[]{:S(2)}, u32[]{:S(2)}) collective-permute-start(f32[3,256,256]{2,1,0:T(8,128)S(1)} %get-tuple-element.54), channel_id=1, source_target_pairs={{0,1},{1,0},{2,3},{3,2},{4,5},{5,4},{6,7},{7,6},{8,9},{9,8},{10,11... | collective-permute-start | bytes 2359304 | tf_op jit(solution)/shard_map/ppermute | solution.py:509
  38.3 16.6 %collective-permute-start.8 = (f32[2,256,256]{2,1,0:T(8,128)S(1)}, f32[2,256,256]{2,1,0:T(8,128)S(1)}, u32[]{:S(2)}, u32[]{:S(2)}) collective-permute-start(f32[2,256,256]{2,1,0:T(8,128)S(1)} %get-tuple-element.51.refs_5_.refs_7_), channel_id=1, source_target_pairs={{0,1},{1,2},{2,3},{3,4},{4,5},{5,6},{6,7},{7,8},{8,9},{9,10},{10,1... | collective-permute-start | bytes 1572872 | tf_op jit(solution)/shard_map/ppermute | solution.py:504
  42.8 12.9 %collective-permute-start.9 = (f32[2,256,256]{2,1,0:T(8,128)S(1)}, f32[2,256,256]{2,1,0:T(8,128)}, u32[]{:S(2)}, u32[]{:S(2)}) collective-permute-start(f32[2,256,256]{2,1,0:T(8,128)S(1)} %get-tuple-element.51.refs_5_.refs_7_), channel_id=1, source_target_pairs={{1,0},{2,1},{3,2},{4,3},{5,4},{6,5},{7,6},{8,7},{9,8},{10,9},{11,1... | collective-permute-start | bytes 1572872 | tf_op jit(solution)/shard_map/ppermute | solution.py:504
  45.8 21.8 %all-to-all-start = ((f32[16,48,256]{2,1,0:T(8,128)}), f32[16,48,256]{2,1,0:T(8,128)}, u32[]{:S(2)}, u32[]{:S(2)}) async-start(f32[16,48,256]{2,1,0:T(8,128)} %bitcast.14), calls=%async_computation | async-start | bytes 1572864 | tf_op jit(solution)/shard_map/all_to_all | solution.py:515
  59.2 28.9 %collective-permute-start.14 = (f32[2,256,256]{2,1,0:T(8,128)}, f32[2,256,256]{2,1,0:T(8,128)}, u32[]{:S(2)}, u32[]{:S(2)}) collective-permute-start(f32[2,256,256]{2,1,0:T(8,128)} %get-tuple-element.55), channel_id=1, source_target_pairs={{0,16},{16,32},{32,48},{48,64},{64,80},{80,96},{96,112},{112,128},... | collective-permute-start | bytes 1572872 | tf_op jit(solution)/shard_map/ppermute | solution.py:504
  63.3 24.9 %collective-permute-start.15 = (f32[2,256,256]{2,1,0:T(8,128)}, f32[2,256,256]{2,1,0:T(8,128)}, u32[]{:S(2)}, u32[]{:S(2)}) collective-permute-start(f32[2,256,256]{2,1,0:T(8,128)} %get-tuple-element.56), channel_id=1, source_target_pairs={{16,0},{32,16},{48,32},{64,48},{80,64},{96,80},{112,96},{128,112},... | collective-permute-start | bytes 1572872 | tf_op jit(solution)/shard_map/ppermute | solution.py:504
  72.4 8.7 %collective-permute-start.12 = (f32[48,256]{1,0:T(8,128)S(1)}, f32[48,256]{1,0:T(8,128)S(1)}, u32[]{:S(2)}, u32[]{:S(2)}) collective-permute-start(f32[48,256]{1,0:T(8,128)S(1)} %add.34), channel_id=1, source_target_pairs={{0,4},{1,5},{2,6},{3,7},{4,0},{5,1},{6,2},{7,3},{8,12},{9,13},{10,... | collective-permute-start | bytes 147464 | tf_op jit(solution)/shard_map/ppermute | solution.py:509
  81.2 6.9 %collective-permute-start.13 = (f32[48,256]{1,0:T(8,128)S(1)}, f32[48,256]{1,0:T(8,128)S(1)}, u32[]{:S(2)}, u32[]{:S(2)}) collective-permute-start(f32[48,256]{1,0:T(8,128)S(1)} %add.35), channel_id=1, source_target_pairs={{0,8},{1,9},{2,10},{3,11},{4,12},{5,13},{6,14},{7,15},{8,0},{9,1},... | collective-permute-start | bytes 147464 | tf_op jit(solution)/shard_map/ppermute | solution.py:509
  102.4 6.6 %collective-permute-start.16 = (f32[3,256,256]{2,1,0:T(8,128)S(1)}, f32[3,256,256]{2,1,0:T(8,128)S(1)}, u32[]{:S(2)}, u32[]{:S(2)}) collective-permute-start(f32[3,256,256]{2,1,0:T(8,128)S(1)} %bitcast.11), channel_id=1, source_target_pairs={{0,1},{1,0},{2,3},{3,2},{4,5},{5,4},{6,7},{7,6},{8,9},{9,8},{10,11... | collective-permute-start | bytes 2359304 | tf_op jit(solution)/shard_map/ppermute | solution.py:509
  119.2 4.5 %collective-permute-start.18 = (f32[3,256,256]{2,1,0:T(8,128)S(1)}, f32[3,256,256]{2,1,0:T(8,128)S(1)}, u32[]{:S(2)}, u32[]{:S(2)}) collective-permute-start(f32[3,256,256]{2,1,0:T(8,128)S(1)} %get-tuple-element.65), channel_id=1, source_target_pairs={{0,1},{1,0},{2,3},{3,2},{4,5},{5,4},{6,7},{7,6},{8,9},{9,8},{10,11... | collective-permute-start | bytes 2359304 | tf_op jit(solution)/shard_map/ppermute | solution.py:509
  119.6 10.5 %collective-permute-start.17 = (f32[2,256,256]{2,1,0:T(8,128)}, f32[2,256,256]{2,1,0:T(8,128)S(1)}, u32[]{:S(2)}, u32[]{:S(2)}) collective-permute-start(f32[2,256,256]{2,1,0:T(8,128)} %get-tuple-element.61.refs_2_), channel_id=1, source_target_pairs={{0,1},{1,2},{2,3},{3,4},{4,5},{5,6},{6,7},{7,8},{8,9},{9,10},{10,1... | collective-permute-start | bytes 1572872 | tf_op jit(solution)/shard_map/ppermute | solution.py:504
  124.7 17.4 %all-to-all-start.2 = ((f32[16,48,256]{2,1,0:T(8,128)}), f32[16,48,256]{2,1,0:T(8,128)S(1)}, u32[]{:S(2)}, u32[]{:S(2)}) async-start(f32[16,48,256]{2,1,0:T(8,128)} %bitcast.8), calls=%async_computation.2 | async-start | bytes 1572864 | tf_op jit(solution)/shard_map/all_to_all | solution.py:515
  131.3 27.1 %collective-permute-start.22 = (f32[2,256,256]{2,1,0:T(8,128)S(1)}, f32[2,256,256]{2,1,0:T(8,128)}, u32[]{:S(2)}, u32[]{:S(2)}) collective-permute-start(f32[2,256,256]{2,1,0:T(8,128)S(1)} %get-tuple-element.66), channel_id=1, source_target_pairs={{0,16},{16,32},{32,48},{48,64},{64,80},{80,96},{96,112},{112,128},... | collective-permute-start | bytes 1572872 | tf_op jit(solution)/shard_map/ppermute | solution.py:504
  145.9 4.7 %collective-permute-start.20 = (f32[48,256]{1,0:T(8,128)S(1)}, f32[48,256]{1,0:T(8,128)S(1)}, u32[]{:S(2)}, u32[]{:S(2)}) collective-permute-start(f32[48,256]{1,0:T(8,128)S(1)} %add.40), channel_id=1, source_target_pairs={{0,4},{1,5},{2,6},{3,7},{4,0},{5,1},{6,2},{7,3},{8,12},{9,13},{10,... | collective-permute-start | bytes 147464 | tf_op jit(solution)/shard_map/ppermute | solution.py:509
  150.6 6.9 %collective-permute-start.21 = (f32[48,256]{1,0:T(8,128)S(1)}, f32[48,256]{1,0:T(8,128)S(1)}, u32[]{:S(2)}, u32[]{:S(2)}) collective-permute-start(f32[48,256]{1,0:T(8,128)S(1)} %add.41), channel_id=1, source_target_pairs={{0,8},{1,9},{2,10},{3,11},{4,12},{5,13},{6,14},{7,15},{8,0},{9,1},... | collective-permute-start | bytes 147464 | tf_op jit(solution)/shard_map/ppermute | solution.py:509
  172.0 7.2 %collective-permute-start.23 = (f32[3,256,256]{2,1,0:T(8,128)S(1)}, f32[3,256,256]{2,1,0:T(8,128)S(1)}, u32[]{:S(2)}, u32[]{:S(2)}) collective-permute-start(f32[3,256,256]{2,1,0:T(8,128)S(1)} %bitcast.15), channel_id=1, source_target_pairs={{0,1},{1,0},{2,3},{3,2},{4,5},{5,4},{6,7},{7,6},{8,9},{9,8},{10,11... | collective-permute-start | bytes 2359304 | tf_op jit(solution)/shard_map/ppermute | solution.py:509
  (20 other events, 247.1 us)

commit v4 on v3

--- a/solution.py
+++ b/solution.py
@@ -14,52 +14,75 @@
 RAMPS = 8
 STRIP = 16
 FIRST = 384
+EXTRA = 8
 
 object_step = 0.05
 probe_step = 0.5
 fresnel = 0.25
 
 WEIGHT = 2 * 10**10
+VMEM_LIMIT = 18 * 2**20
 
 F32 = jnp.float32
 BF16 = jnp.bfloat16
 
 
-def circulant_blocks(eigenvalues):
+def block_rows(eigenvalues):
     counter = np.arange(DET)
     waves = np.exp(2j * np.pi * (np.outer(counter, counter) % DET) / DET)
     column = waves @ eigenvalues / DET
-    full = column[(counter[:, None] - counter[None, :]) % DET]
-    first, second = full[:HALF, :HALF], full[:HALF, HALF:]
-
-    def real_form(block):
-        return np.block([[block.real, -block.imag], [block.imag, block.real]])
-
-    return np.stack([real_form((first + second) / 2), real_form((first - second) / 2)])
-
-
-def split_table(table):
-    table = table.astype(np.float32)
-    high = table.astype(BF16)
-    low = (table - high.astype(np.float32)).astype(BF16)
-    return np.stack([high, low], axis=-3)
-
-
-def shift_tables():
+    columns = [(column[:HALF] + column[HALF:]) / 2, (column[:HALF] - column[HALF:]) / 2]
+    back = (-np.arange(HALF)) % HALF
+    rows = [block[back] for block in columns]
+    return np.stack([part for block in rows + columns for part in (block.real, block.imag)])
+
+
+def shift_rows():
     counter = np.arange(DET)
     signed = np.where(counter < DET // 2, counter, counter - DET).astype(np.float64)
     chirp = -np.pi * fresnel * signed * signed / DET
     slope = -2j * np.pi * signed / DET
-    plain, derived = [], []
-    for step in range(RAMPS):
-        factor = np.exp(1j * chirp + slope * (step / RAMPS))
-        plain.append(circulant_blocks(factor))
-        derived.append(circulant_blocks(slope * factor))
-    plain, derived = np.stack(plain), np.stack(derived)
-    slope_blocks = circulant_blocks(slope)
-    turned = np.swapaxes(plain, -1, -2)
-    order = (plain, turned, derived, np.swapaxes(slope_blocks, -1, -2)[None])
-    return np.concatenate([split_table(table) for table in order])
+    factors = [np.exp(1j * chirp + slope * (step / RAMPS)) for step in range(RAMPS)]
+    every = factors + [slope * factor for factor in factors] + [slope]
+    return np.stack([block_rows(factor) for factor in every]).astype(np.float32)
+
+
+def fill_table(rows, turned, table):
+    down = lax.broadcasted_iota(jnp.int32, (HALF, HALF), 0)
+    along = lax.broadcasted_iota(jnp.int32, (HALF, HALF), 1)
+    ahead = along >= down if turned else down >= along
+    for block in range(2):
+        parts = []
+        for part in range(2):
+            at = 4 * turned + 2 * block + part
+            whole = pltpu.roll(jnp.broadcast_to(rows[at : at + 1, :], (HALF, HALF)), 0, 1, stride=1, stride_axis=0)
+            parts.append(jnp.where(ahead, whole, -whole) if block else whole)
+        real, imag = parts
+        left, right = (imag, -imag) if turned else (-imag, imag)
+        for half, pair in enumerate(((real, left), (right, real))):
+            at = pl.ds(half * HALF, HALF)
+            table[block, 0, at, :], table[block, 1, at, :] = split(jnp.concatenate(pair, axis=1))
+
+
+def fill_tables(ramp, vectors, turned1, plain0, turned0, plain1):
+    rows0, rows1 = vectors[ramp[0, 0]], vectors[ramp[0, 1]]
+    fill_table(rows1, True, turned1)
+    fill_table(rows0, False, plain0)
+    fill_table(rows0, True, turned0)
+    fill_table(rows1, False, plain1)
+
+
+def tables_call(ramp, vectors):
+    vmem = pl.BlockSpec(memory_space=pltpu.VMEM)
+    return pl.pallas_call(
+        fill_tables,
+        out_shape=[jax.ShapeDtypeStruct((2, 2, DET, DET), BF16)] * 4,
+        in_specs=[pl.BlockSpec(memory_space=pltpu.SMEM), vmem],
+        out_specs=[vmem] * 4,
+        compiler_params=pltpu.CompilerParams(vmem_limit_bytes=VMEM_LIMIT),
+        name="tables",
+        cost_estimate=pl.CostEstimate(flops=WEIGHT, bytes_accessed=WEIGHT // 400, transcendentals=0),
+    )(ramp, vectors)
 
 
 def split(value):
@@ -79,38 +102,27 @@
     corner, ramp, place = take(3)
     if last:
         patch_in, merged, from_above, from_below, grad_before = take(5)
-        total_mine, total_other = take(2)
+        total_mine, total_other, keep_before, send_before = take(4)
     else:
         own_first, own_second, lower, right, side, below = take(6)
-    probe, measured, tables = take(3)
-    if last:
-        grad_out, probe_out, keep_out, send_out, shift_out = take(5)
+    probe, measured = take(2)
+    if last:
+        (vectors,) = take(1)
+    else:
+        turned1, plain0, turned0, plain1 = take(4)
+    if last:
+        grad_out, keep_out, send_out, shift_out = take(4)
     else:
         grad_out, patch_out, keep_out, send_out = take(4)
     doubled, field, high, low, result, z_high, z_low, z_result = take(8)
     if last:
-        slope_result, derived_result = take(2)
-    plain0, turned0, plain1, turned1 = take(4)
-    if last:
-        derived0, slope1 = take(2)
-    (arrived,) = take(1)
-
+        slope_result, derived_result, probe_now = take(3)
     row0, col0, core = corner[0, 0], corner[0, 1], place[0]
-    step0, step1 = ramp[0, 0], ramp[0, 1]
-    moves = [
-        (tables.at[RAMPS + step1], turned1),
-        (tables.at[step0], plain0),
-        (tables.at[RAMPS + step0], turned0),
-        (tables.at[step1], plain1),
-    ]
-    if last:
-        moves += [(tables.at[2 * RAMPS + step0], derived0), (tables.at[3 * RAMPS], slope1)]
-    copies = [
-        pltpu.make_async_copy(source, target, arrived.at[index])
-        for index, (source, target) in enumerate(moves)
-    ]
-    for copy in copies:
-        copy.start()
+    if last:
+        turned1, plain0, turned0, plain1, slope1, derived0 = take(6)
+        fill_tables(ramp, vectors, turned1, plain0, turned0, plain1)
+        fill_table(vectors[2 * RAMPS], True, slope1)
+        fill_table(vectors[RAMPS + ramp[0, 0]], False, derived0)
 
     def build(step):
         start = step * STRIP
@@ -142,12 +154,12 @@
             for mode in range(MODES):
                 mine = total_mine[mode, rows, :]
                 other = total_other[mode, rows, :]
-                probe_out[0, mode, rows, :] = probe[0, mode, rows, :] - rate * jnp.where(core == 0, mine, other)
-                probe_out[1, mode, rows, :] = probe[1, mode, rows, :] - rate * jnp.where(core == 0, other, mine)
+                probe_now[0, mode, rows, :] = probe[0, mode, rows, :] - rate * jnp.where(core == 0, mine, other)
+                probe_now[1, mode, rows, :] = probe[1, mode, rows, :] - rate * jnp.where(core == 0, other, mine)
 
     for step in range(DET // STRIP):
         build(step)
-    modes = probe_out if last else probe
+    modes = probe_now if last else probe
     back = lax.rem(DET - col0, DET)
 
     def rows_from(part, first):
@@ -180,9 +192,6 @@
         return 0
 
     lax.fori_loop(0, DET // STRIP, enter, 0, unroll=16)
-    copies[0].wait()
-    if last:
-        copies[5].wait()
 
     def times_right(block, mode, table, where):
         at = pl.ds(mode * DET, DET)
@@ -225,9 +234,6 @@
         return 0
 
     lax.fori_loop(0, HALF // STRIP, rows_to_blocks, 0, unroll=8)
-    copies[1].wait()
-    if last:
-        copies[4].wait()
 
     for block in range(2):
         for mode in range(MODES):
@@ -281,7 +287,6 @@
 
     zeros = jnp.zeros((STRIP, DET), F32) if last else 0
     slope_rows = lax.fori_loop(0, HALF // STRIP, misfits, zeros, unroll=8)
-    copies[2].wait()
 
     for block in range(2):
         for mode in range(MODES):
@@ -306,7 +311,6 @@
         return 0
 
     lax.fori_loop(0, HALF // STRIP, blocks_to_rows, 0, unroll=8)
-    copies[3].wait()
 
     for block in range(2):
         for mode in range(MODES):
@@ -332,8 +336,13 @@
             grad_imag = grad_imag + probe_real * exit_imag - probe_imag * exit_real
             mode_real = real * exit_real + imag * exit_imag
             mode_imag = real * exit_imag - imag * exit_real
-            keep_out[mode, rows, :] = jnp.where(core == 0, mode_real, mode_imag)
-            send_out[mode, rows, :] = jnp.where(core == 0, mode_imag, mode_real)
+            keep = jnp.where(core == 0, mode_real, mode_imag)
+            send = jnp.where(core == 0, mode_imag, mode_real)
+            if last:
+                keep = keep + keep_before[mode, rows, :]
+                send = send + send_before[mode, rows, :]
+            keep_out[mode, rows, :] = keep
+            send_out[mode, rows, :] = send
         again = pl.ds(pl.multiple_of(start + DET, STRIP), STRIP)
         for part, value in ((0, grad_real), (1, grad_imag)):
             turned = pltpu.roll(value, col0, 1)
@@ -348,16 +357,30 @@
         rows = pl.ds(start, STRIP)
         for part in range(2):
             value = rows_from(part, DET - row0 + start)
+            at = pl.ds(pl.multiple_of(part * DET + start, STRIP), STRIP)
             if last:
-                value = value + grad_before[part, rows, :]
-            grad_out[part, rows, :] = value
+                grad_out[part, rows, :] = value + grad_before[at, :]
+            else:
+                grad_out[at, :] = value
         return 0
 
     lax.fori_loop(0, DET // STRIP, wrap, 0, unroll=16)
 
     if last:
-        lane = lax.broadcasted_iota(jnp.int32, (8, HALF), 1)
+        lane = lax.broadcasted_iota(jnp.int32, (1, 2), 1)
         shift_out[...] = jnp.where(lane == 0, jnp.sum(slope_rows), 2.0 * jnp.sum(slope_cols)) / DET
+    else:
+        grad_out[pl.ds(2 * DET, EXTRA), :] = corner_rows(row0, col0)
+
+
+def corner_rows(row0, col0):
+    lane = lax.broadcasted_iota(jnp.int32, (EXTRA, DET), 1)
+    return jnp.where(lane == 0, row0.astype(F32), jnp.where(lane == 1, col0.astype(F32), 0.0))
+
+
+def corner_of(ref, at):
+    row = ref[pl.ds(at, EXTRA), :]
+    return row[:1, :1], row[:1, 1:2]
 
 
 def gradient_call(last, rate, scalars, operands, kept):
@@ -366,15 +389,9 @@
     vmem = pl.BlockSpec(memory_space=pltpu.VMEM)
     smem = pl.BlockSpec(memory_space=pltpu.SMEM)
     if last:
-        outs = (
-            plane,
-            jax.ShapeDtypeStruct((2, MODES, DET, DET), F32),
-            half,
-            half,
-            jax.ShapeDtypeStruct((8, HALF), F32),
-        )
+        outs = (plane, half, half, jax.ShapeDtypeStruct((1, 2), F32))
     else:
-        outs = (plane, plane, half, half)
+        outs = (jax.ShapeDtypeStruct((2 * DET + EXTRA, DET), F32), plane, half, half)
     scratch = [
         pltpu.VMEM((2, 2 * DET + 8, DET), F32),
         pltpu.VMEM((2, DET, DET), F32),
@@ -389,10 +406,10 @@
         scratch += [
             pltpu.VMEM((2, MODES * DET, DET), F32),
             pltpu.VMEM((2, DET, MODES * DET), F32),
+            pltpu.VMEM((2, MODES, DET, DET), F32),
         ]
-    tables = 6 if last else 4
-    scratch += [pltpu.VMEM((2, 2, DET, DET), BF16)] * tables
-    scratch += [pltpu.SemaphoreType.DMA((tables,))]
+    if last:
+        scratch += [pltpu.VMEM((2, 2, DET, DET), BF16)] * 6
 
     def body(*refs):
         gradient_kernel(last, rate, *refs)
@@ -402,10 +419,10 @@
         out_shape=outs,
         in_specs=[smem] * len(scalars)
         + [vmem] * len(operands)
-        + [vmem, vmem, pl.BlockSpec(memory_space=pltpu.HBM)],
+        + [vmem] * len(kept),
         out_specs=(vmem,) * len(outs),
         scratch_shapes=scratch,
-        compiler_params=pltpu.CompilerParams(vmem_limit_bytes=(42 if last else 44) * 2**20),
+        compiler_params=pltpu.CompilerParams(vmem_limit_bytes=VMEM_LIMIT),
         name="gradient_last" if last else "gradient_first",
     )(*scalars, *operands, *kept)
 
@@ -433,13 +450,13 @@
         out_shape=[jax.ShapeDtypeStruct((2, DET, DET), F32)] * outputs,
         in_specs=[pl.BlockSpec(memory_space=pltpu.SMEM)] * len(scalars) + [vmem] * len(operands),
         out_specs=[vmem] * outputs,
-        compiler_params=pltpu.CompilerParams(vmem_limit_bytes=8 * 2**20),
+        compiler_params=pltpu.CompilerParams(vmem_limit_bytes=VMEM_LIMIT),
         name=name,
         cost_estimate=pl.CostEstimate(flops=weight, bytes_accessed=weight // 400, transcendentals=0) if weight else None,
     )(*scalars, *operands)
 
 
-def side_kernel(left_at, above_at, first, second, lower, right, to_left, to_above):
+def side_kernel(here_at, left_at, above_at, first, second, lower, right, to_left, to_above):
     for step in range(2 * DET // STRIP):
         flat = step * STRIP
         if flat < FIRST:
@@ -450,42 +467,85 @@
             at = pl.ds(flat - FIRST, STRIP)
             col = lax.broadcasted_iota(jnp.int32, (STRIP, DET), 1)
             to_above[at, :] = jnp.where(col >= above_at[0, 1], second[at, :], right[at, :])
-
-
-def side_call(left_at, above_at, *operands):
+    to_above[pl.ds(2 * DET - FIRST, EXTRA), :] = corner_rows(here_at[0, 0], here_at[0, 1])
+
+
+def side_call(here_at, left_at, above_at, *operands):
     vmem = pl.BlockSpec(memory_space=pltpu.VMEM)
     return pl.pallas_call(
         side_kernel,
-        out_shape=[jax.ShapeDtypeStruct((rows, DET), F32) for rows in (FIRST, 2 * DET - FIRST)],
+        out_shape=[jax.ShapeDtypeStruct((rows, DET), F32) for rows in (FIRST, 2 * DET - FIRST + EXTRA)],
+        in_specs=[pl.BlockSpec(memory_space=pltpu.SMEM)] * 3 + [vmem] * 4,
+        out_specs=[vmem] * 2,
+        compiler_params=pltpu.CompilerParams(vmem_limit_bytes=VMEM_LIMIT),
+        name="sides",
+    )(here_at, left_at, above_at, *operands)
+
+
+def merge_kernel(here_at, above_at, own_ref, left_ref, right_ref, below_ref, merged, down, up):
+    left_row, left_col = corner_of(left_ref, 2 * DET)
+    right_row, right_col = corner_of(right_ref, 2 * DET)
+    _, below_col = corner_of(below_ref, 2 * DET - FIRST)
+    above_col = above_at[0, 1].astype(F32)
+
+    def strip(step, _):
+        start = pl.multiple_of(step * STRIP, STRIP)
+        row = lax.broadcasted_iota(jnp.int32, (STRIP, DET), 0) + start
+        col = lax.broadcasted_iota(jnp.int32, (STRIP, DET), 1)
+        for part in range(2):
+            flat = pl.ds(pl.multiple_of(part * DET + start, STRIP), STRIP)
+            values = merge_cells(
+                row.astype(F32),
+                col.astype(F32),
+                (here_at[0, 0].astype(F32), here_at[0, 1].astype(F32)),
+                (left_row, left_col),
+                (right_row, right_col),
+                (below_col, above_col),
+                *(ref[flat, :] for ref in (own_ref, left_ref, right_ref)),
+            )
+            for ref, value in zip((merged, down, up), values):
+                ref[part, pl.ds(start, STRIP), :] = value
+        return 0
+
+    lax.fori_loop(0, DET // STRIP, strip, 0, unroll=16)
+
+
+def merge_call(here_at, above_at, *operands):
+    vmem = pl.BlockSpec(memory_space=pltpu.VMEM)
+    return pl.pallas_call(
+        merge_kernel,
+        out_shape=[jax.ShapeDtypeStruct((2, DET, DET), F32)] * 3,
         in_specs=[pl.BlockSpec(memory_space=pltpu.SMEM)] * 2 + [vmem] * 4,
-        out_specs=[vmem] * 2,
-        compiler_params=pltpu.CompilerParams(vmem_limit_bytes=8 * 2**20),
-        name="sides",
-    )(left_at, above_at, *operands)
-
-
-def merge_cells(corners, row, col, own, left, right):
-    here_at, left_at, right_at, above_at, below_at = corners
-    inside = row < here_at[0, 0]
-    inside_left = row < left_at[0, 0]
-    inside_right = row < right_at[0, 0]
-    near = col >= here_at[0, 1]
-    left = jnp.where(col < left_at[0, 1], left, 0.0)
-    right = jnp.where(col >= right_at[0, 1], right, 0.0)
+        out_specs=[vmem] * 3,
+        compiler_params=pltpu.CompilerParams(vmem_limit_bytes=VMEM_LIMIT),
+        name="merge",
+        cost_estimate=pl.CostEstimate(flops=WEIGHT, bytes_accessed=WEIGHT // 400, transcendentals=0),
+    )(here_at, above_at, *operands)
+
+
+def merge_cells(row, col, here_at, left_at, right_at, starts, own, left, right):
+    below_start, above_start = starts
+    inside = row < here_at[0]
+    inside_left = row < left_at[0]
+    inside_right = row < right_at[0]
+    near = col >= here_at[1]
+    left = jnp.where(col < left_at[1], left, 0.0)
+    right = jnp.where(col >= right_at[1], right, 0.0)
     own_near = jnp.where(near, own, 0.0)
     own_far = jnp.where(near, 0.0, own)
 
     def gathered(wanted, start):
-        near_sum = jnp.where(inside == wanted, own_near, 0.0) + jnp.where(inside_left == wanted, left, 0.0)
-        far_sum = jnp.where(inside == wanted, own_far, 0.0) + jnp.where(inside_right == wanted, right, 0.0)
+        kept = (lambda at, value: jnp.where(at, value, 0.0)) if wanted else (lambda at, value: jnp.where(at, 0.0, value))
+        near_sum = kept(inside, own_near) + kept(inside_left, left)
+        far_sum = kept(inside, own_far) + kept(inside_right, right)
         return jnp.where(col >= start, near_sum, far_sum)
 
     merged = own + jnp.where(
         near,
-        jnp.where(inside == inside_left, left, 0.0),
-        jnp.where(inside == inside_right, right, 0.0),
-    )
-    return merged, gathered(True, below_at[0, 1]), gathered(False, above_at[0, 1])
+        jnp.where(inside ^ inside_left, 0.0, left),
+        jnp.where(inside ^ inside_right, 0.0, right),
+    )
+    return merged, gathered(True, below_start), gathered(False, above_start)
 
 
 def settle_cells(corners, row, col, own, left):
@@ -520,6 +580,20 @@
     while distance < lax.axis_size("frame"):
         part = part + swapped(part, "frame", distance)
         distance *= 2
+    return part
+
+
+def quick_chip_sum(part):
+    if lax.axis_size("frame") != 16:
+        return chip_sum(part)
+    for pairs in (
+        ((0, 1), (2, 3), (4, 5), (6, 7)),
+        ((1, 2), (3, 4), (5, 6), (7, 0)),
+        ((1, 6), (2, 5), (3, 0), (4, 7)),
+    ):
+        ways = [way for one, other in pairs for way in ((one, other), (other, one))]
+        moves = [(2 * one + core, 2 * other + core) for one, other in ways for core in range(2)]
+        part = part + lax.ppermute(part, "frame", moves)
     return part
 
 
@@ -550,48 +624,41 @@
     at_left = shifted(offsets, "frame", 1)
     at_above = shifted(offsets, "tile", 1)
     lower, right, at_left, at_above = together((lower, right, at_left, at_above))
-    to_left, to_above = side_call(at_left, at_above, first, second, lower, right)
-    to_left, to_above, corner = together((to_left, to_above, offsets))
+    to_left, to_above = side_call(offsets, at_left, at_above, first, second, lower, right)
     side = shifted(to_left, "frame", -1)
     below = shifted(to_above, "tile", -1)
-    at_right = shifted(corner, "frame", -1)
-    at_below = shifted(corner, "tile", -1)
-    side, below, at_right, at_below = together((side, below, at_right, at_below))
+
+    ramp, _, _ = together((ramp_steps, to_left, to_above))
+    vectors = jnp.asarray(shift_rows())
+    side, below, *filled = together((side, below, *tables_call(ramp, vectors)))
 
     scalars = (offsets, ramp_steps, place)
-    kept = (probe_modes, measured, jnp.asarray(shift_tables()))
+    kept = (probe_modes, measured)
     grad1, patch, keep1, send1 = gradient_call(
-        False, rate, scalars, (first, second, lower, right, side, below), kept
+        False, rate, scalars, (first, second, lower, right, side, below), kept + tuple(filled)
     )
 
     grad_left = shifted(grad1, "frame", 1)
     grad_right = shifted(grad1, "frame", -1)
     parts = tile_parts(keep1, send1)
-    merged, down, up = plane_call(
-        "merge",
-        merge_cells,
-        (offsets, at_left, at_right, at_above, at_below),
-        (grad1, grad_left, grad_right),
-        3,
-        WEIGHT,
-    )
+    merged, down, up = merge_call(offsets, at_above, grad1, grad_left, grad_right, below)
     parts, _, _, _ = together((parts, merged, down, up))
     from_above = shifted(down, "tile", 1)
     from_below = shifted(up, "tile", -1)
-    part = chip_sum(jnp.sum(parts, axis=0))
+    part = quick_chip_sum(jnp.sum(parts, axis=0))
     part, from_above, from_below = together((part, from_above, from_below))
     mine, other = spread(part)
 
-    grad_total, modes_now, keep2, send2, shift_grad = gradient_call(
+    grad_total, keep2, send2, shift_grad = gradient_call(
         True,
         rate,
         scalars,
-        (patch, merged, from_above, from_below, grad1, mine, other),
-        kept,
+        (patch, merged, from_above, from_below, grad1, mine, other, keep1, send1),
+        kept + (vectors,),
     )
 
     count = lax.axis_size("tile")
-    planes = modes_now.reshape(2, count, MODES * DET // count, DET)
+    planes = probe_modes.reshape(2, count, MODES * DET // count, DET)
     own_part = lax.dynamic_slice(planes, (core, tile_at, 0, 0), (1, 1) + planes.shape[2:])[0, 0]
 
     moved = shifted(grad_total, "frame", 1)
@@ -609,7 +676,7 @@
     mine, other = spread(part)
     plane = lax.broadcasted_iota(jnp.int32, (2, MODES, DET, DET), 0)
     probe_final = jnp.where(plane == core, mine[None], other[None])
-    return (object_final, probe_final, shift_grad[:1, :2])
+    return (object_final, probe_final, shift_grad)
 
 
 def solution(mesh):

time: 182 us -> 176 us (0.967)
  starting transfers between devices: 78.8 us -> 72.9 us
  Pallas kernels: 21.4 us -> 18.9 us
  blocking collectives: 27.8 us -> 29.7 us
    ppermute x10 -> x7, starting transfers between devices: 27.1 us -> 14.4 us  [swapped(): lax.ppermute(value, axis, [(source, source ^ distance) for source in rang...]
    ppermute x0 -> x3, starting transfers between devices: none -> 9.77 us  [quick_chip_sum(): part = part + lax.ppermute(part, 'frame', moves)]
    ppermute x10 -> x7, waiting for transfers between devices: 19.5 us -> 11 us  [swapped(): lax.ppermute(value, axis, [(source, source ^ distance) for source in rang...]
    ppermute x0 -> x3, waiting for transfers between devices: none -> 6.01 us  [quick_chip_sum(): part = part + lax.ppermute(part, 'frame', moves)]
    ppermute x14 -> x12, starting transfers between devices: 39 us -> 34.3 us  [shifted(): lax.ppermute(value, axis, [(source, source + steps) for source in range(i...]
    pallas_call x0 -> x2, Pallas kernels: none -> 3.76 us  [the longest x1 2.86 us: merge_call(): pl.pallas_call(merge_kernel, out_shape=[jax.ShapeDtypeStruct((2, DET, DET...]
    pallas_call x2, Pallas kernels: 16.3 us -> 13.3 us  [gradient_call(): pl.pallas_call(body, out_shape=outs, in_specs=[smem] * len(scalars) + [vm...]
    all_to_all x2, waiting for transfers between devices: 11.1 us -> 14 us  [tile_parts(): lax.all_to_all(summed.reshape(count, MODES * DET // count, DET), 'tile',...]
  transfers between devices with their start and end apart: 26 -> 24, of which waited for: 13 -> 12; matrix products, arithmetic and copies ran while one was open for 4% -> 4% of each run, Pallas kernels for 2% -> 3%
where the time goes in v4:
time: 176 us; the launch traced here: 175 us
  starting transfers between devices  72.9 us (41%)
  waiting for transfers between devices  38 us (22%)
  blocking collectives  29.7 us (17%)
  Pallas kernels  18.9 us (11%)
  other arithmetic  7.83 us (4%)
  local copies, waits for them, and re-layouts  6.33 us (4%)
    ppermute x12, starting transfers between devices, shifted(): lax.ppermute(value, axis, [(source, source + steps) for source in range(i...  34.3 us
    all_to_all x2, blocking collectives, spread(): mine = lax.all_to_all(parts, 'tile', 0, 0).reshape(MODES, DET, DET)  29.7 us
    all_to_all x2, starting transfers between devices, tile_parts(): lax.all_to_all(summed.reshape(count, MODES * DET // count, DET), 'tile',...  14.4 us
    ppermute x7, starting transfers between devices, swapped(): lax.ppermute(value, axis, [(source, source ^ distance) for source in rang...  14.4 us
    all_to_all x2, waiting for transfers between devices, tile_parts(): lax.all_to_all(summed.reshape(count, MODES * DET // count, DET), 'tile',...  14 us
    pallas_call x2, Pallas kernels, gradient_call(): pl.pallas_call(body, out_shape=outs, in_specs=[smem] * len(scalars) + [vm...  13.3 us
    ppermute x7, waiting for transfers between devices, swapped(): lax.ppermute(value, axis, [(source, source ^ distance) for source in rang...  11 us
    ppermute x3, starting transfers between devices, quick_chip_sum(): part = part + lax.ppermute(part, 'frame', moves)  9.77 us
  transfers between devices with their start and end apart: 24, of which 12 were waited for; matrix products, arithmetic and copies ran while one was open for 4% of the time, Pallas kernels for 3%

profile of v4, /device:TPU:1, one launch (start us, length us, event | category | flops | bytes accessed | tf_op | source)
XLA Modules:
  0.0 174.6 jit_solution(9384690505448695225)
XLA Ops:
  3.9 5.1 %collective-permute-start.1 = (f32[128,256]{1,0:T(8,128)S(1)}, f32[128,256]{1,0:T(8,128)S(1)}, u32[]{:S(2)}, u32[]{:S(2)}) collective-permute-start(f32[128,256]{1,0:T(8,128)S(1)} %slice.9.second.refs_4_), channel_id=1, source_target_pairs={{1,0},{2,1},{3,2},{4,3},{5,4},{6,5},{7,6},{8,7},{9,8},{10,9},{11,1... | collective-permute-start | bytes 393224 | tf_op jit(solution)/shard_map/ppermute | solution.py:564
  11.0 4.3 %collective-permute-start.3 = (s32[1,2]{1,0:T(1,128)}, s32[1,2]{1,0:T(1,128)S(1)}, u32[]{:S(2)}, u32[]{:S(2)}) collective-permute-start(s32[1,2]{1,0:T(1,128)} %refs_0_.5), channel_id=1, source_target_pairs={{0,16},{16,32},{32,48},{48,64},{64,80},{80,96},{96,112},{112,128},... | collective-permute-start | bytes 32 | tf_op jit(solution)/shard_map/ppermute | solution.py:564
  17.4 3.3 %collective-permute-start.4 = (f32[384,256]{1,0:T(8,128)S(1)}, f32[384,256]{1,0:T(8,128)S(1)}, u32[]{:S(2)}, u32[]{:S(2)}) collective-permute-start(f32[384,256]{1,0:T(8,128)S(1)} %get-tuple-element.44), channel_id=1, source_target_pairs={{1,0},{2,1},{3,2},{4,3},{5,4},{6,5},{7,6},{8,7},{9,8},{10,9},{11,1... | collective-permute-start | bytes 1179656 | tf_op jit(solution)/shard_map/ppermute | solution.py:564
  23.1 5.1 %collective-permute-done.5.refs_8_.below_ref = f32[136,256]{1,0:T(8,128)S(1)} collective-permute-done((f32[136,256]{1,0:T(8,128)S(1)}, f32[136,256]{1,0:T(8,128)S(1)}, u32[]{:S(2)}, u32[]{:S(2)}) %collective-permute-start.5) | collective-permute-done | bytes 139296 | tf_op jit(solution)/shard_map/ppermute | solution.py:564
  29.2 5.5 %gradient_first.1 = (f32[520,256]{1,0:T(8,128)}, f32[2,256,256]{2,1,0:T(8,128)S(1)}, f32[3,256,256]{2,1,0:T(8,128)S(1)}, f32[3,256,256]{2,1,0:T(8,128)S(1)}) custom-call(s32[1,2]{1,0:T(1,128)S(1)} %copy-done.15, s32[1,2]{1,0:T(1,128)S(1)} %copy-done.16, s32[3]{0:T(128)S(1)} %pad_add_fusion.refs_2_, f32[384,256]{1,0:T(8,128)S(1)} %slice.8.first.refs_3_, ...), custom_call_target="tpu_custom_call" | custom-call | tf_op jit(solution)/shard_map/gradient_first/pallas_call | solution.py:417
  36.8 2.5 %collective-permute-start.6 = (f32[520,256]{1,0:T(8,128)}, f32[520,256]{1,0:T(8,128)}, u32[]{:S(2)}, u32[]{:S(2)}) collective-permute-start(f32[520,256]{1,0:T(8,128)} %get-tuple-element.58.own_ref.refs_7_), channel_id=1, source_target_pairs={{0,1},{1,2},{2,3},{3,4},{4,5},{5,6},{6,7},{7,8},{8,9},{9,10},{10,1... | collective-permute-start | bytes 1597448 | tf_op jit(solution)/shard_map/ppermute | solution.py:564
  39.3 2.6 %collective-permute-start.7 = (f32[520,256]{1,0:T(8,128)}, f32[520,256]{1,0:T(8,128)}, u32[]{:S(2)}, u32[]{:S(2)}) collective-permute-start(f32[520,256]{1,0:T(8,128)} %get-tuple-element.58.own_ref.refs_7_), channel_id=1, source_target_pairs={{1,0},{2,1},{3,2},{4,3},{5,4},{6,5},{7,6},{8,7},{9,8},{10,9},{11,1... | collective-permute-start | bytes 1597448 | tf_op jit(solution)/shard_map/ppermute | solution.py:564
  43.0 10.1 %all-to-all-start = ((f32[16,48,256]{2,1,0:T(8,128)}), f32[16,48,256]{2,1,0:T(8,128)}, u32[]{:S(2)}, u32[]{:S(2)}) async-start(f32[16,48,256]{2,1,0:T(8,128)} %bitcast.14), calls=%async_computation | async-start | bytes 1572864 | tf_op jit(solution)/shard_map/all_to_all | solution.py:575
  53.2 2.9 %merge.1 = (f32[2,256,256]{2,1,0:T(8,128)S(1)}, f32[2,256,256]{2,1,0:T(8,128)}, f32[2,256,256]{2,1,0:T(8,128)}) custom-call(s32[1,2]{1,0:T(1,128)S(1)} %copy-done.15, s32[1,2]{1,0:T(1,128)S(1)} %copy-done.18, f32[520,256]{1,0:T(8,128)} %get-tuple-element.58.own_ref.refs_7_, f32[520,256]{1,0:T(8,128)} %collective-permute-done.6.left_ref, ...), custom_call_target="tpu_custom_call" | custom-call | flops 20000000000 | bytes 50000000 | tf_op jit(solution)/shard_map/merge/pallas_call | solution.py:515
  56.9 4.0 %collective-permute-start.12 = (f32[2,256,256]{2,1,0:T(8,128)}, f32[2,256,256]{2,1,0:T(8,128)}, u32[]{:S(2)}, u32[]{:S(2)}) collective-permute-start(f32[2,256,256]{2,1,0:T(8,128)} %get-tuple-element.62), channel_id=1, source_target_pairs={{0,16},{16,32},{32,48},{48,64},{64,80},{80,96},{96,112},{112,128},... | collective-permute-start | bytes 1572872 | tf_op jit(solution)/shard_map/ppermute | solution.py:564
  62.2 5.1 %all-to-all-done = f32[16,48,256]{2,1,0:T(8,128)} async-done(((f32[16,48,256]{2,1,0:T(8,128)}), f32[16,48,256]{2,1,0:T(8,128)}, u32[]{:S(2)}, u32[]{:S(2)}) %all-to-all-start) | async-done | bytes 786464 | tf_op jit(solution)/shard_map/all_to_all | solution.py:575
  68.9 3.1 %collective-permute-done.9 = f32[48,256]{1,0:T(8,128)S(1)} collective-permute-done((f32[48,256]{1,0:T(8,128)S(1)}, f32[48,256]{1,0:T(8,128)S(1)}, u32[]{:S(2)}, u32[]{:S(2)}) %collective-permute-start.9) | collective-permute-done | bytes 49184 | tf_op jit(solution)/shard_map/ppermute | solution.py:596
  71.9 4.2 %collective-permute-start.10 = (f32[48,256]{1,0:T(8,128)S(1)}, f32[48,256]{1,0:T(8,128)S(1)}, u32[]{:S(2)}, u32[]{:S(2)}) collective-permute-start(f32[48,256]{1,0:T(8,128)S(1)} %add.34), channel_id=1, source_target_pairs={{2,4},{3,5},{4,2},{5,3},{6,8},{7,9},{8,6},{9,7},{10,12},{11,13},{1... | collective-permute-start | bytes 147464 | tf_op jit(solution)/shard_map/ppermute | solution.py:596
  77.6 5.2 %collective-permute-start.11 = (f32[48,256]{1,0:T(8,128)S(1)}, f32[48,256]{1,0:T(8,128)S(1)}, u32[]{:S(2)}, u32[]{:S(2)}) collective-permute-start(f32[48,256]{1,0:T(8,128)S(1)} %add.35), channel_id=1, source_target_pairs={{2,12},{3,13},{12,2},{13,3},{4,10},{5,11},{10,4},{11,5},{6,0},{7,1... | collective-permute-start | bytes 147464 | tf_op jit(solution)/shard_map/ppermute | solution.py:596
  84.4 15.4 %all_to_all.20 = f32[16,48,256]{2,1,0:T(8,128)S(1)} all-to-all(f32[16,48,256]{2,1,0:T(8,128)S(1)} %broadcast_in_dim.31), channel_id=1, replica_groups=mesh['tile'=16,'frame'=16] {'tile'}, dimensions={0} | all-to-all | bytes 1572864 | tf_op jit(solution)/shard_map/all_to_all | solution.py:603
  99.8 4.0 %collective-permute-start.14 = (f32[3,256,256]{2,1,0:T(8,128)S(1)}, f32[3,256,256]{2,1,0:T(8,128)S(1)}, u32[]{:S(2)}, u32[]{:S(2)}) collective-permute-start(f32[3,256,256]{2,1,0:T(8,128)S(1)} %bitcast.12), channel_id=1, source_target_pairs={{0,1},{1,0},{2,3},{3,2},{4,5},{5,4},{6,7},{7,6},{8,9},{9,8},{10,11... | collective-permute-start | bytes 2359304 | tf_op jit(solution)/shard_map/ppermute | solution.py:569
  105.8 7.8 %gradient_last.1 = (f32[2,256,256]{2,1,0:T(8,128)}, f32[3,256,256]{2,1,0:T(8,128)S(1)}, f32[3,256,256]{2,1,0:T(8,128)S(1)}, f32[1,2]{1,0:T(1,128)}) custom-call(s32[1,2]{1,0:T(1,128)S(1)} %copy-done.15, s32[1,2]{1,0:T(1,128)S(1)} %copy-done.16, s32[3]{0:T(128)S(1)} %pad_add_fusion.refs_2_, f32[2,256,256]{2,1,0:T(8,128)S(1)} %copy-done.5, ...), custom_call_target="tpu_custom_call" | custom-call | tf_op jit(solution)/shard_map/gradient_last/pallas_call | solution.py:417
  113.9 3.7 %collective-permute-start.15 = (f32[2,256,256]{2,1,0:T(8,128)}, f32[2,256,256]{2,1,0:T(8,128)S(1)}, u32[]{:S(2)}, u32[]{:S(2)}) collective-permute-start(f32[2,256,256]{2,1,0:T(8,128)} %get-tuple-element.68.refs_2_), channel_id=1, source_target_pairs={{0,1},{1,2},{2,3},{3,4},{4,5},{5,6},{6,7},{7,8},{8,9},{9,10},{10,1... | collective-permute-start | bytes 1572872 | tf_op jit(solution)/shard_map/ppermute | solution.py:564
  118.6 4.3 %all-to-all-start.2 = ((f32[16,48,256]{2,1,0:T(8,128)}), f32[16,48,256]{2,1,0:T(8,128)}, u32[]{:S(2)}, u32[]{:S(2)}) async-start(f32[16,48,256]{2,1,0:T(8,128)} %bitcast.8), calls=%async_computation.2 | async-start | bytes 1572864 | tf_op jit(solution)/shard_map/all_to_all | solution.py:575
  125.3 2.8 %collective-permute-start.20 = (f32[2,256,256]{2,1,0:T(8,128)S(1)}, f32[2,256,256]{2,1,0:T(8,128)}, u32[]{:S(2)}, u32[]{:S(2)}) collective-permute-start(f32[2,256,256]{2,1,0:T(8,128)S(1)} %get-tuple-element.72), channel_id=1, source_target_pairs={{0,16},{16,32},{32,48},{48,64},{64,80},{80,96},{96,112},{112,128},... | collective-permute-start | bytes 1572872 | tf_op jit(solution)/shard_map/ppermute | solution.py:564
  128.1 8.9 %all-to-all-done.2 = f32[16,48,256]{2,1,0:T(8,128)} async-done(((f32[16,48,256]{2,1,0:T(8,128)}), f32[16,48,256]{2,1,0:T(8,128)}, u32[]{:S(2)}, u32[]{:S(2)}) %all-to-all-start.2) | async-done | bytes 786464 | tf_op jit(solution)/shard_map/all_to_all | solution.py:575
  147.5 4.8 %collective-permute-done.19 = f32[48,256]{1,0:T(8,128)S(1)} collective-permute-done((f32[48,256]{1,0:T(8,128)S(1)}, f32[48,256]{1,0:T(8,128)S(1)}, u32[]{:S(2)}, u32[]{:S(2)}) %collective-permute-start.19) | collective-permute-done | bytes 49184 | tf_op jit(solution)/shard_map/ppermute | solution.py:569
  152.3 14.2 %all_to_all.21 = f32[16,48,256]{2,1,0:T(8,128)S(1)} all-to-all(f32[16,48,256]{2,1,0:T(8,128)S(1)} %broadcast_in_dim.32), channel_id=1, replica_groups=mesh['tile'=16,'frame'=16] {'tile'}, dimensions={0} | all-to-all | bytes 1572864 | tf_op jit(solution)/shard_map/all_to_all | solution.py:603
  166.6 4.7 %collective-permute-start.21 = (f32[3,256,256]{2,1,0:T(8,128)S(1)}, f32[3,256,256]{2,1,0:T(8,128)S(1)}, u32[]{:S(2)}, u32[]{:S(2)}) collective-permute-start(f32[3,256,256]{2,1,0:T(8,128)S(1)} %bitcast.15), channel_id=1, source_target_pairs={{0,1},{1,0},{2,3},{3,2},{4,5},{5,4},{6,7},{7,6},{8,9},{9,8},{10,11... | collective-permute-start | bytes 2359304 | tf_op jit(solution)/shard_map/ppermute | solution.py:569
  (90 shorter events, 39.9 us)
Async XLA Ops:
  1.7 14.4 %collective-permute-start = (f32[384,256]{1,0:T(8,128)S(1)}, f32[384,256]{1,0:T(8,128)S(1)}, u32[]{:S(2)}, u32[]{:S(2)}) collective-permute-start(f32[384,256]{1,0:T(8,128)S(1)} %slice.8.first.refs_3_), channel_id=1, source_target_pairs={{16,0},{32,16},{48,32},{64,48},{80,64},{96,80},{112,96},{128,112},... | collective-permute-start | bytes 1179656 | tf_op jit(solution)/shard_map/ppermute | solution.py:564
  3.9 12.2 %collective-permute-start.1 = (f32[128,256]{1,0:T(8,128)S(1)}, f32[128,256]{1,0:T(8,128)S(1)}, u32[]{:S(2)}, u32[]{:S(2)}) collective-permute-start(f32[128,256]{1,0:T(8,128)S(1)} %slice.9.second.refs_4_), channel_id=1, source_target_pairs={{1,0},{2,1},{3,2},{4,3},{5,4},{6,5},{7,6},{8,7},{9,8},{10,9},{11,1... | collective-permute-start | bytes 393224 | tf_op jit(solution)/shard_map/ppermute | solution.py:564
  9.1 6.3 %collective-permute-start.2 = (s32[1,2]{1,0:T(1,128)}, s32[1,2]{1,0:T(1,128)S(1)}, u32[]{:S(2)}, u32[]{:S(2)}) collective-permute-start(s32[1,2]{1,0:T(1,128)} %refs_0_.5), channel_id=1, source_target_pairs={{0,1},{1,2},{2,3},{3,4},{4,5},{5,6},{6,7},{7,8},{8,9},{9,10},{10,1... | collective-permute-start | bytes 32 | tf_op jit(solution)/shard_map/ppermute | solution.py:564
  11.0 5.1 %collective-permute-start.3 = (s32[1,2]{1,0:T(1,128)}, s32[1,2]{1,0:T(1,128)S(1)}, u32[]{:S(2)}, u32[]{:S(2)}) collective-permute-start(s32[1,2]{1,0:T(1,128)} %refs_0_.5), channel_id=1, source_target_pairs={{0,16},{16,32},{32,48},{48,64},{64,80},{80,96},{96,112},{112,128},... | collective-permute-start | bytes 32 | tf_op jit(solution)/shard_map/ppermute | solution.py:564
  17.4 10.8 %collective-permute-start.4 = (f32[384,256]{1,0:T(8,128)S(1)}, f32[384,256]{1,0:T(8,128)S(1)}, u32[]{:S(2)}, u32[]{:S(2)}) collective-permute-start(f32[384,256]{1,0:T(8,128)S(1)} %get-tuple-element.44), channel_id=1, source_target_pairs={{1,0},{2,1},{3,2},{4,3},{5,4},{6,5},{7,6},{8,7},{9,8},{10,9},{11,1... | collective-permute-start | bytes 1179656 | tf_op jit(solution)/shard_map/ppermute | solution.py:564
  20.8 7.5 %collective-permute-start.5 = (f32[136,256]{1,0:T(8,128)S(1)}, f32[136,256]{1,0:T(8,128)S(1)}, u32[]{:S(2)}, u32[]{:S(2)}) collective-permute-start(f32[136,256]{1,0:T(8,128)S(1)} %get-tuple-element.45), channel_id=1, source_target_pairs={{16,0},{32,16},{48,32},{64,48},{80,64},{96,80},{112,96},{128,112},... | collective-permute-start | bytes 417800 | tf_op jit(solution)/shard_map/ppermute | solution.py:564
  35.6 6.4 %collective-permute-start.8 = (f32[3,256,256]{2,1,0:T(8,128)S(1)}, f32[3,256,256]{2,1,0:T(8,128)S(1)}, u32[]{:S(2)}, u32[]{:S(2)}) collective-permute-start(f32[3,256,256]{2,1,0:T(8,128)S(1)} %get-tuple-element.61.refs_11_), channel_id=1, source_target_pairs={{0,1},{1,0},{2,3},{3,2},{4,5},{5,4},{6,7},{7,6},{8,9},{9,8},{10,11... | collective-permute-start | bytes 2359304 | tf_op jit(solution)/shard_map/ppermute | solution.py:569
  36.8 16.3 %collective-permute-start.6 = (f32[520,256]{1,0:T(8,128)}, f32[520,256]{1,0:T(8,128)}, u32[]{:S(2)}, u32[]{:S(2)}) collective-permute-start(f32[520,256]{1,0:T(8,128)} %get-tuple-element.58.own_ref.refs_7_), channel_id=1, source_target_pairs={{0,1},{1,2},{2,3},{3,4},{4,5},{5,6},{6,7},{7,8},{8,9},{9,10},{10,1... | collective-permute-start | bytes 1597448 | tf_op jit(solution)/shard_map/ppermute | solution.py:564
  39.3 13.9 %collective-permute-start.7 = (f32[520,256]{1,0:T(8,128)}, f32[520,256]{1,0:T(8,128)}, u32[]{:S(2)}, u32[]{:S(2)}) collective-permute-start(f32[520,256]{1,0:T(8,128)} %get-tuple-element.58.own_ref.refs_7_), channel_id=1, source_target_pairs={{1,0},{2,1},{3,2},{4,3},{5,4},{6,5},{7,6},{8,7},{9,8},{10,9},{11,1... | collective-permute-start | bytes 1597448 | tf_op jit(solution)/shard_map/ppermute | solution.py:564
  43.0 24.2 %all-to-all-start = ((f32[16,48,256]{2,1,0:T(8,128)}), f32[16,48,256]{2,1,0:T(8,128)}, u32[]{:S(2)}, u32[]{:S(2)}) async-start(f32[16,48,256]{2,1,0:T(8,128)} %bitcast.14), calls=%async_computation | async-start | bytes 1572864 | tf_op jit(solution)/shard_map/all_to_all | solution.py:575
  56.9 27.4 %collective-permute-start.12 = (f32[2,256,256]{2,1,0:T(8,128)}, f32[2,256,256]{2,1,0:T(8,128)}, u32[]{:S(2)}, u32[]{:S(2)}) collective-permute-start(f32[2,256,256]{2,1,0:T(8,128)} %get-tuple-element.62), channel_id=1, source_target_pairs={{0,16},{16,32},{32,48},{48,64},{64,80},{80,96},{96,112},{112,128},... | collective-permute-start | bytes 1572872 | tf_op jit(solution)/shard_map/ppermute | solution.py:564
  60.9 23.4 %collective-permute-start.13 = (f32[2,256,256]{2,1,0:T(8,128)}, f32[2,256,256]{2,1,0:T(8,128)}, u32[]{:S(2)}, u32[]{:S(2)}) collective-permute-start(f32[2,256,256]{2,1,0:T(8,128)} %get-tuple-element.63), channel_id=1, source_target_pairs={{16,0},{32,16},{48,32},{64,48},{80,64},{96,80},{112,96},{128,112},... | collective-permute-start | bytes 1572872 | tf_op jit(solution)/shard_map/ppermute | solution.py:564
  68.5 3.4 %collective-permute-start.9 = (f32[48,256]{1,0:T(8,128)S(1)}, f32[48,256]{1,0:T(8,128)S(1)}, u32[]{:S(2)}, u32[]{:S(2)}) collective-permute-start(f32[48,256]{1,0:T(8,128)S(1)} %reduce_sum.18), channel_id=1, source_target_pairs={{0,2},{1,3},{2,0},{3,1},{4,6},{5,7},{6,4},{7,5},{8,10},{9,11},{10,... | collective-permute-start | bytes 147464 | tf_op jit(solution)/shard_map/ppermute | solution.py:596
  71.9 5.7 %collective-permute-start.10 = (f32[48,256]{1,0:T(8,128)S(1)}, f32[48,256]{1,0:T(8,128)S(1)}, u32[]{:S(2)}, u32[]{:S(2)}) collective-permute-start(f32[48,256]{1,0:T(8,128)S(1)} %add.34), channel_id=1, source_target_pairs={{2,4},{3,5},{4,2},{5,3},{6,8},{7,9},{8,6},{9,7},{10,12},{11,13},{1... | collective-permute-start | bytes 147464 | tf_op jit(solution)/shard_map/ppermute | solution.py:596
  77.6 6.7 %collective-permute-start.11 = (f32[48,256]{1,0:T(8,128)S(1)}, f32[48,256]{1,0:T(8,128)S(1)}, u32[]{:S(2)}, u32[]{:S(2)}) collective-permute-start(f32[48,256]{1,0:T(8,128)S(1)} %add.35), channel_id=1, source_target_pairs={{2,12},{3,13},{12,2},{13,3},{4,10},{5,11},{10,4},{11,5},{6,0},{7,1... | collective-permute-start | bytes 147464 | tf_op jit(solution)/shard_map/ppermute | solution.py:596
  99.8 5.9 %collective-permute-start.14 = (f32[3,256,256]{2,1,0:T(8,128)S(1)}, f32[3,256,256]{2,1,0:T(8,128)S(1)}, u32[]{:S(2)}, u32[]{:S(2)}) collective-permute-start(f32[3,256,256]{2,1,0:T(8,128)S(1)} %bitcast.12), channel_id=1, source_target_pairs={{0,1},{1,0},{2,3},{3,2},{4,5},{5,4},{6,7},{7,6},{8,9},{9,8},{10,11... | collective-permute-start | bytes 2359304 | tf_op jit(solution)/shard_map/ppermute | solution.py:569
  113.5 4.1 %collective-permute-start.16 = (f32[3,256,256]{2,1,0:T(8,128)S(1)}, f32[3,256,256]{2,1,0:T(8,128)S(1)}, u32[]{:S(2)}, u32[]{:S(2)}) collective-permute-start(f32[3,256,256]{2,1,0:T(8,128)S(1)} %get-tuple-element.71), channel_id=1, source_target_pairs={{0,1},{1,0},{2,3},{3,2},{4,5},{5,4},{6,7},{7,6},{8,9},{9,8},{10,11... | collective-permute-start | bytes 2359304 | tf_op jit(solution)/shard_map/ppermute | solution.py:569
  113.9 10.1 %collective-permute-start.15 = (f32[2,256,256]{2,1,0:T(8,128)}, f32[2,256,256]{2,1,0:T(8,128)S(1)}, u32[]{:S(2)}, u32[]{:S(2)}) collective-permute-start(f32[2,256,256]{2,1,0:T(8,128)} %get-tuple-element.68.refs_2_), channel_id=1, source_target_pairs={{0,1},{1,2},{2,3},{3,4},{4,5},{5,6},{6,7},{7,8},{8,9},{9,10},{10,1... | collective-permute-start | bytes 1572872 | tf_op jit(solution)/shard_map/ppermute | solution.py:564
  118.6 18.4 %all-to-all-start.2 = ((f32[16,48,256]{2,1,0:T(8,128)}), f32[16,48,256]{2,1,0:T(8,128)}, u32[]{:S(2)}, u32[]{:S(2)}) async-start(f32[16,48,256]{2,1,0:T(8,128)} %bitcast.8), calls=%async_computation.2 | async-start | bytes 1572864 | tf_op jit(solution)/shard_map/all_to_all | solution.py:575
  125.3 27.0 %collective-permute-start.20 = (f32[2,256,256]{2,1,0:T(8,128)S(1)}, f32[2,256,256]{2,1,0:T(8,128)}, u32[]{:S(2)}, u32[]{:S(2)}) collective-permute-start(f32[2,256,256]{2,1,0:T(8,128)S(1)} %get-tuple-element.72), channel_id=1, source_target_pairs={{0,16},{16,32},{32,48},{48,64},{64,80},{80,96},{96,112},{112,128},... | collective-permute-start | bytes 1572872 | tf_op jit(solution)/shard_map/ppermute | solution.py:564
  138.2 3.0 %collective-permute-start.17 = (f32[48,256]{1,0:T(8,128)S(1)}, f32[48,256]{1,0:T(8,128)S(1)}, u32[]{:S(2)}, u32[]{:S(2)}) collective-permute-start(f32[48,256]{1,0:T(8,128)S(1)} %reduce_sum.19), channel_id=1, source_target_pairs={{0,2},{1,3},{2,0},{3,1},{4,6},{5,7},{6,4},{7,5},{8,10},{9,11},{10,... | collective-permute-start | bytes 147464 | tf_op jit(solution)/shard_map/ppermute | solution.py:569
  141.3 3.9 %collective-permute-start.18 = (f32[48,256]{1,0:T(8,128)S(1)}, f32[48,256]{1,0:T(8,128)S(1)}, u32[]{:S(2)}, u32[]{:S(2)}) collective-permute-start(f32[48,256]{1,0:T(8,128)S(1)} %add.40), channel_id=1, source_target_pairs={{0,4},{1,5},{2,6},{3,7},{4,0},{5,1},{6,2},{7,3},{8,12},{9,13},{10,... | collective-permute-start | bytes 147464 | tf_op jit(solution)/shard_map/ppermute | solution.py:569
  145.2 7.0 %collective-permute-start.19 = (f32[48,256]{1,0:T(8,128)S(1)}, f32[48,256]{1,0:T(8,128)S(1)}, u32[]{:S(2)}, u32[]{:S(2)}) collective-permute-start(f32[48,256]{1,0:T(8,128)S(1)} %add.41), channel_id=1, source_target_pairs={{0,8},{1,9},{2,10},{3,11},{4,12},{5,13},{6,14},{7,15},{8,0},{9,1},... | collective-permute-start | bytes 147464 | tf_op jit(solution)/shard_map/ppermute | solution.py:569
  166.6 6.7 %collective-permute-start.21 = (f32[3,256,256]{2,1,0:T(8,128)S(1)}, f32[3,256,256]{2,1,0:T(8,128)S(1)}, u32[]{:S(2)}, u32[]{:S(2)}) collective-permute-start(f32[3,256,256]{2,1,0:T(8,128)S(1)} %bitcast.15), channel_id=1, source_target_pairs={{0,1},{1,0},{2,3},{3,2},{4,5},{5,4},{6,7},{7,6},{8,9},{9,8},{10,11... | collective-permute-start | bytes 2359304 | tf_op jit(solution)/shard_map/ppermute | solution.py:569
  (20 other events, 292.7 us)

commit v5 on v4

--- a/solution.py
+++ b/solution.py
@@ -442,7 +442,7 @@
                     ref[at] = value
             return 0
 
-        lax.fori_loop(0, DET // STRIP, strip, 0, unroll=16)
+        lax.fori_loop(0, DET // STRIP, strip, 0, unroll=4)
 
     vmem = pl.BlockSpec(memory_space=pltpu.VMEM)
     return pl.pallas_call(
@@ -479,6 +479,7 @@
         out_specs=[vmem] * 2,
         compiler_params=pltpu.CompilerParams(vmem_limit_bytes=VMEM_LIMIT),
         name="sides",
+        cost_estimate=pl.CostEstimate(flops=WEIGHT, bytes_accessed=WEIGHT // 400, transcendentals=0),
     )(here_at, left_at, above_at, *operands)
 
 
@@ -507,7 +508,7 @@
                 ref[part, pl.ds(start, STRIP), :] = value
         return 0
 
-    lax.fori_loop(0, DET // STRIP, strip, 0, unroll=16)
+    lax.fori_loop(0, DET // STRIP, strip, 0, unroll=4)
 
 
 def merge_call(here_at, above_at, *operands):

time: 176 us -> 174 us (0.989)
    unnamed x40 -> x52, local copies, waits for them, and re-layouts: 4.22 us -> 3.34 us
where the time goes in v5:
time: 174 us; the launch traced here: 173 us
  starting transfers between devices  72.7 us (42%)
  waiting for transfers between devices  37.7 us (22%)
  blocking collectives  30.2 us (17%)
  Pallas kernels  18.1 us (10%)
  other arithmetic  7.79 us (4%)
  local copies, waits for them, and re-layouts  5.42 us (3%)
    ppermute x12, starting transfers between devices, shifted(): lax.ppermute(value, axis, [(source, source + steps) for source in range(i...  34.2 us
    all_to_all x2, blocking collectives, spread(): mine = lax.all_to_all(parts, 'tile', 0, 0).reshape(MODES, DET, DET)  30.2 us
    all_to_all x2, starting transfers between devices, tile_parts(): lax.all_to_all(summed.reshape(count, MODES * DET // count, DET), 'tile',...  14.4 us
    ppermute x7, starting transfers between devices, swapped(): lax.ppermute(value, axis, [(source, source ^ distance) for source in rang...  14.3 us
    all_to_all x2, waiting for transfers between devices, tile_parts(): lax.all_to_all(summed.reshape(count, MODES * DET // count, DET), 'tile',...  13.9 us
    pallas_call x2, Pallas kernels, gradient_call(): pl.pallas_call(body, out_shape=outs, in_specs=[smem] * len(scalars) + [vm...  12.4 us
    ppermute x7, waiting for transfers between devices, swapped(): lax.ppermute(value, axis, [(source, source ^ distance) for source in rang...  10.7 us
    ppermute x3, starting transfers between devices, quick_chip_sum(): part = part + lax.ppermute(part, 'frame', moves)  9.76 us
  transfers between devices with their start and end apart: 24, of which 12 were waited for; matrix products, arithmetic and copies ran while one was open for 4% of the time, Pallas kernels for 3%

profile of v5, /device:TPU:1, one launch (start us, length us, event | category | flops | bytes accessed | tf_op | source)
XLA Modules:
  0.0 173.0 jit_solution(13101944474935613464)
XLA Ops:
  3.9 5.1 %collective-permute-start.1 = (f32[128,256]{1,0:T(8,128)S(1)}, f32[128,256]{1,0:T(8,128)S(1)}, u32[]{:S(2)}, u32[]{:S(2)}) collective-permute-start(f32[128,256]{1,0:T(8,128)S(1)} %slice.9.second.refs_4_), channel_id=1, source_target_pairs={{1,0},{2,1},{3,2},{4,3},{5,4},{6,5},{7,6},{8,7},{9,8},{10,9},{11,1... | collective-permute-start | bytes 393224 | tf_op jit(solution)/shard_map/ppermute | solution.py:565
  11.0 4.3 %collective-permute-start.3 = (s32[1,2]{1,0:T(1,128)}, s32[1,2]{1,0:T(1,128)S(1)}, u32[]{:S(2)}, u32[]{:S(2)}) collective-permute-start(s32[1,2]{1,0:T(1,128)} %refs_0_.5), channel_id=1, source_target_pairs={{0,16},{16,32},{32,48},{48,64},{64,80},{80,96},{96,112},{112,128},... | collective-permute-start | bytes 32 | tf_op jit(solution)/shard_map/ppermute | solution.py:565
  17.5 3.2 %collective-permute-start.4 = (f32[384,256]{1,0:T(8,128)S(1)}, f32[384,256]{1,0:T(8,128)S(1)}, u32[]{:S(2)}, u32[]{:S(2)}) collective-permute-start(f32[384,256]{1,0:T(8,128)S(1)} %get-tuple-element.44), channel_id=1, source_target_pairs={{1,0},{2,1},{3,2},{4,3},{5,4},{6,5},{7,6},{8,7},{9,8},{10,9},{11,1... | collective-permute-start | bytes 1179656 | tf_op jit(solution)/shard_map/ppermute | solution.py:565
  23.2 5.1 %collective-permute-done.5.refs_8_.below_ref = f32[136,256]{1,0:T(8,128)S(1)} collective-permute-done((f32[136,256]{1,0:T(8,128)S(1)}, f32[136,256]{1,0:T(8,128)S(1)}, u32[]{:S(2)}, u32[]{:S(2)}) %collective-permute-start.5) | collective-permute-done | bytes 139296 | tf_op jit(solution)/shard_map/ppermute | solution.py:565
  28.4 4.8 %gradient_first.1 = (f32[520,256]{1,0:T(8,128)S(1)}, f32[2,256,256]{2,1,0:T(8,128)S(1)}, f32[3,256,256]{2,1,0:T(8,128)S(1)}, f32[3,256,256]{2,1,0:T(8,128)S(1)}) custom-call(s32[1,2]{1,0:T(1,128)S(1)} %copy-done.19, s32[1,2]{1,0:T(1,128)S(1)} %copy-done.18, s32[3]{0:T(128)S(1)} %pad_add_fusion.refs_2_, f32[384,256]{1,0:T(8,128)S(1)} %slice.8.first.refs_3_, ...), custom_call_target="tpu_custom_call" | custom-call | tf_op jit(solution)/shard_map/gradient_first/pallas_call | solution.py:417
  35.2 2.5 %collective-permute-start.6 = (f32[520,256]{1,0:T(8,128)S(1)}, f32[520,256]{1,0:T(8,128)}, u32[]{:S(2)}, u32[]{:S(2)}) collective-permute-start(f32[520,256]{1,0:T(8,128)S(1)} %get-tuple-element.58.own_ref.refs_7_), channel_id=1, source_target_pairs={{0,1},{1,2},{2,3},{3,4},{4,5},{5,6},{6,7},{7,8},{8,9},{9,10},{10,1... | collective-permute-start | bytes 1597448 | tf_op jit(solution)/shard_map/ppermute | solution.py:565
  37.7 2.6 %collective-permute-start.7 = (f32[520,256]{1,0:T(8,128)S(1)}, f32[520,256]{1,0:T(8,128)}, u32[]{:S(2)}, u32[]{:S(2)}) collective-permute-start(f32[520,256]{1,0:T(8,128)S(1)} %get-tuple-element.58.own_ref.refs_7_), channel_id=1, source_target_pairs={{1,0},{2,1},{3,2},{4,3},{5,4},{6,5},{7,6},{8,7},{9,8},{10,9},{11,1... | collective-permute-start | bytes 1597448 | tf_op jit(solution)/shard_map/ppermute | solution.py:565
  41.4 10.1 %all-to-all-start = ((f32[16,48,256]{2,1,0:T(8,128)}), f32[16,48,256]{2,1,0:T(8,128)}, u32[]{:S(2)}, u32[]{:S(2)}) async-start(f32[16,48,256]{2,1,0:T(8,128)} %bitcast.14), calls=%async_computation | async-start | bytes 1572864 | tf_op jit(solution)/shard_map/all_to_all | solution.py:576
  51.6 3.0 %merge.1 = (f32[2,256,256]{2,1,0:T(8,128)S(1)}, f32[2,256,256]{2,1,0:T(8,128)}, f32[2,256,256]{2,1,0:T(8,128)}) custom-call(s32[1,2]{1,0:T(1,128)S(1)} %copy-done.20, s32[1,2]{1,0:T(1,128)S(1)} %copy-done.24, f32[520,256]{1,0:T(8,128)S(1)} %get-tuple-element.58.own_ref.refs_7_, f32[520,256]{1,0:T(8,128)} %collective-permute-done.6.left_ref, ...), custom_call_target="tpu_custom_call" | custom-call | flops 20000000000 | bytes 50000000 | tf_op jit(solution)/shard_map/merge/pallas_call | solution.py:516
  55.4 4.0 %collective-permute-start.12 = (f32[2,256,256]{2,1,0:T(8,128)}, f32[2,256,256]{2,1,0:T(8,128)}, u32[]{:S(2)}, u32[]{:S(2)}) collective-permute-start(f32[2,256,256]{2,1,0:T(8,128)} %get-tuple-element.62), channel_id=1, source_target_pairs={{0,16},{16,32},{32,48},{48,64},{64,80},{80,96},{96,112},{112,128},... | collective-permute-start | bytes 1572872 | tf_op jit(solution)/shard_map/ppermute | solution.py:565
  60.7 4.9 %all-to-all-done = f32[16,48,256]{2,1,0:T(8,128)} async-done(((f32[16,48,256]{2,1,0:T(8,128)}), f32[16,48,256]{2,1,0:T(8,128)}, u32[]{:S(2)}, u32[]{:S(2)}) %all-to-all-start) | async-done | bytes 786464 | tf_op jit(solution)/shard_map/all_to_all | solution.py:576
  67.2 3.1 %collective-permute-done.9 = f32[48,256]{1,0:T(8,128)S(1)} collective-permute-done((f32[48,256]{1,0:T(8,128)S(1)}, f32[48,256]{1,0:T(8,128)S(1)}, u32[]{:S(2)}, u32[]{:S(2)}) %collective-permute-start.9) | collective-permute-done | bytes 49184 | tf_op jit(solution)/shard_map/ppermute | solution.py:597
  70.3 4.2 %collective-permute-start.10 = (f32[48,256]{1,0:T(8,128)S(1)}, f32[48,256]{1,0:T(8,128)S(1)}, u32[]{:S(2)}, u32[]{:S(2)}) collective-permute-start(f32[48,256]{1,0:T(8,128)S(1)} %add.34), channel_id=1, source_target_pairs={{2,4},{3,5},{4,2},{5,3},{6,8},{7,9},{8,6},{9,7},{10,12},{11,13},{1... | collective-permute-start | bytes 147464 | tf_op jit(solution)/shard_map/ppermute | solution.py:597
  76.0 5.2 %collective-permute-start.11 = (f32[48,256]{1,0:T(8,128)S(1)}, f32[48,256]{1,0:T(8,128)S(1)}, u32[]{:S(2)}, u32[]{:S(2)}) collective-permute-start(f32[48,256]{1,0:T(8,128)S(1)} %add.35), channel_id=1, source_target_pairs={{2,12},{3,13},{12,2},{13,3},{4,10},{5,11},{10,4},{11,5},{6,0},{7,1... | collective-permute-start | bytes 147464 | tf_op jit(solution)/shard_map/ppermute | solution.py:597
  82.8 15.4 %all_to_all.20 = f32[16,48,256]{2,1,0:T(8,128)S(1)} all-to-all(f32[16,48,256]{2,1,0:T(8,128)S(1)} %broadcast_in_dim.31), channel_id=1, replica_groups=mesh['tile'=16,'frame'=16] {'tile'}, dimensions={0} | all-to-all | bytes 1572864 | tf_op jit(solution)/shard_map/all_to_all | solution.py:604
  98.2 4.0 %collective-permute-start.14 = (f32[3,256,256]{2,1,0:T(8,128)S(1)}, f32[3,256,256]{2,1,0:T(8,128)S(1)}, u32[]{:S(2)}, u32[]{:S(2)}) collective-permute-start(f32[3,256,256]{2,1,0:T(8,128)S(1)} %bitcast.12), channel_id=1, source_target_pairs={{0,1},{1,0},{2,3},{3,2},{4,5},{5,4},{6,7},{7,6},{8,9},{9,8},{10,11... | collective-permute-start | bytes 2359304 | tf_op jit(solution)/shard_map/ppermute | solution.py:570
  104.1 7.6 %gradient_last.1 = (f32[2,256,256]{2,1,0:T(8,128)}, f32[3,256,256]{2,1,0:T(8,128)S(1)}, f32[3,256,256]{2,1,0:T(8,128)S(1)}, f32[1,2]{1,0:T(1,128)}) custom-call(s32[1,2]{1,0:T(1,128)S(1)} %copy-done.20, s32[1,2]{1,0:T(1,128)S(1)} %copy-done.18, s32[3]{0:T(128)S(1)} %pad_add_fusion.refs_2_, f32[2,256,256]{2,1,0:T(8,128)S(1)} %copy-done.5, ...), custom_call_target="tpu_custom_call" | custom-call | tf_op jit(solution)/shard_map/gradient_last/pallas_call | solution.py:417
  112.1 3.7 %collective-permute-start.15 = (f32[2,256,256]{2,1,0:T(8,128)}, f32[2,256,256]{2,1,0:T(8,128)S(1)}, u32[]{:S(2)}, u32[]{:S(2)}) collective-permute-start(f32[2,256,256]{2,1,0:T(8,128)} %get-tuple-element.68.refs_2_), channel_id=1, source_target_pairs={{0,1},{1,2},{2,3},{3,4},{4,5},{5,6},{6,7},{7,8},{8,9},{9,10},{10,1... | collective-permute-start | bytes 1572872 | tf_op jit(solution)/shard_map/ppermute | solution.py:565
  116.8 4.3 %all-to-all-start.2 = ((f32[16,48,256]{2,1,0:T(8,128)}), f32[16,48,256]{2,1,0:T(8,128)}, u32[]{:S(2)}, u32[]{:S(2)}) async-start(f32[16,48,256]{2,1,0:T(8,128)} %bitcast.15), calls=%async_computation.2 | async-start | bytes 1572864 | tf_op jit(solution)/shard_map/all_to_all | solution.py:576
  123.4 2.8 %collective-permute-start.20 = (f32[2,256,256]{2,1,0:T(8,128)S(1)}, f32[2,256,256]{2,1,0:T(8,128)}, u32[]{:S(2)}, u32[]{:S(2)}) collective-permute-start(f32[2,256,256]{2,1,0:T(8,128)S(1)} %get-tuple-element.72), channel_id=1, source_target_pairs={{0,16},{16,32},{32,48},{48,64},{64,80},{80,96},{96,112},{112,128},... | collective-permute-start | bytes 1572872 | tf_op jit(solution)/shard_map/ppermute | solution.py:565
  126.3 9.0 %all-to-all-done.2 = f32[16,48,256]{2,1,0:T(8,128)} async-done(((f32[16,48,256]{2,1,0:T(8,128)}), f32[16,48,256]{2,1,0:T(8,128)}, u32[]{:S(2)}, u32[]{:S(2)}) %all-to-all-start.2) | async-done | bytes 786464 | tf_op jit(solution)/shard_map/all_to_all | solution.py:576
  145.6 4.9 %collective-permute-done.19 = f32[48,256]{1,0:T(8,128)S(1)} collective-permute-done((f32[48,256]{1,0:T(8,128)S(1)}, f32[48,256]{1,0:T(8,128)S(1)}, u32[]{:S(2)}, u32[]{:S(2)}) %collective-permute-start.19) | collective-permute-done | bytes 49184 | tf_op jit(solution)/shard_map/ppermute | solution.py:570
  150.5 14.8 %all_to_all.21 = f32[16,48,256]{2,1,0:T(8,128)S(1)} all-to-all(f32[16,48,256]{2,1,0:T(8,128)S(1)} %broadcast_in_dim.32), channel_id=1, replica_groups=mesh['tile'=16,'frame'=16] {'tile'}, dimensions={0} | all-to-all | bytes 1572864 | tf_op jit(solution)/shard_map/all_to_all | solution.py:604
  165.3 4.4 %collective-permute-start.21 = (f32[3,256,256]{2,1,0:T(8,128)S(1)}, f32[3,256,256]{2,1,0:T(8,128)S(1)}, u32[]{:S(2)}, u32[]{:S(2)}) collective-permute-start(f32[3,256,256]{2,1,0:T(8,128)S(1)} %bitcast.16), channel_id=1, source_target_pairs={{0,1},{1,0},{2,3},{3,2},{4,5},{5,4},{6,7},{7,6},{8,9},{9,8},{10,11... | collective-permute-start | bytes 2359304 | tf_op jit(solution)/shard_map/ppermute | solution.py:570
  (102 shorter events, 38.8 us)
Async XLA Ops:
  1.7 14.4 %collective-permute-start = (f32[384,256]{1,0:T(8,128)S(1)}, f32[384,256]{1,0:T(8,128)S(1)}, u32[]{:S(2)}, u32[]{:S(2)}) collective-permute-start(f32[384,256]{1,0:T(8,128)S(1)} %slice.8.first.refs_3_), channel_id=1, source_target_pairs={{16,0},{32,16},{48,32},{64,48},{80,64},{96,80},{112,96},{128,112},... | collective-permute-start | bytes 1179656 | tf_op jit(solution)/shard_map/ppermute | solution.py:565
  3.9 12.2 %collective-permute-start.1 = (f32[128,256]{1,0:T(8,128)S(1)}, f32[128,256]{1,0:T(8,128)S(1)}, u32[]{:S(2)}, u32[]{:S(2)}) collective-permute-start(f32[128,256]{1,0:T(8,128)S(1)} %slice.9.second.refs_4_), channel_id=1, source_target_pairs={{1,0},{2,1},{3,2},{4,3},{5,4},{6,5},{7,6},{8,7},{9,8},{10,9},{11,1... | collective-permute-start | bytes 393224 | tf_op jit(solution)/shard_map/ppermute | solution.py:565
  9.0 6.3 %collective-permute-start.2 = (s32[1,2]{1,0:T(1,128)}, s32[1,2]{1,0:T(1,128)S(1)}, u32[]{:S(2)}, u32[]{:S(2)}) collective-permute-start(s32[1,2]{1,0:T(1,128)} %refs_0_.5), channel_id=1, source_target_pairs={{0,1},{1,2},{2,3},{3,4},{4,5},{5,6},{6,7},{7,8},{8,9},{9,10},{10,1... | collective-permute-start | bytes 32 | tf_op jit(solution)/shard_map/ppermute | solution.py:565
  11.0 5.1 %collective-permute-start.3 = (s32[1,2]{1,0:T(1,128)}, s32[1,2]{1,0:T(1,128)S(1)}, u32[]{:S(2)}, u32[]{:S(2)}) collective-permute-start(s32[1,2]{1,0:T(1,128)} %refs_0_.5), channel_id=1, source_target_pairs={{0,16},{16,32},{32,48},{48,64},{64,80},{80,96},{96,112},{112,128},... | collective-permute-start | bytes 32 | tf_op jit(solution)/shard_map/ppermute | solution.py:565
  17.5 10.8 %collective-permute-start.4 = (f32[384,256]{1,0:T(8,128)S(1)}, f32[384,256]{1,0:T(8,128)S(1)}, u32[]{:S(2)}, u32[]{:S(2)}) collective-permute-start(f32[384,256]{1,0:T(8,128)S(1)} %get-tuple-element.44), channel_id=1, source_target_pairs={{1,0},{2,1},{3,2},{4,3},{5,4},{6,5},{7,6},{8,7},{9,8},{10,9},{11,1... | collective-permute-start | bytes 1179656 | tf_op jit(solution)/shard_map/ppermute | solution.py:565
  20.8 7.5 %collective-permute-start.5 = (f32[136,256]{1,0:T(8,128)S(1)}, f32[136,256]{1,0:T(8,128)S(1)}, u32[]{:S(2)}, u32[]{:S(2)}) collective-permute-start(f32[136,256]{1,0:T(8,128)S(1)} %get-tuple-element.45), channel_id=1, source_target_pairs={{16,0},{32,16},{48,32},{64,48},{80,64},{96,80},{112,96},{128,112},... | collective-permute-start | bytes 417800 | tf_op jit(solution)/shard_map/ppermute | solution.py:565
  34.0 6.3 %collective-permute-start.8 = (f32[3,256,256]{2,1,0:T(8,128)S(1)}, f32[3,256,256]{2,1,0:T(8,128)S(1)}, u32[]{:S(2)}, u32[]{:S(2)}) collective-permute-start(f32[3,256,256]{2,1,0:T(8,128)S(1)} %get-tuple-element.61.refs_11_), channel_id=1, source_target_pairs={{0,1},{1,0},{2,3},{3,2},{4,5},{5,4},{6,7},{7,6},{8,9},{9,8},{10,11... | collective-permute-start | bytes 2359304 | tf_op jit(solution)/shard_map/ppermute | solution.py:570
  35.2 16.3 %collective-permute-start.6 = (f32[520,256]{1,0:T(8,128)S(1)}, f32[520,256]{1,0:T(8,128)}, u32[]{:S(2)}, u32[]{:S(2)}) collective-permute-start(f32[520,256]{1,0:T(8,128)S(1)} %get-tuple-element.58.own_ref.refs_7_), channel_id=1, source_target_pairs={{0,1},{1,2},{2,3},{3,4},{4,5},{5,6},{6,7},{7,8},{8,9},{9,10},{10,1... | collective-permute-start | bytes 1597448 | tf_op jit(solution)/shard_map/ppermute | solution.py:565
  37.7 13.8 %collective-permute-start.7 = (f32[520,256]{1,0:T(8,128)S(1)}, f32[520,256]{1,0:T(8,128)}, u32[]{:S(2)}, u32[]{:S(2)}) collective-permute-start(f32[520,256]{1,0:T(8,128)S(1)} %get-tuple-element.58.own_ref.refs_7_), channel_id=1, source_target_pairs={{1,0},{2,1},{3,2},{4,3},{5,4},{6,5},{7,6},{8,7},{9,8},{10,9},{11,1... | collective-permute-start | bytes 1597448 | tf_op jit(solution)/shard_map/ppermute | solution.py:565
  41.4 24.2 %all-to-all-start = ((f32[16,48,256]{2,1,0:T(8,128)}), f32[16,48,256]{2,1,0:T(8,128)}, u32[]{:S(2)}, u32[]{:S(2)}) async-start(f32[16,48,256]{2,1,0:T(8,128)} %bitcast.14), calls=%async_computation | async-start | bytes 1572864 | tf_op jit(solution)/shard_map/all_to_all | solution.py:576
  55.4 27.3 %collective-permute-start.12 = (f32[2,256,256]{2,1,0:T(8,128)}, f32[2,256,256]{2,1,0:T(8,128)}, u32[]{:S(2)}, u32[]{:S(2)}) collective-permute-start(f32[2,256,256]{2,1,0:T(8,128)} %get-tuple-element.62), channel_id=1, source_target_pairs={{0,16},{16,32},{32,48},{48,64},{64,80},{80,96},{96,112},{112,128},... | collective-permute-start | bytes 1572872 | tf_op jit(solution)/shard_map/ppermute | solution.py:565
  59.4 23.3 %collective-permute-start.13 = (f32[2,256,256]{2,1,0:T(8,128)}, f32[2,256,256]{2,1,0:T(8,128)}, u32[]{:S(2)}, u32[]{:S(2)}) collective-permute-start(f32[2,256,256]{2,1,0:T(8,128)} %get-tuple-element.63), channel_id=1, source_target_pairs={{16,0},{32,16},{48,32},{64,48},{80,64},{96,80},{112,96},{128,112},... | collective-permute-start | bytes 1572872 | tf_op jit(solution)/shard_map/ppermute | solution.py:565
  66.8 3.4 %collective-permute-start.9 = (f32[48,256]{1,0:T(8,128)S(1)}, f32[48,256]{1,0:T(8,128)S(1)}, u32[]{:S(2)}, u32[]{:S(2)}) collective-permute-start(f32[48,256]{1,0:T(8,128)S(1)} %reduce_sum.18), channel_id=1, source_target_pairs={{0,2},{1,3},{2,0},{3,1},{4,6},{5,7},{6,4},{7,5},{8,10},{9,11},{10,... | collective-permute-start | bytes 147464 | tf_op jit(solution)/shard_map/ppermute | solution.py:597
  70.3 5.7 %collective-permute-start.10 = (f32[48,256]{1,0:T(8,128)S(1)}, f32[48,256]{1,0:T(8,128)S(1)}, u32[]{:S(2)}, u32[]{:S(2)}) collective-permute-start(f32[48,256]{1,0:T(8,128)S(1)} %add.34), channel_id=1, source_target_pairs={{2,4},{3,5},{4,2},{5,3},{6,8},{7,9},{8,6},{9,7},{10,12},{11,13},{1... | collective-permute-start | bytes 147464 | tf_op jit(solution)/shard_map/ppermute | solution.py:597
  76.0 6.7 %collective-permute-start.11 = (f32[48,256]{1,0:T(8,128)S(1)}, f32[48,256]{1,0:T(8,128)S(1)}, u32[]{:S(2)}, u32[]{:S(2)}) collective-permute-start(f32[48,256]{1,0:T(8,128)S(1)} %add.35), channel_id=1, source_target_pairs={{2,12},{3,13},{12,2},{13,3},{4,10},{5,11},{10,4},{11,5},{6,0},{7,1... | collective-permute-start | bytes 147464 | tf_op jit(solution)/shard_map/ppermute | solution.py:597
  98.2 5.9 %collective-permute-start.14 = (f32[3,256,256]{2,1,0:T(8,128)S(1)}, f32[3,256,256]{2,1,0:T(8,128)S(1)}, u32[]{:S(2)}, u32[]{:S(2)}) collective-permute-start(f32[3,256,256]{2,1,0:T(8,128)S(1)} %bitcast.12), channel_id=1, source_target_pairs={{0,1},{1,0},{2,3},{3,2},{4,5},{5,4},{6,7},{7,6},{8,9},{9,8},{10,11... | collective-permute-start | bytes 2359304 | tf_op jit(solution)/shard_map/ppermute | solution.py:570
  111.7 4.1 %collective-permute-start.16 = (f32[3,256,256]{2,1,0:T(8,128)S(1)}, f32[3,256,256]{2,1,0:T(8,128)S(1)}, u32[]{:S(2)}, u32[]{:S(2)}) collective-permute-start(f32[3,256,256]{2,1,0:T(8,128)S(1)} %get-tuple-element.71), channel_id=1, source_target_pairs={{0,1},{1,0},{2,3},{3,2},{4,5},{5,4},{6,7},{7,6},{8,9},{9,8},{10,11... | collective-permute-start | bytes 2359304 | tf_op jit(solution)/shard_map/ppermute | solution.py:570
  112.1 10.1 %collective-permute-start.15 = (f32[2,256,256]{2,1,0:T(8,128)}, f32[2,256,256]{2,1,0:T(8,128)S(1)}, u32[]{:S(2)}, u32[]{:S(2)}) collective-permute-start(f32[2,256,256]{2,1,0:T(8,128)} %get-tuple-element.68.refs_2_), channel_id=1, source_target_pairs={{0,1},{1,2},{2,3},{3,4},{4,5},{5,6},{6,7},{7,8},{8,9},{9,10},{10,1... | collective-permute-start | bytes 1572872 | tf_op jit(solution)/shard_map/ppermute | solution.py:565
  116.8 18.5 %all-to-all-start.2 = ((f32[16,48,256]{2,1,0:T(8,128)}), f32[16,48,256]{2,1,0:T(8,128)}, u32[]{:S(2)}, u32[]{:S(2)}) async-start(f32[16,48,256]{2,1,0:T(8,128)} %bitcast.15), calls=%async_computation.2 | async-start | bytes 1572864 | tf_op jit(solution)/shard_map/all_to_all | solution.py:576
  123.4 27.0 %collective-permute-start.20 = (f32[2,256,256]{2,1,0:T(8,128)S(1)}, f32[2,256,256]{2,1,0:T(8,128)}, u32[]{:S(2)}, u32[]{:S(2)}) collective-permute-start(f32[2,256,256]{2,1,0:T(8,128)S(1)} %get-tuple-element.72), channel_id=1, source_target_pairs={{0,16},{16,32},{32,48},{48,64},{64,80},{80,96},{96,112},{112,128},... | collective-permute-start | bytes 1572872 | tf_op jit(solution)/shard_map/ppermute | solution.py:565
  136.4 3.0 %collective-permute-start.17 = (f32[48,256]{1,0:T(8,128)S(1)}, f32[48,256]{1,0:T(8,128)S(1)}, u32[]{:S(2)}, u32[]{:S(2)}) collective-permute-start(f32[48,256]{1,0:T(8,128)S(1)} %reduce_sum.19), channel_id=1, source_target_pairs={{0,2},{1,3},{2,0},{3,1},{4,6},{5,7},{6,4},{7,5},{8,10},{9,11},{10,... | collective-permute-start | bytes 147464 | tf_op jit(solution)/shard_map/ppermute | solution.py:570
  139.5 3.9 %collective-permute-start.18 = (f32[48,256]{1,0:T(8,128)S(1)}, f32[48,256]{1,0:T(8,128)S(1)}, u32[]{:S(2)}, u32[]{:S(2)}) collective-permute-start(f32[48,256]{1,0:T(8,128)S(1)} %add.40), channel_id=1, source_target_pairs={{0,4},{1,5},{2,6},{3,7},{4,0},{5,1},{6,2},{7,3},{8,12},{9,13},{10,... | collective-permute-start | bytes 147464 | tf_op jit(solution)/shard_map/ppermute | solution.py:570
  143.4 7.0 %collective-permute-start.19 = (f32[48,256]{1,0:T(8,128)S(1)}, f32[48,256]{1,0:T(8,128)S(1)}, u32[]{:S(2)}, u32[]{:S(2)}) collective-permute-start(f32[48,256]{1,0:T(8,128)S(1)} %add.41), channel_id=1, source_target_pairs={{0,8},{1,9},{2,10},{3,11},{4,12},{5,13},{6,14},{7,15},{8,0},{9,1},... | collective-permute-start | bytes 147464 | tf_op jit(solution)/shard_map/ppermute | solution.py:570
  165.3 6.3 %collective-permute-start.21 = (f32[3,256,256]{2,1,0:T(8,128)S(1)}, f32[3,256,256]{2,1,0:T(8,128)S(1)}, u32[]{:S(2)}, u32[]{:S(2)}) collective-permute-start(f32[3,256,256]{2,1,0:T(8,128)S(1)} %bitcast.16), channel_id=1, source_target_pairs={{0,1},{1,0},{2,3},{3,2},{4,5},{5,4},{6,7},{7,6},{8,9},{9,8},{10,11... | collective-permute-start | bytes 2359304 | tf_op jit(solution)/shard_map/ppermute | solution.py:570
  (26 other events, 301.1 us)
